TPU v7x, 32 devices: a whole 2x2x4 slice. The times are simulated.
32 devices in a mesh: ctx: 8 (over y, x, core), wsh: 4 (over z).
Axes of the slice: x: 2, y: 2, z: 4, core: 2. Of those that a mesh axis runs over, the one named last changes fastest.
Arguments:
- tokens: bfloat16 [4, 2048, 1024], P('wsh', 'ctx'), may hold values from -6 to 6
- starts: int32 [4, 8], P('wsh'), may hold values from 0 to 2047, as said below
- query_weight: bfloat16 [1024, 1024], P('wsh'), may hold values from -0.1875 to 0.1875
- key_weight: bfloat16 [1024, 1024], P('wsh'), may hold values from -0.1875 to 0.1875
- value_weight: bfloat16 [1024, 1024], P('wsh'), may hold values from -0.1875 to 0.1875
- output_weight: bfloat16 [1024, 1024], P('wsh'), may hold values from -0.15625 to 0.15625
- inner_weight: bfloat16 [1024, 4096], P('wsh'), may hold values from -0.1875 to 0.1875
- outer_weight: bfloat16 [4096, 1024], P('wsh'), may hold values from -0.09375 to 0.09375
- query_bias: bfloat16 [1024], P('wsh'), may hold values from -3 to 3
- value_bias: bfloat16 [1024], P('wsh'), may hold values from -0.3125 to 0.3125
- output_bias: bfloat16 [1024], P('wsh'), may hold values from -1.75 to 1.75
- first_gain: bfloat16 [1024], P('wsh'), may hold values from 0.5 to 1.5
- first_shift: bfloat16 [1024], P('wsh'), may hold values from -1.75 to 1.75
- inner_bias: bfloat16 [4096], P('wsh'), may hold values from -3 to 3
- outer_bias: bfloat16 [1024], P('wsh'), may hold values from -1.75 to 1.75
- second_gain: bfloat16 [1024], P('wsh'), may hold values from 0.5 to 1.5
- second_shift: bfloat16 [1024], P('wsh'), may hold values from -1.75 to 1.75
- cotangent: bfloat16 [4, 2048, 1024], P('wsh', 'ctx'), may hold values from -6 to 6
Outputs:
- result: bfloat16 [4, 2048, 1024], P('wsh', 'ctx')
- input_grad: bfloat16 [4, 2048, 1024], P('wsh', 'ctx')
- query_weight_grad: float32 [1024, 1024], P('wsh')
- key_weight_grad: float32 [1024, 1024], P('wsh')
- value_weight_grad: float32 [1024, 1024], P('wsh')
- output_weight_grad: float32 [1024, 1024], P('wsh')
- inner_weight_grad: float32 [1024, 4096], P('wsh')
- outer_weight_grad: float32 [4096, 1024], P('wsh')
- query_bias_grad: float32 [1024], P('wsh')
- value_bias_grad: float32 [1024], P('wsh')
- output_bias_grad: float32 [1024], P('wsh')
- first_gain_grad: float32 [1024], P('wsh')
- first_shift_grad: float32 [1024], P('wsh')
- inner_bias_grad: float32 [4096], P('wsh')
- outer_bias_grad: float32 [1024], P('wsh')
- second_gain_grad: float32 [1024], P('wsh')
- second_shift_grad: float32 [1024], P('wsh')
Inputs may be any that keep to these rules, and one draw needn't show every extreme that they name: `starts`: each row begins with 0 and rises strictly.
All inputs are finite; a program needn't handle non-finite values.
Results may differ from a plain program's by a relative error of at most 0.023.
Values may be sent and summed in bfloat16 or wider, within the bound.
No kernel may reach another device: no remote copies, remote signals or barrier semaphores. Data moves between devices by JAX's collectives and lax.ppermute only.
A program may use at most 320 MiB of HBM per device.

v0:
```python
import math

import jax
import jax.numpy as jnp
from jax import lax
from jax.sharding import PartitionSpec as P

HEADS = 16


def segment_ids(starts_row, length):
    positions = jnp.arange(length, dtype=jnp.int32)
    return jnp.sum((starts_row[None, :] <= positions[:, None]).astype(jnp.int32), axis=1) - 1


def layer_norm(residual, norm_gain, norm_shift):
    row_mean = jnp.mean(residual, axis=-1, keepdims=True)
    centered = residual - row_mean
    spread = jnp.mean(centered * centered, axis=-1, keepdims=True)
    return centered * lax.rsqrt(spread + 1e-05) * norm_gain + norm_shift


def exact_gelu(source):
    return jax.nn.gelu(source, approximate=False)


def split_heads(row_block):
    return row_block.reshape(row_block.shape[0], HEADS, row_block.shape[1] // HEADS)


def block_view(source, block_len):
    return source.reshape((source.shape[0] // block_len, block_len) + source.shape[1:])


def times_transposed(left_side, right_side):
    return lax.dot_general(
        left_side, right_side, (((1,), (1,)), ((), ())), preferred_element_type=jnp.float32
    )


def transposed_times(left_side, right_side):
    return lax.dot_general(
        left_side, right_side, (((0,), (0,)), ((), ())), preferred_element_type=jnp.float32
    )


def masked_scores(queries, key_block, seg_rows, seg_block):
    scores = jnp.einsum(
        "qhe,khe->hqk",
        split_heads(queries),
        split_heads(key_block),
        preferred_element_type=jnp.float32,
    )
    return jnp.where((seg_rows[:, None] == seg_block[None, :])[None], scores, -1e30)


def block_probs(queries, key_block, seg_rows, seg_block, maximum, row_total):
    scores = masked_scores(queries, key_block, seg_rows, seg_block)
    return jnp.exp(scores - maximum[:, :, None]) / row_total[:, :, None]


def score_gradient(attn_probs, mixed_grad, value_block, row_terms):
    dprobs = jnp.einsum(
        "qhe,khe->hqk",
        split_heads(mixed_grad),
        split_heads(value_block),
        preferred_element_type=jnp.float32,
    )
    return (attn_probs * (dprobs - row_terms[:, :, None])).astype(jnp.bfloat16)


def softmax_stats(queries, key_all, seg_rows, seg_all, block_len):
    local_rows = queries.shape[0]

    def softmax_visit_block(running, inputs):
        maximum, row_total = running
        scores = masked_scores(queries, inputs[0], seg_rows, inputs[1])
        new_max = jnp.maximum(maximum, jnp.max(scores, axis=2))
        row_total = row_total * jnp.exp(maximum - new_max) + jnp.sum(
            jnp.exp(scores - new_max[:, :, None]), axis=2
        )
        return ((new_max, row_total), None)

    start_state = (
        jnp.full((HEADS, local_rows), -1e30, jnp.float32),
        jnp.zeros((HEADS, local_rows), jnp.float32),
    )
    finished, _ = lax.scan(
        softmax_visit_block,
        start_state,
        (block_view(key_all, block_len), block_view(seg_all, block_len)),
    )
    return finished


def attend(queries, key_all, value_all, seg_rows, seg_all, maximum, row_total, block_len):
    local_rows = queries.shape[0]

    def attend_visit_block(running, inputs):
        key_block, value_block, seg_block = inputs
        attn_probs = block_probs(queries, key_block, seg_rows, seg_block, maximum, row_total)
        rounded = attn_probs.astype(jnp.bfloat16)
        remainder = (attn_probs - rounded.astype(jnp.float32)).astype(jnp.bfloat16)
        value_heads = split_heads(value_block)
        rounded_sum = running[0] + jnp.einsum(
            "hqk,khe->qhe", rounded, value_heads, preferred_element_type=jnp.float32
        )
        exact_sum = running[1] + jnp.einsum(
            "hqk,khe->qhe", remainder, value_heads, preferred_element_type=jnp.float32
        )
        return ((rounded_sum, exact_sum), None)

    zero_start = jnp.zeros((local_rows, HEADS, queries.shape[1] // HEADS), jnp.float32)
    finished, _ = lax.scan(
        attend_visit_block,
        (zero_start, zero_start),
        (
            block_view(key_all, block_len),
            block_view(value_all, block_len),
            block_view(seg_all, block_len),
        ),
    )
    return (finished[0], finished[0] + finished[1])


def joint_gradient(
    queries,
    key_all,
    value_all,
    seg_rows,
    seg_all,
    maximum,
    row_total,
    mixed_grad,
    row_terms,
    block_len,
):
    local_rows = queries.shape[0]
    model_width = queries.shape[1]

    def joint_visit_block(running, inputs):
        key_block, value_block, seg_block = inputs
        attn_probs = block_probs(queries, key_block, seg_rows, seg_block, maximum, row_total)
        score_grad = score_gradient(attn_probs, mixed_grad, value_block, row_terms)
        running = running + jnp.einsum(
            "hqk,khe->qhe", score_grad, split_heads(key_block), preferred_element_type=jnp.float32
        )
        key_term = jnp.einsum(
            "hqk,qhe->khe", score_grad, split_heads(queries), preferred_element_type=jnp.float32
        )
        value_term = jnp.einsum(
            "hqk,qhe->khe",
            attn_probs.astype(jnp.bfloat16),
            split_heads(mixed_grad),
            preferred_element_type=jnp.float32,
        )
        both = jnp.concatenate(
            [key_term.reshape(block_len, model_width), value_term.reshape(block_len, model_width)],
            axis=1,
        )
        return (running, both)

    zero_start = jnp.zeros((local_rows, HEADS, model_width // HEADS), jnp.float32)
    finished, term_blocks = lax.scan(
        joint_visit_block,
        zero_start,
        (
            block_view(key_all, block_len),
            block_view(value_all, block_len),
            block_view(seg_all, block_len),
        ),
    )
    return (finished, term_blocks.reshape(key_all.shape[0], 2 * model_width))


def local(
    tokens,
    starts,
    query_weight,
    key_weight,
    value_weight,
    output_weight,
    inner_weight,
    outer_weight,
    query_bias,
    value_bias,
    output_bias,
    first_gain,
    first_shift,
    inner_bias,
    outer_bias,
    second_gain,
    second_shift,
    cotangent,
):
    gathered = (
        lax.all_gather(query_weight, "wsh", axis=0, tiled=True),
        lax.all_gather(key_weight, "wsh", axis=0, tiled=True),
        lax.all_gather(value_weight, "wsh", axis=0, tiled=True),
        lax.all_gather(output_weight, "wsh", axis=0, tiled=True),
        lax.all_gather(inner_weight, "wsh", axis=0, tiled=True),
        lax.all_gather(outer_weight, "wsh", axis=0, tiled=True),
        lax.all_gather(query_bias, "wsh", axis=0, tiled=True),
        lax.all_gather(value_bias, "wsh", axis=0, tiled=True),
        lax.all_gather(output_bias, "wsh", axis=0, tiled=True),
        lax.all_gather(first_gain, "wsh", axis=0, tiled=True),
        lax.all_gather(first_shift, "wsh", axis=0, tiled=True),
        lax.all_gather(inner_bias, "wsh", axis=0, tiled=True),
        lax.all_gather(outer_bias, "wsh", axis=0, tiled=True),
        lax.all_gather(second_gain, "wsh", axis=0, tiled=True),
        lax.all_gather(second_shift, "wsh", axis=0, tiled=True),
    )
    (
        full_query,
        full_key,
        full_value,
        full_output,
        full_inner,
        full_outer,
        bias_query,
        bias_value,
        bias_output,
        gain_first,
        shift_first,
        bias_inner,
        bias_outer,
        gain_second,
        shift_second,
    ) = gathered
    inputs_low = tokens[0]
    local_rows = inputs_low.shape[0]
    model_width = inputs_low.shape[1]
    length = local_rows * lax.axis_size("ctx")
    block_len = math.gcd(1024, length)
    seg_all = segment_ids(starts[0], length)
    seg_rows = lax.dynamic_slice_in_dim(seg_all, lax.axis_index("ctx") * local_rows, local_rows)
    query_scale = (model_width // HEADS) ** (-0.5)
    inputs = inputs_low.astype(jnp.float32)
    queries = (
        (
            jnp.dot(inputs_low, full_query, preferred_element_type=jnp.float32)
            + bias_query.astype(jnp.float32)
        )
        * query_scale
    ).astype(jnp.bfloat16)
    key_rows = jnp.dot(inputs_low, full_key, preferred_element_type=jnp.float32).astype(
        jnp.bfloat16
    )
    value_rows = (
        jnp.dot(inputs_low, full_value, preferred_element_type=jnp.float32)
        + bias_value.astype(jnp.float32)
    ).astype(jnp.bfloat16)
    key_all, value_all = (
        lax.all_gather(key_rows, "ctx", axis=0, tiled=True),
        lax.all_gather(value_rows, "ctx", axis=0, tiled=True),
    )
    maximum, row_total = softmax_stats(queries, key_all, seg_rows, seg_all, block_len)
    rounded_sum, exact_sum = attend(
        queries, key_all, value_all, seg_rows, seg_all, maximum, row_total, block_len
    )
    mixed_low = rounded_sum.reshape(local_rows, model_width).astype(jnp.bfloat16)
    attn_out = jnp.dot(
        mixed_low, full_output, preferred_element_type=jnp.float32
    ) + bias_output.astype(jnp.float32)
    hidden, first_pull = jax.vjp(
        layer_norm,
        inputs + attn_out,
        gain_first.astype(jnp.float32),
        shift_first.astype(jnp.float32),
    )
    hidden_low = hidden.astype(jnp.bfloat16)
    inner_act = jnp.dot(
        hidden_low, full_inner, preferred_element_type=jnp.float32
    ) + bias_inner.astype(jnp.float32)
    act_value, act_pull = jax.vjp(exact_gelu, inner_act)
    act_low = act_value.astype(jnp.bfloat16)
    branch = jnp.dot(act_low, full_outer, preferred_element_type=jnp.float32) + bias_outer.astype(
        jnp.float32
    )
    normed, second_pull = jax.vjp(
        layer_norm,
        hidden + branch,
        gain_second.astype(jnp.float32),
        shift_second.astype(jnp.float32),
    )
    result = normed.astype(jnp.bfloat16)
    grad_second, second_gain_grad, second_shift_grad = second_pull(cotangent[0].astype(jnp.float32))
    branch_grad = grad_second.astype(jnp.bfloat16)
    outer_weight_grad = transposed_times(act_low, branch_grad)
    outer_bias_grad = jnp.sum(branch_grad.astype(jnp.float32), axis=0)
    act_grad = times_transposed(branch_grad, full_outer).astype(jnp.bfloat16)
    (inner_raw,) = act_pull(act_grad.astype(jnp.float32))
    inner_grad = inner_raw.astype(jnp.bfloat16)
    inner_weight_grad = transposed_times(hidden_low, inner_grad)
    inner_bias_grad = jnp.sum(inner_grad.astype(jnp.float32), axis=0)
    hidden_grad = grad_second + times_transposed(inner_grad, full_inner)
    grad_first, first_gain_grad, first_shift_grad = first_pull(hidden_grad)
    attn_grad = grad_first.astype(jnp.bfloat16)
    output_weight_grad = transposed_times(mixed_low, attn_grad)
    output_bias_grad = jnp.sum(attn_grad.astype(jnp.float32), axis=0)
    mixed_grad = times_transposed(attn_grad, full_output).astype(jnp.bfloat16)
    row_terms = jnp.einsum("qhe,qhe->hq", split_heads(mixed_grad).astype(jnp.float32), exact_sum)
    back_keys, back_values = (
        lax.all_gather(key_rows, "ctx", axis=0, tiled=True),
        lax.all_gather(value_rows, "ctx", axis=0, tiled=True),
    )
    query_raw, all_terms = joint_gradient(
        queries,
        back_keys,
        back_values,
        seg_rows,
        seg_all,
        maximum,
        row_total,
        mixed_grad,
        row_terms,
        block_len,
    )
    summed = lax.psum_scatter(
        all_terms.astype(jnp.bfloat16), "ctx", scatter_dimension=0, tiled=True
    ).astype(jnp.float32)
    key_grad = summed[:, :model_width].astype(jnp.bfloat16)
    value_grad = summed[:, model_width:].astype(jnp.bfloat16)
    query_grad = query_raw.reshape(local_rows, model_width).astype(jnp.bfloat16)
    query_weight_grad = transposed_times(inputs_low, query_grad) * query_scale
    query_bias_grad = jnp.sum(query_grad.astype(jnp.float32), axis=0) * query_scale
    key_weight_grad = transposed_times(inputs_low, key_grad)
    value_weight_grad = transposed_times(inputs_low, value_grad)
    value_bias_grad = jnp.sum(value_grad.astype(jnp.float32), axis=0)
    input_grad = (
        grad_first
        + query_scale * times_transposed(query_grad, full_query)
        + times_transposed(key_grad, full_key)
        + times_transposed(value_grad, full_value)
    )
    owner_parts = (
        lax.psum_scatter(
            query_weight_grad.astype(jnp.bfloat16), "wsh", scatter_dimension=0, tiled=True
        ).astype(jnp.float32),
        lax.psum_scatter(
            key_weight_grad.astype(jnp.bfloat16), "wsh", scatter_dimension=0, tiled=True
        ).astype(jnp.float32),
        lax.psum_scatter(
            value_weight_grad.astype(jnp.bfloat16), "wsh", scatter_dimension=0, tiled=True
        ).astype(jnp.float32),
        lax.psum_scatter(
            output_weight_grad.astype(jnp.bfloat16), "wsh", scatter_dimension=0, tiled=True
        ).astype(jnp.float32),
        lax.psum_scatter(
            inner_weight_grad.astype(jnp.bfloat16), "wsh", scatter_dimension=0, tiled=True
        ).astype(jnp.float32),
        lax.psum_scatter(
            outer_weight_grad.astype(jnp.bfloat16), "wsh", scatter_dimension=0, tiled=True
        ).astype(jnp.float32),
        lax.psum_scatter(
            query_bias_grad.astype(jnp.bfloat16), "wsh", scatter_dimension=0, tiled=True
        ).astype(jnp.float32),
        lax.psum_scatter(
            value_bias_grad.astype(jnp.bfloat16), "wsh", scatter_dimension=0, tiled=True
        ).astype(jnp.float32),
        lax.psum_scatter(
            output_bias_grad.astype(jnp.bfloat16), "wsh", scatter_dimension=0, tiled=True
        ).astype(jnp.float32),
        lax.psum_scatter(
            first_gain_grad.astype(jnp.bfloat16), "wsh", scatter_dimension=0, tiled=True
        ).astype(jnp.float32),
        lax.psum_scatter(
            first_shift_grad.astype(jnp.bfloat16), "wsh", scatter_dimension=0, tiled=True
        ).astype(jnp.float32),
        lax.psum_scatter(
            inner_bias_grad.astype(jnp.bfloat16), "wsh", scatter_dimension=0, tiled=True
        ).astype(jnp.float32),
        lax.psum_scatter(
            outer_bias_grad.astype(jnp.bfloat16), "wsh", scatter_dimension=0, tiled=True
        ).astype(jnp.float32),
        lax.psum_scatter(
            second_gain_grad.astype(jnp.bfloat16), "wsh", scatter_dimension=0, tiled=True
        ).astype(jnp.float32),
        lax.psum_scatter(
            second_shift_grad.astype(jnp.bfloat16), "wsh", scatter_dimension=0, tiled=True
        ).astype(jnp.float32),
    )
    totals = (
        lax.psum(owner_parts[0].astype(jnp.bfloat16), "ctx").astype(jnp.float32),
        lax.psum(owner_parts[1].astype(jnp.bfloat16), "ctx").astype(jnp.float32),
        lax.psum(owner_parts[2].astype(jnp.bfloat16), "ctx").astype(jnp.float32),
        lax.psum(owner_parts[3].astype(jnp.bfloat16), "ctx").astype(jnp.float32),
        lax.psum(owner_parts[4].astype(jnp.bfloat16), "ctx").astype(jnp.float32),
        lax.psum(owner_parts[5].astype(jnp.bfloat16), "ctx").astype(jnp.float32),
        lax.psum(owner_parts[6].astype(jnp.bfloat16), "ctx").astype(jnp.float32),
        lax.psum(owner_parts[7].astype(jnp.bfloat16), "ctx").astype(jnp.float32),
        lax.psum(owner_parts[8].astype(jnp.bfloat16), "ctx").astype(jnp.float32),
        lax.psum(owner_parts[9].astype(jnp.bfloat16), "ctx").astype(jnp.float32),
        lax.psum(owner_parts[10].astype(jnp.bfloat16), "ctx").astype(jnp.float32),
        lax.psum(owner_parts[11].astype(jnp.bfloat16), "ctx").astype(jnp.float32),
        lax.psum(owner_parts[12].astype(jnp.bfloat16), "ctx").astype(jnp.float32),
        lax.psum(owner_parts[13].astype(jnp.bfloat16), "ctx").astype(jnp.float32),
        lax.psum(owner_parts[14].astype(jnp.bfloat16), "ctx").astype(jnp.float32),
    )
    return (
        result[None],
        input_grad.astype(jnp.bfloat16)[None],
        totals[0],
        totals[1],
        totals[2],
        totals[3],
        totals[4],
        totals[5],
        totals[6],
        totals[7],
        totals[8],
        totals[9],
        totals[10],
        totals[11],
        totals[12],
        totals[13],
        totals[14],
    )


def solution(mesh):
    return jax.shard_map(
        local,
        mesh=mesh,
        in_specs=(
            P("wsh", "ctx", None),
            P("wsh", None),
            P("wsh", None),
            P("wsh", None),
            P("wsh", None),
            P("wsh", None),
            P("wsh", None),
            P("wsh", None),
            P("wsh"),
            P("wsh"),
            P("wsh"),
            P("wsh"),
            P("wsh"),
            P("wsh"),
            P("wsh"),
            P("wsh"),
            P("wsh"),
            P("wsh", "ctx", None),
        ),
        out_specs=(
            P("wsh", "ctx", None),
            P("wsh", "ctx", None),
            P("wsh", None),
            P("wsh", None),
            P("wsh", None),
            P("wsh", None),
            P("wsh", None),
            P("wsh", None),
            P("wsh"),
            P("wsh"),
            P("wsh"),
            P("wsh"),
            P("wsh"),
            P("wsh"),
            P("wsh"),
            P("wsh"),
            P("wsh"),
        ),
        check_vma=False,
    )
```

profile of v0, /device:TPU:9, one launch (start us, length us, event | category | flops | bytes accessed | tf_op | source)
XLA Modules:
  0.0 1401.3 jit_solution(11585988571039204624)
XLA Ops:
  16.3 38.5 %all-gather.17.cloned.1.call-done = bf16[1024,1024]{1,0:T(8,128)(2,1)} async-done(((bf16[256,1024]{1,0:T(8,128)(2,1)}), bf16[1024,1024]{1,0:T(8,128)(2,1)}) %all-gather.17.cloned.1.call-update) | async-done | bytes 2097168 | tf_op jit(solution)/shard_map/all_gather | solution.py:199
  58.3 42.8 %all-gather.21.cloned.1.call-done = bf16[1024,1024]{1,0:T(8,128)(2,1)} async-done(((bf16[256,1024]{1,0:T(8,128)(2,1)}), bf16[1024,1024]{1,0:T(8,128)(2,1)}) %all-gather.21.cloned.1.call-update) | async-done | bytes 2097168 | tf_op jit(solution)/shard_map/all_gather | solution.py:198
  106.5 8.3 all-gather.5
  115.4 8.9 all_gather.65
  124.9 8.1 all-gather.2
  133.8 6.6 all-gather.1
  140.4 7.1 all-gather.4
  148.1 6.6 all-gather.3
  155.3 7.3 all-gather.6
  172.1 15.6 %all-gather.19.cloned.1.call-done = bf16[2048,1024]{1,0:T(8,128)(2,1)} async-done(((bf16[256,1024]{1,0:T(8,128)(2,1)}), bf16[2048,1024]{1,0:T(8,128)(2,1)}) %all-gather.19.cloned.1.call-update) | async-done | bytes 4194320 | tf_op jit(solution)/shard_map/all_gather | solution.py:255
  187.7 6.3 copy.97
  194.1 32.7 %all-gather.23.cloned.1.call-done = bf16[2048,1024]{1,0:T(8,128)(2,1)} async-done(((bf16[256,1024]{1,0:T(8,128)(2,1)}), bf16[2048,1024]{1,0:T(8,128)(2,1)}) %all-gather.23.cloned.1.call-update) | async-done | bytes 4194320 | tf_op jit(solution)/shard_map/all_gather | solution.py:254
  233.0 37.9 %while.39 = (s32[]{:T(128)}, f32[16,256]{1,0:T(8,128)S(1)}, f32[16,256]{1,0:T(8,128)S(1)}, s32[256]{0:T(256)S(1)}, s32[2,1024]{1,0:T(2,128)S(1)}, /*index=5*/bf1...) while((s32[]{:T(128)}, f32[16,256]{1,0:T(8,128)S(1)}, ...), condition=%wide.region_4.5_spmd.clone, body=%wide.region_1.4_spmd.clone.sunk | while | flops 558125056 | bytes 41383028 | solution.py:88
  235.0 8.3 fusion.144
  243.2 8.7 exponential_reduce_fusion.2
  254.0 8.3 fusion.144
  262.3 8.6 exponential_reduce_fusion.2
  270.9 52.3 %while.40 = (s32[]{:T(128)}, f32[256,16,64]{0,2,1:T(8,128)}, f32[256,16,64]{0,2,1:T(8,128)}, bf16[2,1024,1024]{1,2,0:T(8,128)(2,1)}, s32[256]{0:T(256)S(1)}, /*i...) while((s32[]{:T(128)}, f32[256,16,64]{0,2,1:T(8,128)}, ...), condition=%wide.region_6.7_spmd.clone, body=%wide.region_5.6_spmd.clone.sunk | while | flops 1645477888 | bytes 145798384 | solution.py:114
  273.9 8.1 fusion.151
  282.0 10.0 fusion.152
  300.5 8.0 fusion.151
  308.5 8.8 fusion.152
  327.7 93.2 %all-gather.29.cloned.1.call-done = bf16[1024,4096]{1,0:T(8,128)(2,1)} async-done(((bf16[256,4096]{1,0:T(8,128)(2,1)}), bf16[1024,4096]{1,0:T(8,128)(2,1)}) %all-gather.29.cloned.1.call-update) | async-done | bytes 8388624 | tf_op jit(solution)/shard_map/all_gather | solution.py:201
  420.9 16.1 %multiply_convert_fusion.1 = (bf16[256,4096]{1,0:T(8,128)(2,1)}, f32[256,4096]{1,0:T(8,128)}, f32[256,4096]{1,0:T(8,128)}) fusion(f32[4096]{0:T(1024)S(1)} %copy-done.44, bf16[1024,4096]{1,0:T(8,128)(2,1)} %all-gather.29.cloned.1.call-done, f32[256,1024]{1,0:T(8,128)S(1)} %get-tuple-element.564, f32[1024]{0:T(1024)S(1)} %bitcast.256, ...), kind=kOutput, calls=%fused_computation.58 | convolution fusion | flops 2218000384 | bytes 19949568 | tf_op jit(solution)/shard_map/dot_general | solution.py:272
  437.1 133.3 %all-gather.31.cloned.1.call-done = bf16[4096,1024]{1,0:T(8,128)(2,1)} async-done(((bf16[1024,1024]{1,0:T(8,128)(2,1)}), bf16[4096,1024]{1,0:T(8,128)(2,1)}) %all-gather.31.cloned.1.call-update) | async-done | bytes 8388624 | tf_op jit(solution)/shard_map/all_gather | solution.py:202
  570.4 6.5 fusion.73
  580.3 12.3 fusion.74
  603.8 117.3 %while.41 = (s32[]{:T(128)}, f32[256,16,64]{0,2,1:T(8,128)S(1)}, bf16[2,1024,2048]{2,1,0:T(8,128)(2,1)}, bf16[2,1024,1024]{1,2,0:T(8,128)(2,1)}, s32[256]{0:T(25...) while((s32[]{:T(128)}, f32[256,16,64]{0,2,1:T(8,128)S(1)}, ...), condition=%wide.region_16.17_spmd.clone, body=%wide.region_15.16_spmd.clone.sunk | while | flops 2722889728 | bytes 130610416 | solution.py:164
  609.0 7.9 fusion.164
  616.9 12.2 fusion.165
  634.1 8.5 fusion.167
  651.1 6.6 copy.138
  667.6 7.9 fusion.164
  675.4 12.2 fusion.165
  692.7 8.5 fusion.167
  709.6 6.6 copy.138
  726.7 66.9 %reduce-scatter.8.cloned.1.call-done = bf16[256,2048]{1,0:T(8,128)(2,1)} async-done(((bf16[2048,2048]{1,0:T(8,128)(2,1)}), bf16[256,2048]{1,0:T(8,128)(2,1)}) %reduce-scatter.8.cloned.1.call-update) | async-done | bytes 1048592 | tf_op jit(solution)/shard_map/reduce_scatter | solution.py:319
  799.1 7.4 convolution_convert_fusion.1
  807.5 7.3 convolution_convert_fusion
  814.9 23.0 %reduce-scatter.10.cloned.1.call-done = bf16[256,1024]{0,1:T(8,128)(2,1)} async-done(((bf16[1024,1024]{0,1:T(8,128)(2,1)}), bf16[256,1024]{0,1:T(8,128)(2,1)}) %reduce-scatter.10.cloned.1.call-update) | async-done | bytes 524304 | tf_op jit(solution)/shard_map/reduce_scatter | solution.py:337
  837.9 45.5 %reduce-scatter.16.cloned.1.call-done = bf16[256,1024]{1,0:T(8,128)(2,1)} async-done(((bf16[1024,1024]{1,0:T(8,128)(2,1)}), bf16[256,1024]{1,0:T(8,128)(2,1)}) %reduce-scatter.16.cloned.1.call-update) | async-done | bytes 524304 | tf_op jit(solution)/shard_map/reduce_scatter | solution.py:346
  883.4 46.0 %reduce-scatter.12.cloned.1.call-done = bf16[256,1024]{0,1:T(8,128)(2,1)} async-done(((bf16[1024,1024]{0,1:T(8,128)(2,1)}), bf16[256,1024]{0,1:T(8,128)(2,1)}) %reduce-scatter.12.cloned.1.call-update) | async-done | bytes 524304 | tf_op jit(solution)/shard_map/reduce_scatter | solution.py:340
  929.4 45.5 %reduce-scatter.14.cloned.1.call-done = bf16[256,1024]{0,1:T(8,128)(2,1)} async-done(((bf16[1024,1024]{0,1:T(8,128)(2,1)}), bf16[256,1024]{0,1:T(8,128)(2,1)}) %reduce-scatter.14.cloned.1.call-update) | async-done | bytes 524304 | tf_op jit(solution)/shard_map/reduce_scatter | solution.py:343
  975.0 148.3 %reduce-scatter.18.cloned.1.call-done = bf16[256,4096]{1,0:T(8,128)(2,1)} async-done(((bf16[1024,4096]{1,0:T(8,128)(2,1)}), bf16[256,4096]{1,0:T(8,128)(2,1)}) %reduce-scatter.18.cloned.1.call-update) | async-done | bytes 2097168 | tf_op jit(solution)/shard_map/reduce_scatter | solution.py:349
  1123.2 147.5 %reduce-scatter.20.cloned.1.call-done = bf16[1024,1024]{1,0:T(8,128)(2,1)} async-done(((bf16[4096,1024]{1,0:T(8,128)(2,1)}), bf16[1024,1024]{1,0:T(8,128)(2,1)}) %reduce-scatter.20.cloned.1.call-update) | async-done | bytes 2097168 | tf_op jit(solution)/shard_map/reduce_scatter | solution.py:352
  1276.5 12.8 all-reduce.11
  1289.9 15.7 %all-reduce.9 = (bf16[256]{0:T(256)(128)(2,1)S(1)}, bf16[256]{0:T(256)(128)(2,1)S(1)}, bf16[256]{0:T(256)(128)(2,1)S(1)}, bf16[256]{0:T(256)(128)(2,1)S(1)}, bf1...) all-reduce(bf16[256]{0:T(256)(128)(2,1)S(1)} %dynamic-slice.1, ...), channel_id=1, replica_groups=mesh['ctx'=8,'wsh'=4] {'ctx'}, use_global_device_ids=true, to_apply=%region_32.33 | all-reduce | flops 3072 | bytes 12288 | tf_op jit(solution)/shard_map/psum | solution.py:390
  1314.9 66.8 %all-reduce.14.cloned.1.call-done = (bf16[256,1024]{0,1:T(8,128)(2,1)}, bf16[256,1024]{0,1:T(8,128)(2,1)}, bf16[256,1024]{0,1:T(8,128)(2,1)}, bf16[256,1024]{1,0...) async-done(((bf16[256,1024]{0,1:T(8,128)(2,1)}, bf16[256,1024]{0,1:T(8,128)(2,1)}, bf16[256,1024]{0,1:T(8,128)(2,1)}, bf16[256,1024]{1,0:T(8,128)(2,1)}, ...) | async-done | bytes 6291472 | tf_op jit(solution)/shard_map/psum | solution.py:384
  (305 shorter events, 162.2 us)
Async XLA Ops:
  7.2 93.9 %copy-start.13 = (bf16[1,256,1024]{2,1,0:T(8,128)(2,1)S(1)}, bf16[1,256,1024]{2,1,0:T(8,128)(2,1)}, u32[]{:S(2)}) copy-start(bf16[1,256,1024]{2,1,0:T(8,128)(2,1)} %param.24) | copy-start | bytes 1572868
  7.2 47.7 %all-gather.17.cloned.1.call-start = ((), (), s32[]{:S(2)}) async-start(), calls=%async_computation.7 | async-start | bytes 2621440 | tf_op jit(solution)/shard_map/all_gather | solution.py:199
  7.9 93.2 %all-gather.21.cloned.1.call-start = ((), (), s32[]{:S(2)}) async-start(), calls=%async_computation.9 | async-start | bytes 2621440 | tf_op jit(solution)/shard_map/all_gather | solution.py:198
  8.7 160.9 %all-gather.25.cloned.1.call-start = ((), (), s32[]{:S(2)}) async-start(), calls=%async_computation.11 | async-start | bytes 2621440 | tf_op jit(solution)/shard_map/all_gather | solution.py:197
  9.4 178.3 %all-gather.19.cloned.1.call-start = ((), (), s32[]{:S(2)}) async-start(), calls=%async_computation.8 | async-start | bytes 4718592 | tf_op jit(solution)/shard_map/all_gather | solution.py:255
  58.2 48.3 %copy-start.56 = (bf16[256]{0:T(256)(128)(2,1)S(1)}, bf16[256]{0:T(256)(128)(2,1)}, u32[]{:S(2)}) copy-start(bf16[256]{0:T(256)(128)(2,1)} %param.38) | copy-start | bytes 1540
  58.2 57.2 %copy-start.52 = (bf16[1024]{0:T(1024)(128)(2,1)S(1)}, bf16[1024]{0:T(1024)(128)(2,1)}, u32[]{:S(2)}) copy-start(bf16[1024]{0:T(1024)(128)(2,1)} %param.37) | copy-start | bytes 6148
  58.2 66.7 %copy-start.57 = (bf16[256]{0:T(256)(128)(2,1)S(1)}, bf16[256]{0:T(256)(128)(2,1)}, u32[]{:S(2)}) copy-start(bf16[256]{0:T(256)(128)(2,1)} %param.34) | copy-start | bytes 1540
  58.2 75.3 %copy-start.55 = (s32[1,8]{1,0:T(1,128)S(1)}, s32[1,8]{1,0:T(1,128)}, u32[]{:S(2)}) copy-start(s32[1,8]{1,0:T(1,128)} %param.25) | copy-start | bytes 100
  58.2 75.5 %copy-start.58 = (bf16[256]{0:T(256)(128)(2,1)S(1)}, bf16[256]{0:T(256)(128)(2,1)}, u32[]{:S(2)}) copy-start(bf16[256]{0:T(256)(128)(2,1)} %param.32) | copy-start | bytes 1540
  58.2 82.2 %copy-start.59 = (bf16[256]{0:T(256)(128)(2,1)S(1)}, bf16[256]{0:T(256)(128)(2,1)}, u32[]{:S(2)}) copy-start(bf16[256]{0:T(256)(128)(2,1)} %param.36) | copy-start | bytes 1540
  58.2 89.9 %copy-start.60 = (bf16[256]{0:T(256)(128)(2,1)S(1)}, bf16[256]{0:T(256)(128)(2,1)}, u32[]{:S(2)}) copy-start(bf16[256]{0:T(256)(128)(2,1)} %param.35) | copy-start | bytes 1540
  58.3 97.0 %copy-start.61 = (bf16[256]{0:T(256)(128)(2,1)S(1)}, bf16[256]{0:T(256)(128)(2,1)}, u32[]{:S(2)}) copy-start(bf16[256]{0:T(256)(128)(2,1)} %param.39) | copy-start | bytes 1540
  58.3 105.0 %copy-start.62 = (bf16[256]{0:T(256)(128)(2,1)S(1)}, bf16[256]{0:T(256)(128)(2,1)}, u32[]{:S(2)}) copy-start(bf16[256]{0:T(256)(128)(2,1)} %param.40) | copy-start | bytes 1540
  58.3 168.5 %all-gather.23.cloned.1.call-start = ((), (), s32[]{:S(2)}) async-start(), calls=%async_computation.10 | async-start | bytes 4718592 | tf_op jit(solution)/shard_map/all_gather | solution.py:254
  104.2 220.5 %all-gather.27.cloned.1.call-start = ((), (), s32[]{:S(2)}) async-start(), calls=%async_computation.12 | async-start | bytes 2621440 | tf_op jit(solution)/shard_map/all_gather | solution.py:200
  104.8 316.1 %all-gather.29.cloned.1.call-start = ((), (), s32[]{:S(2)}) async-start(), calls=%async_computation.13 | async-start | bytes 10485760 | tf_op jit(solution)/shard_map/all_gather | solution.py:201
  105.6 464.8 %all-gather.31.cloned.1.call-start = ((), (), s32[]{:S(2)}) async-start(), calls=%async_computation.14 | async-start | bytes 10485760 | tf_op jit(solution)/shard_map/all_gather | solution.py:202
  106.3 687.2 %reduce-scatter.8.cloned.1.call-start = ((), (), s32[]{:S(2)}) async-start(), calls=%async_computation.15 | async-start | bytes 9437184 | tf_op jit(solution)/shard_map/reduce_scatter | solution.py:319
  270.9 53.9 %copy-start.14 = (bf16[1,256,1024]{2,1,0:T(8,128)(2,1)S(1)}, bf16[1,256,1024]{2,1,0:T(8,128)(2,1)}, u32[]{:S(2)}) copy-start(bf16[1,256,1024]{2,1,0:T(8,128)(2,1)} %param.24) | copy-start | bytes 1572868
  270.9 53.9 %copy-start.37 = (f32[4,1,256]{2,1,0:T(1,128)S(1)}, f32[4,1,256]{2,1,0:T(1,128)}, u32[]{:S(2)}) copy-start(f32[4,1,256]{2,1,0:T(1,128)} %convert_element_type.312) | copy-start | bytes 12292
  282.0 12.5 copy-start
  282.0 12.7 copy-start.7
  308.5 11.6 copy-start.7
  323.2 113.8 %copy-start.4 = (bf16[256,1024]{0,1:T(8,128)(2,1)}, bf16[256,1024]{0,1:T(8,128)(2,1)S(1)}, u32[]{:S(2)}) copy-start(bf16[256,1024]{0,1:T(8,128)(2,1)S(1)} %get-tuple-element.896) | copy-start | bytes 1572868
  323.3 97.6 %copy-start.33 = (f32[4,1,256]{2,1,0:T(1,128)S(1)}, f32[4,1,256]{2,1,0:T(1,128)}, u32[]{:S(2)}) copy-start(f32[4,1,256]{2,1,0:T(1,128)} %convert_element_type.313) | copy-start | bytes 12292
  323.3 97.6 %copy-start.35 = (f32[4,1,256]{2,1,0:T(1,128)S(1)}, f32[4,1,256]{2,1,0:T(1,128)}, u32[]{:S(2)}) copy-start(f32[4,1,256]{2,1,0:T(1,128)} %convert_element_type.314) | copy-start | bytes 12292
  323.3 97.6 %copy-start.44 = (f32[4096]{0:T(1024)S(1)}, f32[4096]{0:T(1024)}, u32[]{:S(2)}) copy-start(f32[4096]{0:T(1024)} %convert_element_type.260) | copy-start | bytes 49156
  324.8 112.3 %copy-start.17 = (bf16[256,16,64]{0,2,1:T(8,128)(2,1)}, bf16[256,16,64]{0,2,1:T(8,128)(2,1)S(1)}, u32[]{:S(2)}) copy-start(bf16[256,16,64]{0,2,1:T(8,128)(2,1)S(1)} %convert_element_type.254) | copy-start | bytes 1572868
  327.4 265.2 %copy-start.9 = (f32[256,1024]{1,0:T(8,128)}, f32[256,1024]{1,0:T(8,128)S(1)}, u32[]{:S(2)}) copy-start(f32[256,1024]{1,0:T(8,128)S(1)} %get-tuple-element.564) | copy-start | bytes 3145732
  327.4 268.5 %copy-start.39 = (f32[256]{0:T(256)}, f32[256]{0:T(256)S(1)}, u32[]{:S(2)}) copy-start(f32[256]{0:T(256)S(1)} %broadcast_multiply_fusion.1) | copy-start | bytes 3076
  327.7 268.2 %copy-start.41 = (f32[256]{0:T(256)}, f32[256]{0:T(256)S(1)}, u32[]{:S(2)}) copy-start(f32[256]{0:T(256)S(1)} %fusion.63) | copy-start | bytes 3076
  420.9 149.5 %copy-start.51 = (f32[4,1,256]{2,1,0:T(1,128)S(1)}, f32[4,1,256]{2,1,0:T(1,128)}, u32[]{:S(2)}) copy-start(f32[4,1,256]{2,1,0:T(1,128)} %convert_element_type.315) | copy-start | bytes 12292
  578.2 14.4 %slice-start = ((s8[8388608]{0:T(1024)(128)(4,1)}), s8[4194304]{0:T(1024)(128)(4,1)S(1)}, s32[]{:S(2)}) async-start(s8[8388608]{0:T(1024)(128)(4,1)} %bitcast.267), calls=%async_computation.23 | async-start | bytes 8388608
  580.3 12.3 copy-start.23
  580.3 12.3 slice-start.1
  721.1 116.8 %reduce-scatter.10.cloned.1.call-start = ((), (), s32[]{:S(2)}) async-start(), calls=%async_computation.16 | async-start | bytes 2621440 | tf_op jit(solution)/shard_map/reduce_scatter | solution.py:337
  724.2 159.2 %reduce-scatter.16.cloned.1.call-start = ((), (), s32[]{:S(2)}) async-start(), calls=%async_computation.19 | async-start | bytes 2621440 | tf_op jit(solution)/shard_map/reduce_scatter | solution.py:346
  726.6 202.8 %reduce-scatter.12.cloned.1.call-start = ((), (), s32[]{:S(2)}) async-start(), calls=%async_computation.17 | async-start | bytes 2621440 | tf_op jit(solution)/shard_map/reduce_scatter | solution.py:340
  796.8 178.2 %reduce-scatter.14.cloned.1.call-start = ((), (), s32[]{:S(2)}) async-start(), calls=%async_computation.18 | async-start | bytes 2621440 | tf_op jit(solution)/shard_map/reduce_scatter | solution.py:343
  799.0 324.3 %reduce-scatter.18.cloned.1.call-start = ((), (), s32[]{:S(2)}) async-start(), calls=%async_computation.20 | async-start | bytes 10485760 | tf_op jit(solution)/shard_map/reduce_scatter | solution.py:349
  806.5 464.3 %reduce-scatter.20.cloned.1.call-start = ((), (), s32[]{:S(2)}) async-start(), calls=%async_computation.21 | async-start | bytes 10485760 | tf_op jit(solution)/shard_map/reduce_scatter | solution.py:352
  814.8 456.1 %copy-start.22 = (bf16[1,256,1024]{2,1,0:T(8,128)(2,1)S(1)}, bf16[1,256,1024]{2,1,0:T(8,128)(2,1)}, u32[]{:S(2)}) copy-start(bf16[1,256,1024]{2,1,0:T(8,128)(2,1)} %param.41) | copy-start | bytes 1572868
  814.8 456.2 %copy-start.63 = (u32[32]{0:T(128)S(1)}, u32[32]{0:T(128)}, u32[]{:S(2)}) copy-start(u32[32]{0:T(128)} %constant.150) | copy-start | bytes 388
  814.8 458.2 %copy-start.12 = (f32[256,1024]{1,0:T(8,128)S(1)}, f32[256,1024]{1,0:T(8,128)}, u32[]{:S(2)}) copy-start(f32[256,1024]{1,0:T(8,128)} %copy-done.11) | copy-start | bytes 3145732
  814.8 458.2 %copy-start.20 = (bf16[256,16,64]{0,2,1:T(8,128)(2,1)S(1)}, bf16[256,16,64]{0,2,1:T(8,128)(2,1)}, u32[]{:S(2)}) copy-start(bf16[256,16,64]{0,2,1:T(8,128)(2,1)} %copy-done.19) | copy-start | bytes 1572868
  814.8 458.2 %copy-start.46 = (f32[256]{0:T(256)S(1)}, f32[256]{0:T(256)}, u32[]{:S(2)}) copy-start(f32[256]{0:T(256)} %copy-done.45) | copy-start | bytes 3076
  814.8 566.9 %all-reduce.14.cloned.1.call-start = ((), (), s32[]{:S(2)}) async-start(), calls=%async_computation.22 | async-start | bytes 12582912 | tf_op jit(solution)/shard_map/psum | solution.py:384
  (40 other events, 166.9 us)
Sparse Core Ops, SparseCore 0:
  9.6 45.2 all-gather.16
  56.4 44.6 all-gather.20
  102.7 45.0 all-gather.24
  150.1 37.5 all-gather.18
  190.0 36.7 all-gather.22
  228.2 43.6 all-gather.26
  273.5 147.3 all-gather.28
  422.5 147.8 all-gather.30
  721.2 72.3 reduce-scatter.7
  796.4 41.4 reduce-scatter.9
  840.2 43.1 reduce-scatter.15
  886.2 43.1 reduce-scatter.11
  931.7 43.1 reduce-scatter.13
  977.3 145.9 reduce-scatter.17
  1125.6 145.1 reduce-scatter.19
  1275.2 106.4 all-reduce.13
where the time goes:
time: 1410 us; the launch traced here: 1400 us
  waiting for transfers between devices  950 us (67%)
  matrix products  217 us (15%)
  blocking collectives  93.4 us (7%)
  local copies, waits for them, and re-layouts  74.8 us (5%)
  other arithmetic  48.4 us (3%)
  between operations  16.3 us (1%)
    reduce_scatter x1, waiting for transfers between devices, local(): lax.psum_scatter(inner_weight_grad.astype(jnp.bfloat16), 'wsh', scatter_d...  148 us
    reduce_scatter x1, waiting for transfers between devices, local(): lax.psum_scatter(outer_weight_grad.astype(jnp.bfloat16), 'wsh', scatter_d...  148 us
    all_gather x1, waiting for transfers between devices, local(): lax.all_gather(outer_weight, 'wsh', axis=0, tiled=True)  133 us
    all_gather x1, waiting for transfers between devices, local(): lax.all_gather(inner_weight, 'wsh', axis=0, tiled=True)  93.2 us
    reduce_scatter x1, waiting for transfers between devices, local(): lax.psum_scatter(all_terms.astype(jnp.bfloat16), 'ctx', scatter_dimension...  66.9 us
    psum x1, waiting for transfers between devices, local(): lax.psum(owner_parts[0].astype(jnp.bfloat16), 'ctx').astype(jnp.float32)  66.8 us
    dot_general x6, matrix products, masked_scores(): jnp.einsum('qhe,khe->hqk', split_heads(queries), split_heads(key_block),...  48.4 us
    reduce_scatter x1, waiting for transfers between devices, local(): lax.psum_scatter(key_weight_grad.astype(jnp.bfloat16), 'wsh', scatter_dim...  46 us
  transfers between devices with their start and end apart: 16, of which 14 were waited for; matrix products, arithmetic and copies ran while one was open for 12% of the time, Pallas kernels for 0%

commit v1 on v0

v1 whole, which is shorter than its diff:
```python
import functools

import jax
import jax.numpy as jnp
from jax import lax
from jax.experimental import pallas as pl
from jax.experimental.pallas import tpu as pltpu
from jax.sharding import PartitionSpec as P

HEADS = 16
LANES = 128
BF = jnp.bfloat16
F32 = jnp.float32
VMEM = 60 * 1024 * 1024


def dot(a, b):
    return lax.dot_general(a, b, (((1,), (0,)), ((), ())), preferred_element_type=F32)


def dot_nt(a, b):
    return lax.dot_general(a, b, (((1,), (1,)), ((), ())), preferred_element_type=F32)


def dot_tn(a, b):
    return lax.dot_general(a, b, (((0,), (0,)), ((), ())), preferred_element_type=F32)


def params(semantics=None):
    return pltpu.CompilerParams(vmem_limit_bytes=VMEM, dimension_semantics=semantics)


def as_row(column):
    return jnp.broadcast_to(column, (column.shape[0], LANES)).T[0:1, :]


def attend_kernel(q_ref, k_ref, v_ref, o_ref, lse_ref):
    scores = dot_nt(q_ref[0], k_ref[0])
    top = jnp.max(scores, axis=1, keepdims=True)
    probs = jnp.exp(scores - top)
    total = jnp.sum(probs, axis=1, keepdims=True)
    o_ref[0] = dot(probs.astype(BF), v_ref[0]) / total
    lse_ref[0] = as_row(top + jnp.log(total))


def attend(q, k, v, rows):
    heads, length, wide = q.shape
    size = v.shape[2]
    return pl.pallas_call(
        attend_kernel,
        grid=(heads, length // rows),
        in_specs=[
            pl.BlockSpec((1, rows, wide), lambda h, i: (h, i, 0)),
            pl.BlockSpec((1, length, wide), lambda h, i: (h, 0, 0)),
            pl.BlockSpec((1, length, size), lambda h, i: (h, 0, 0)),
        ],
        out_specs=[
            pl.BlockSpec((1, rows, size), lambda h, i: (h, i, 0)),
            pl.BlockSpec((1, 1, rows), lambda h, i: (h, 0, i)),
        ],
        out_shape=[
            jax.ShapeDtypeStruct((heads, length, size), F32),
            jax.ShapeDtypeStruct((heads, 1, length), F32),
        ],
        compiler_params=params(),
        name="attend",
    )(q, k, v)


def attend_back_kernel(
    q_ref, k_ref, v_ref, kt_ref, mg_ref, o_ref, lse_ref, dqt_ref, dk_ref, dv_ref, dk_acc, dv_acc
):
    step = pl.program_id(1)
    size = v_ref.shape[2]

    @pl.when(step == 0)
    def _():
        dk_acc[...] = jnp.zeros_like(dk_acc)
        dv_acc[...] = jnp.zeros_like(dv_acc)

    q = q_ref[0]
    mg = mg_ref[0]
    row_terms = as_row(jnp.sum(mg.astype(F32) * o_ref[0], axis=1, keepdims=True))
    probs = jnp.exp(dot_nt(k_ref[0], q) - lse_ref[0])
    dv_acc[...] += dot(probs.astype(BF), mg)
    grads = (probs * (dot_nt(v_ref[0], mg) - row_terms)).astype(BF)
    dk_acc[...] += dot(grads, q[:, :size])
    dqt_ref[0] = dot(kt_ref[0], grads).astype(BF)

    @pl.when(step == pl.num_programs(1) - 1)
    def _():
        dk_ref[0] = dk_acc[...].astype(BF)
        dv_ref[0] = dv_acc[...].astype(BF)


def attend_back(q, k, v, kt, mg, o, lse, rows):
    heads, length, wide = q.shape
    size = v.shape[2]
    whole = lambda h, i: (h, 0, 0)
    part = lambda h, i: (h, i, 0)
    lane = lambda h, i: (h, 0, i)
    return pl.pallas_call(
        attend_back_kernel,
        grid=(heads, length // rows),
        in_specs=[
            pl.BlockSpec((1, rows, wide), part),
            pl.BlockSpec((1, length, wide), whole),
            pl.BlockSpec((1, length, size), whole),
            pl.BlockSpec((1, size, length), whole),
            pl.BlockSpec((1, rows, size), part),
            pl.BlockSpec((1, rows, size), part),
            pl.BlockSpec((1, 1, rows), lane),
        ],
        out_specs=[
            pl.BlockSpec((1, size, rows), lane),
            pl.BlockSpec((1, length, size), whole),
            pl.BlockSpec((1, length, size), whole),
        ],
        out_shape=[
            jax.ShapeDtypeStruct((heads, size, length), BF),
            jax.ShapeDtypeStruct((heads, length, size), BF),
            jax.ShapeDtypeStruct((heads, length, size), BF),
        ],
        scratch_shapes=[pltpu.VMEM((length, size), F32), pltpu.VMEM((length, size), F32)],
        compiler_params=params(),
        name="attend_back",
    )(q, k, v, kt, mg, o, lse)


def normalize(source):
    mean = jnp.mean(source, axis=-1, keepdims=True)
    centered = source - mean
    root = lax.rsqrt(jnp.mean(centered * centered, axis=-1, keepdims=True) + 1e-05)
    return centered * root, root


def norm_back(normed, root, grad, gain):
    scaled = grad * gain
    mean = jnp.mean(scaled, axis=-1, keepdims=True)
    mix = jnp.mean(scaled * normed, axis=-1, keepdims=True)
    return root * (scaled - mean - normed * mix)


def first_norm_kernel(count, offs_ref, x_ref, wo_ref, vec_ref, *refs):
    blocks, (hidden_ref, low_ref, normed_ref, root_ref) = refs[:count], refs[count:]
    wide = blocks[0].shape[1]
    out = x_ref[...].astype(F32) + vec_ref[0:1, :]
    for r, block in enumerate(blocks):
        out = out + dot(block[...], wo_ref[pl.ds(pl.multiple_of(offs_ref[r], wide), wide), :])
    normed, root = normalize(out)
    hidden = normed * vec_ref[1:2, :] + vec_ref[2:3, :]
    hidden_ref[...] = hidden
    low_ref[...] = hidden.astype(BF)
    normed_ref[...] = normed
    root_ref[...] = root


def first_norm(offs, x, wo, vec, blocks):
    rows, width = x.shape
    vm = pl.BlockSpec(memory_space=pltpu.VMEM)
    return pl.pallas_call(
        functools.partial(first_norm_kernel, len(blocks)),
        in_specs=[pl.BlockSpec(memory_space=pltpu.SMEM)] + [vm] * (3 + len(blocks)),
        out_specs=[vm] * 4,
        out_shape=[
            jax.ShapeDtypeStruct((rows, width), F32),
            jax.ShapeDtypeStruct((rows, width), BF),
            jax.ShapeDtypeStruct((rows, width), F32),
            jax.ShapeDtypeStruct((rows, 1), F32),
        ],
        compiler_params=params(),
        name="first_norm",
    )(offs, x, wo, vec, *blocks)


def second_norm_kernel(hidden_ref, branch_ref, vec_ref, cot_ref, res_ref, resid_ref, bgrad_ref, sums_ref):
    normed, root = normalize(hidden_ref[...] + branch_ref[...].astype(F32) + vec_ref[0:1, :])
    gain = vec_ref[1:2, :]
    res_ref[...] = (normed * gain + vec_ref[2:3, :]).astype(BF)
    grad = cot_ref[...].astype(F32)
    resid = norm_back(normed, root, grad, gain)
    resid_ref[...] = resid
    low = resid.astype(BF)
    bgrad_ref[...] = low
    sums_ref[0:1, :] = jnp.sum(grad * normed, axis=0, keepdims=True)
    sums_ref[1:2, :] = jnp.sum(grad, axis=0, keepdims=True)
    sums_ref[2:3, :] = jnp.sum(low.astype(F32), axis=0, keepdims=True)
    sums_ref[3:8, :] = jnp.zeros((5, sums_ref.shape[1]), F32)


def second_norm(hidden, branch, vec, cot):
    rows, width = hidden.shape
    vm = pl.BlockSpec(memory_space=pltpu.VMEM)
    return pl.pallas_call(
        second_norm_kernel,
        in_specs=[vm] * 4,
        out_specs=[vm] * 4,
        out_shape=[
            jax.ShapeDtypeStruct((rows, width), BF),
            jax.ShapeDtypeStruct((rows, width), F32),
            jax.ShapeDtypeStruct((rows, width), BF),
            jax.ShapeDtypeStruct((8, width), F32),
        ],
        compiler_params=params(),
        name="second_norm",
    )(hidden, branch, vec, cot)


def first_back_kernel(count, offs_ref, resid_ref, more_ref, normed_ref, root_ref, vec_ref, wo_ref, *refs):
    blocks = refs[:count]
    first_ref, wog_ref, sums_ref = refs[count : count + 3]
    outs = refs[count + 3 :]
    wide = blocks[0].shape[1]
    grad = resid_ref[...] + more_ref[...].astype(F32)
    normed = normed_ref[...]
    first = norm_back(normed, root_ref[...], grad, vec_ref[1:2, :])
    first_ref[...] = first
    low = first.astype(BF)
    sums_ref[0:1, :] = jnp.sum(grad * normed, axis=0, keepdims=True)
    sums_ref[1:2, :] = jnp.sum(grad, axis=0, keepdims=True)
    sums_ref[2:3, :] = jnp.sum(low.astype(F32), axis=0, keepdims=True)
    sums_ref[3:8, :] = jnp.zeros((5, sums_ref.shape[1]), F32)
    for r in range(count):
        rows = pl.ds(pl.multiple_of(offs_ref[r], wide), wide)
        outs[r][...] = dot_nt(low, wo_ref[rows, :]).astype(BF)
        wog_ref[rows, :] = dot_tn(blocks[r][...], low).astype(BF)


def first_back(offs, resid, more, normed, root, vec, wo, blocks):
    rows, width = resid.shape
    wide = blocks[0].shape[1]
    vm = pl.BlockSpec(memory_space=pltpu.VMEM)
    return pl.pallas_call(
        functools.partial(first_back_kernel, len(blocks)),
        in_specs=[pl.BlockSpec(memory_space=pltpu.SMEM)] + [vm] * (6 + len(blocks)),
        out_specs=[vm] * (3 + len(blocks)),
        out_shape=[
            jax.ShapeDtypeStruct((rows, width), F32),
            jax.ShapeDtypeStruct((width, width), BF),
            jax.ShapeDtypeStruct((8, width), F32),
        ]
        + [jax.ShapeDtypeStruct((rows, wide), BF)] * len(blocks),
        compiler_params=params(),
        name="first_back",
    )(offs, resid, more, normed, root, vec, wo, *blocks)


def flip(source, bit):
    return lax.ppermute(source, "ctx", [(i, i ^ bit) for i in range(8)])


class Cube:
    def __init__(self):
        self.count = 8

    def at(self, r):
        return lax.axis_index("ctx") ^ r

    def gather(self, own):
        half = own.shape[0] // 2
        side = flip(own, 2)
        down = flip(own, 4)
        core = flip(own, 1)
        far = jnp.concatenate([flip(side[:half], 4), flip(down[half:], 2)], axis=0)
        return [own, core, side, flip(side, 1), down, flip(down, 1), far, flip(far, 1)]

    def scatter(self, blocks):
        half = blocks[0].shape[0] // 2
        low = [b.astype(BF) for b in blocks]
        far = blocks[6].astype(F32) + flip(low[7], 1).astype(F32)
        far = far.astype(BF)
        over_side = flip(far[:half], 2)
        over_down = flip(far[half:], 4)
        side = blocks[2].astype(F32) + flip(low[3], 1).astype(F32)
        down = blocks[4].astype(F32) + flip(low[5], 1).astype(F32)
        side_a = flip(side[:half].astype(BF), 2)
        down_b = flip(down[half:].astype(BF), 4)
        side_b = flip((side[half:] + over_down.astype(F32)).astype(BF), 2)
        down_a = flip((down[:half] + over_side.astype(F32)).astype(BF), 4)
        own = blocks[0].astype(F32) + flip(low[1], 1).astype(F32)
        return (
            own
            + jnp.concatenate([side_a, side_b], axis=0).astype(F32)
            + jnp.concatenate([down_a, down_b], axis=0).astype(F32)
        )

    def exchange(self, blocks):
        return [blocks[0]] + [flip(blocks[r], r) for r in range(1, 8)]


class Line:
    def __init__(self, count):
        self.count = count

    def at(self, r):
        return jnp.int32(r)

    def gather(self, own):
        return list(lax.all_gather(own, "ctx", axis=0, tiled=False))

    def scatter(self, blocks):
        whole = jnp.concatenate([b.astype(BF) for b in blocks], axis=0)
        return lax.psum_scatter(whole, "ctx", scatter_dimension=0, tiled=True).astype(F32)

    def exchange(self, blocks):
        return list(lax.all_to_all(jnp.stack(blocks), "ctx", 0, 0, tiled=False))


def gelu_pair(source):
    bell = 0.5 * (1.0 + lax.erf(source * (0.5**0.5)))
    slope = bell + source * jnp.exp(-0.5 * source * source) * ((2.0 * jnp.pi) ** -0.5)
    return source * bell, slope


def local(
    tokens, starts, query_weight, key_weight, value_weight, output_weight, inner_weight, outer_weight,
    query_bias, value_bias, output_bias, first_gain, first_shift, inner_bias, outer_bias,
    second_gain, second_shift, cotangent,
):
    count, shards = lax.axis_size("ctx"), lax.axis_size("wsh")
    net = Cube() if count == 8 else Line(count)
    me, shard = lax.axis_index("ctx"), lax.axis_index("wsh")
    x = tokens[0]
    rows, width = x.shape
    length = rows * count
    size = width // HEADS
    heads = max(1, HEADS // count)
    copies = max(1, count // HEADS)
    cols = heads * size
    depth = width // shards
    units = outer_weight.shape[0] // count
    strip = depth // count
    scale = size**-0.5

    first_col = me // copies * cols
    qkv_own = jnp.concatenate(
        [lax.dynamic_slice_in_dim(w, first_col, cols, 1) for w in (query_weight, key_weight, value_weight)],
        axis=1,
    )
    small_own = jnp.concatenate(
        [query_bias, value_bias, output_bias, first_gain, first_shift, outer_bias, second_gain,
         second_shift, inner_bias]
    )
    small = lax.all_gather(small_own, "wsh", axis=0, tiled=False).astype(F32)
    qkv = lax.all_gather(qkv_own, "wsh", axis=0, tiled=True)
    wo_own = lax.dynamic_slice_in_dim(output_weight, me * strip, strip, 0)
    wo_part = lax.all_gather(wo_own, "wsh", axis=0, tiled=False)
    inner_own = lax.dynamic_slice_in_dim(inner_weight.reshape(depth, shards, -1), me * units, units, 2)
    inner = lax.all_gather(inner_own.reshape(depth, shards * units), "wsh", axis=0, tiled=True)
    outer_own = lax.dynamic_slice_in_dim(outer_weight, me * units, units, 0)
    outer = lax.all_gather(outer_own, "wsh", axis=0, tiled=True)
    wo = lax.all_gather(wo_part, "ctx", axis=0, tiled=False)
    wo = wo.transpose(1, 0, 2, 3).reshape(width, width)

    def vector(i):
        return small[:, i * depth : (i + 1) * depth].reshape(1, width)

    query_b = lax.dynamic_slice_in_dim(vector(0), first_col, cols, 1)
    value_b = lax.dynamic_slice_in_dim(vector(1), first_col, cols, 1)
    pad = jnp.zeros((5, width), F32)
    first_vec = jnp.concatenate([vector(2), vector(3), vector(4), pad], axis=0)
    second_vec = jnp.concatenate([vector(5), vector(6), vector(7), pad], axis=0)
    inner_b = lax.dynamic_slice_in_dim(small[:, 8 * depth :], me * units, units, 1).reshape(1, -1)

    stream = jnp.concatenate(net.gather(x), axis=0)
    place = jnp.concatenate([net.at(r) * rows + jnp.arange(rows, dtype=jnp.int32) for r in range(count)])
    segment = jnp.sum((starts[0][None, :] <= place[:, None]).astype(jnp.int32), axis=1) - 1
    same = segment[:, None] == jnp.arange(starts.shape[1], dtype=jnp.int32)[None, :]
    fill = jnp.zeros((length, LANES - size - starts.shape[1]), BF)
    query_tail = jnp.concatenate([jnp.where(same, 0.0, -1e30).astype(BF), fill], axis=1)
    key_tail = jnp.concatenate([same.astype(BF), fill], axis=1)
    raw = dot(stream, qkv)
    queries = ((raw[:, :cols] + query_b) * scale).astype(BF)
    keys = raw[:, cols : 2 * cols].astype(BF)
    values = (raw[:, 2 * cols :] + value_b).astype(BF)

    def head(source, h):
        return source[:, h * size : (h + 1) * size]

    q_ext = jnp.stack([jnp.concatenate([head(queries, h), query_tail], axis=1) for h in range(heads)])
    k_ext = jnp.stack([jnp.concatenate([head(keys, h), key_tail], axis=1) for h in range(heads)])
    v_heads = jnp.stack([head(values, h) for h in range(heads)])
    mixed, lse = attend(q_ext, k_ext, v_heads, rows)
    mixed_low = jnp.concatenate([mixed[h] for h in range(heads)], axis=1).astype(BF)
    blocks = net.exchange([mixed_low[r * rows : (r + 1) * rows] for r in range(count)])[::copies]
    offs = jnp.stack([net.at(r) // copies * cols for r in range(0, count, copies)])
    hidden, hidden_low, normed, root = first_norm(offs, x, wo, first_vec, blocks)

    hidden_all = jnp.concatenate(net.gather(hidden_low), axis=0)
    act, slope = gelu_pair(dot(hidden_all, inner) + inner_b)
    act_low, slope = act.astype(BF), slope.astype(BF)
    branch = dot(act_low, outer).astype(BF)
    branch = net.scatter([branch[r * rows : (r + 1) * rows] for r in range(count)])
    result, resid, branch_grad, sums_two = second_norm(hidden, branch, second_vec, cotangent[0])

    grad_all = jnp.concatenate(net.gather(branch_grad), axis=0)
    inner_grad = (dot_nt(grad_all, outer) * slope.astype(F32)).astype(BF)
    hidden_grad = dot_nt(inner_grad, inner).astype(BF)
    hidden_grad = net.scatter([hidden_grad[r * rows : (r + 1) * rows] for r in range(count)])
    outer_wg = dot_tn(act_low, grad_all).astype(BF)
    inner_wg = dot_tn(hidden_all, inner_grad).astype(BF)
    inner_bg = jnp.sum(inner_grad.astype(F32), axis=0)

    first, wo_grad, sums_one, *mixed_grads = first_back(
        offs, resid, hidden_grad, normed, root, first_vec, wo, blocks
    )
    if copies > 1:
        mixed_grads = [b for b in mixed_grads for _ in range(copies)]
    mixed_grad = jnp.concatenate(net.exchange(mixed_grads), axis=0)
    mg_heads = jnp.stack([head(mixed_grad, h) for h in range(heads)])
    k_t = jnp.stack([head(keys, h).T for h in range(heads)])
    dqt, dk, dv = attend_back(q_ext, k_ext, v_heads, k_t, mg_heads, mixed, lse, rows)
    triple = jnp.concatenate(
        [dqt[h].T * BF(scale) for h in range(heads)]
        + [dk[h] for h in range(heads)]
        + [dv[h] for h in range(heads)],
        axis=1,
    )
    into = dot_nt(triple, qkv)
    if copies > 1:
        into = into * (1.0 / copies)
    into = into.astype(BF)
    into = net.scatter([into[r * rows : (r + 1) * rows] for r in range(count)])
    input_grad = (first + into).astype(BF)
    qkv_wg = dot_tn(stream, triple).astype(BF)
    qkv_bg = jnp.sum(triple.astype(F32), axis=0)

    def own_rows(source):
        return lax.psum_scatter(source, "wsh", scatter_dimension=0, tiled=True)

    def everywhere(source):
        return lax.all_gather(source, "ctx", axis=0, tiled=False).astype(F32)

    outer_out = everywhere(own_rows(outer_wg)).reshape(-1, width)
    inner_out = everywhere(own_rows(inner_wg)).reshape(count, depth, shards, units)
    inner_out = inner_out.transpose(1, 2, 0, 3).reshape(depth, -1)
    wo_grad = wo_grad.reshape(shards, count, strip, width).transpose(1, 0, 2, 3).reshape(width, width)
    wo_grad = lax.psum_scatter(wo_grad, "ctx", scatter_dimension=0, tiled=True)
    wo_out = everywhere(own_rows(wo_grad)).reshape(depth, width)
    qkv_out = everywhere(own_rows(qkv_wg))[::copies]
    qkv_out = qkv_out.reshape(-1, depth, 3, cols).transpose(2, 1, 0, 3).reshape(3, depth, width)

    zero = jnp.zeros((width,), F32)
    weight = 1.0 / copies
    vecs = jnp.concatenate(
        [
            lax.dynamic_update_slice(zero, qkv_bg[:cols] * weight, (first_col,)),
            lax.dynamic_update_slice(zero, qkv_bg[2 * cols :] * weight, (first_col,)),
            sums_one[2], sums_one[0], sums_one[1], sums_two[2], sums_two[0], sums_two[1],
            lax.dynamic_update_slice(
                jnp.zeros((shards, units * count), F32), inner_bg.reshape(shards, units),
                (jnp.int32(0), me * units),
            ).reshape(-1),
        ]
    )
    vecs = lax.psum(vecs, ("ctx", "wsh"))

    def piece(i):
        return lax.dynamic_slice_in_dim(vecs, i * width + shard * depth, depth, 0)

    inner_bias_out = lax.dynamic_slice_in_dim(vecs, 8 * width + shard * units * count, units * count, 0)
    return (
        result[None], input_grad[None], qkv_out[0], qkv_out[1], qkv_out[2], wo_out, inner_out, outer_out,
        piece(0), piece(1), piece(2), piece(3), piece(4), inner_bias_out, piece(5), piece(6), piece(7),
    )


def solution(mesh):
    sheet, matrix, vector = P("wsh", "ctx", None), P("wsh", None), P("wsh")
    return jax.shard_map(
        local,
        mesh=mesh,
        in_specs=(sheet, matrix) + (matrix,) * 6 + (vector,) * 9 + (sheet,),
        out_specs=(sheet, sheet) + (matrix,) * 6 + (vector,) * 9,
        check_vma=False,
    )
```

time: 1410 us -> 545 us (0.39)
  waiting for transfers between devices: 950 us -> 134 us
  matrix products: 217 us -> 43.3 us
  starting transfers between devices: 0.85 us -> 63 us
  Pallas kernels: 0 us -> 61.8 us
  local copies, waits for them, and re-layouts: 74.8 us -> 99.9 us
  other arithmetic: 48.4 us -> 25.9 us
    reduce_scatter x7 -> x5, waiting for transfers between devices: 523 us -> 57.2 us  [the longest x4 57.2 us: own_rows(): return lax.psum_scatter(source, 'wsh', scatter_dimension=0, tiled=True)]
    all_gather x8 -> x6, waiting for transfers between devices: 356 us -> 6.93 us  [the longest x3 6.93 us: everywhere(): return lax.all_gather(source, 'ctx', axis=0, tiled=False).astype(F32)]
    dot_general x36 -> x9, matrix products: 217 us -> 43.3 us  [the longest x3 17.9 us: dot_tn(): lax.dot_general(a, b, (((0,), (0,)), ((), ())), preferred_element_type=F32)]
    ppermute x0 -> x68, waiting for transfers between devices: none -> 69.4 us  [flip(): return lax.ppermute(source, 'ctx', [(i, i ^ bit) for i in range(8)])]
    psum x1 -> x0, waiting for transfers between devices: 66.8 us -> none  [local(): lax.psum(owner_parts[0].astype(jnp.bfloat16), 'ctx').astype(jnp.float32)]
    ppermute x0 -> x68, starting transfers between devices: none -> 62.3 us  [flip(): return lax.ppermute(source, 'ctx', [(i, i ^ bit) for i in range(8)])]
    pallas_call x0 -> x5, Pallas kernels: none -> 61.8 us  [the longest x1 27.1 us: attend_back(): pl.pallas_call(attend_back_kernel, grid=(heads, length // rows), in_specs...]
    psum x1, blocking collectives: 15.7 us -> 43.2 us  [local(): vecs = lax.psum(vecs, ('ctx', 'wsh'))]
  transfers between devices with their start and end apart: 16 -> 79, of which waited for: 14 -> 30; matrix products, arithmetic and copies ran while one was open for 12% -> 27% of each run, Pallas kernels for 0% -> 10%
where the time goes in v1:
time: 545 us; the launch traced here: 538 us
  waiting for transfers between devices  134 us (25%)
  local copies, waits for them, and re-layouts  99.9 us (18%)
  blocking collectives  94.7 us (17%)
  starting transfers between devices  63 us (12%)
  Pallas kernels  61.8 us (11%)
  matrix products  43.3 us (8%)
  other arithmetic  25.9 us (5%)
  between operations  15.4 us (3%)
    ppermute x68, waiting for transfers between devices, flip(): return lax.ppermute(source, 'ctx', [(i, i ^ bit) for i in range(8)])  69.4 us
    ppermute x68, starting transfers between devices, flip(): return lax.ppermute(source, 'ctx', [(i, i ^ bit) for i in range(8)])  62.3 us
    reduce_scatter x4, waiting for transfers between devices, own_rows(): return lax.psum_scatter(source, 'wsh', scatter_dimension=0, tiled=True)  57.2 us
    psum x1, blocking collectives, local(): vecs = lax.psum(vecs, ('ctx', 'wsh'))  43.2 us
    unnamed x142, local copies, waits for them, and re-layouts  42.8 us
    pallas_call x1, Pallas kernels, attend_back(): pl.pallas_call(attend_back_kernel, grid=(heads, length // rows), in_specs...  27.1 us
    pallas_call x1, Pallas kernels, attend(): pl.pallas_call(attend_kernel, grid=(heads, length // rows), in_specs=[pl....  19.6 us
    dot_general x3, matrix products, dot_tn(): lax.dot_general(a, b, (((0,), (0,)), ((), ())), preferred_element_type=F32)  17.9 us
  transfers between devices with their start and end apart: 79, of which 30 were waited for; matrix products, arithmetic and copies ran while one was open for 27% of the time, Pallas kernels for 10%

profile of v1, /device:TPU:9, one launch (start us, length us, event | category | flops | bytes accessed | tf_op | source)
XLA Modules:
  0.0 538.5 jit_solution(13252374572910975931)
XLA Ops:
  8.4 11.9 %all-gather = bf16[128,1024]{1,0:T(8,128)(2,1)} all-gather(bf16[32,1024]{1,0:T(8,128)(2,1)S(1)} %constant_dynamic-slice_fusion.8), channel_id=2, replica_groups=mesh['ctx'=8,'wsh'=4] {'wsh'}, dimensions={0}, use_global_device_ids=true | all-gather | bytes 327680 | tf_op jit(solution)/shard_map/all_gather | solution.py:347
  20.3 4.2 collective-permute-start
  27.0 4.5 reshape.128
  37.2 15.8 %all_gather.57 = bf16[1024,384]{1,0:T(8,128)(2,1)} all-gather(bf16[256,384]{1,0:T(8,128)(2,1)S(1)} %pad_maximum_fusion.10), channel_id=1, replica_groups=mesh['ctx'=8,'wsh'=4] {'wsh'}, dimensions={0}, use_global_device_ids=true | all-gather | bytes 983040 | tf_op jit(solution)/shard_map/all_gather | solution.py:345
  53.1 10.9 %all-gather.2 = bf16[12288]{0:T(1024)(128)(2,1)S(1)} all-gather(bf16[3072]{0:T(1024)(128)(2,1)S(1)} %constant_dynamic-update-slice_fusion.45), channel_id=4, replica_groups=mesh['ctx'=8,'wsh'=4] {'wsh'}, dimensions={0}, use_global_device_ids=true | all-gather | bytes 30720 | tf_op jit(solution)/shard_map/all_gather | solution.py:344
  64.8 6.0 %collective-permute-start.2 = (bf16[256,1024]{1,0:T(8,128)(2,1)}, bf16[256,1024]{1,0:T(8,128)(2,1)}, u32[]{:S(2)}, u32[]{:S(2)}) collective-permute-start(bf16[256,1024]{1,0:T(8,128)(2,1)} %collective-permute-done.1), channel_id=1, source_target_pairs={{0,4},{4,0},{8,12},{12,8},{16,20},{20,16},{24,28},{28,24},{1,5},{5... | collective-permute-start | bytes 1572872 | tf_op jit(solution)/shard_map/ppermute | solution.py:249
  88.3 5.2 fusion.41
  107.2 19.6 %attend.1 = (f32[2,2048,64]{2,1,0:T(8,128)}, f32[2,1,2048]{2,1,0:T(1,128)}) custom-call(bf16[2,2048,128]{2,1,0:T(8,128)(2,1)} %pad_maximum_fusion.q_ref, bf16[2,2048,128]{2,1,0:T(8,128)(2,1)} %copy.111.k_ref, bf16[2,2048,64]{2,1,0:T(8,128)(2,1)} %pad_maximum_fusion.2.v_ref), custom_call_target="tpu_custom_call" | custom-call | tf_op jit(solution)/shard_map/attend/pallas_call | solution.py:49
  137.6 3.2 copy.104
  141.5 4.9 first_norm.1
  149.5 10.9 %collective-permute-done.16 = bf16[256,1024]{1,0:T(8,128)(2,1)S(1)} collective-permute-done((bf16[256,1024]{1,0:T(8,128)(2,1)}, bf16[256,1024]{1,0:T(8,128)(2,1)S(1)}, u32[]{:S(2)}, u32[]{:S(2)}) %collective-permute-start.16) | collective-permute-done | bytes 524320 | tf_op jit(solution)/shard_map/ppermute | solution.py:249
  176.0 7.4 %multiply_convert_fusion.1 = (bf16[2048,512]{1,0:T(8,128)(2,1)S(1)}, f32[2048,512]{1,0:T(8,128)}) fusion(f32[512]{0:T(512)S(1)} %fusion.26, bf16[2048,1024]{1,0:T(8,128)(2,1)} %constant_dynamic-update-slice_fusion.10, bf16[1024,512]{1,0:T(8,128)(2,1)} %all-gather.14.cloned.1.call-done), kind=kOutput, calls=%fused_computation.9 | convolution fusion | flops 2153775104 | bytes 11536384 | tf_op jit(solution)/shard_map/dot_general | solution.py:18
  184.8 3.6 convolution_convert_fusion.2
  196.6 3.9 collective-permute-done.27
  201.9 4.1 collective-permute-done.25
  206.1 5.5 %collective-permute-done.28 = bf16[128,1024]{1,0:T(8,128)(2,1)S(1)} collective-permute-done((bf16[128,1024]{1,0:T(8,128)(2,1)S(1)}, bf16[128,1024]{1,0:T(8,128)(2,1)S(1)}, u32[]{:S(2)}, u32[]{:S(2)}) %collective-permute-start.28) | collective-permute-done | bytes 262176 | tf_op jit(solution)/shard_map/ppermute | solution.py:249
  213.1 3.8 second_norm.1
  220.1 9.3 %collective-permute-done.34 = bf16[256,1024]{1,0:T(8,128)(2,1)S(1)} collective-permute-done((bf16[256,1024]{1,0:T(8,128)(2,1)}, bf16[256,1024]{1,0:T(8,128)(2,1)S(1)}, u32[]{:S(2)}, u32[]{:S(2)}) %collective-permute-start.34) | collective-permute-done | bytes 524320 | tf_op jit(solution)/shard_map/ppermute | solution.py:249
  234.8 4.7 collective-permute-done.38
  243.2 4.5 convert_reduce_fusion
  247.8 2.4 convolution_convert_fusion.1
  258.6 3.5 collective-permute-done.45
  264.3 3.4 collective-permute-done.43
  267.7 5.6 %collective-permute-done.46 = bf16[128,1024]{1,0:T(8,128)(2,1)S(1)} collective-permute-done((bf16[128,1024]{1,0:T(8,128)(2,1)S(1)}, bf16[128,1024]{1,0:T(8,128)(2,1)S(1)}, u32[]{:S(2)}, u32[]{:S(2)}) %collective-permute-start.46) | collective-permute-done | bytes 262176 | tf_op jit(solution)/shard_map/ppermute | solution.py:249
  274.6 6.4 %first_back.1 = (f32[256,1024]{1,0:T(8,128)}, bf16[1024,1024]{1,0:T(8,128)(2,1)}, f32[8,1024]{1,0:T(8,128)}, bf16[256,128]{1,0:T(8,128)(2,1)}, bf16[256,128]{1,0...) custom-call(s32[8]{0:T(128)} %stack.80.offs_ref, ...), custom_call_target="tpu_custom_call" | custom-call | tf_op jit(solution)/shard_map/first_back/pallas_call | solution.py:233
  286.2 3.2 copy.119
  297.1 27.1 %attend_back.1 = (bf16[2,64,2048]{2,1,0:T(8,128)(2,1)}, bf16[2,2048,64]{2,1,0:T(8,128)(2,1)}, bf16[2,2048,64]{2,1,0:T(8,128)(2,1)}) custom-call(bf16[2,2048,128]{2,1,0:T(8,128)(2,1)} %pad_maximum_fusion.q_ref, bf16[2,2048,128]{2,1,0:T(8,128)(2,1)} %copy.111.k_ref, bf16[2,2048,64]{2,1,0:T(8,128)(2,1)} %pad_maximum_fusion.2.v_ref, ...), custom_call_target="tpu_custom_call" | custom-call | tf_op jit(solution)/shard_map/attend_back/pallas_call | solution.py:102
  326.0 2.1 slice_bitcast_fusion.8
  329.1 5.2 concatenate.106
  334.3 5.4 %convolution_convert_fusion.5 = bf16[1024,384]{1,0:T(8,128)(2,1)} fusion(bf16[2048,1024]{1,0:T(8,128)(2,1)} %constant_dynamic-update-slice_fusion, bf16[2048,384]{1,0:T(8,128)(2,1)S(1)} %concatenate.106), kind=kOutput, calls=%fused_computation.17 | convolution fusion | flops 1611005952 | bytes 6553600 | tf_op jit(solution)/shard_map/dot_general | solution.py:26
  339.8 6.2 %convolution_convert_fusion.4 = bf16[1024,512]{1,0:T(8,128)(2,1)} fusion(bf16[2048,1024]{1,0:T(8,128)(2,1)} %constant_dynamic-update-slice_fusion.10, bf16[2048,512]{1,0:T(8,128)(2,1)} %copy-done.36), kind=kOutput, calls=%fused_computation.16 | convolution fusion | flops 2148007936 | bytes 7340032 | tf_op jit(solution)/shard_map/dot_general | solution.py:26
  346.1 6.2 %convolution_convert_fusion.3 = bf16[512,1024]{1,0:T(8,128)(2,1)} fusion(bf16[2048,512]{1,0:T(8,128)(2,1)} %copy-done.37, bf16[2048,1024]{1,0:T(8,128)(2,1)} %copy-done.17), kind=kOutput, calls=%fused_computation.15 | convolution fusion | flops 2148007936 | bytes 7340032 | tf_op jit(solution)/shard_map/dot_general | solution.py:26
  353.1 7.8 %reduce-scatter.6.cloned.1.call-done = bf16[256,384]{1,0:T(8,128)(2,1)} async-done(((bf16[1024,384]{1,0:T(8,128)(2,1)}), bf16[256,384]{1,0:T(8,128)(2,1)}) %reduce-scatter.6.cloned.1.call-update) | async-done | bytes 196624 | tf_op jit(solution)/shard_map/reduce_scatter | solution.py:429
  361.0 29.3 %reduce-scatter.12.cloned.1.call-done = bf16[256,512]{1,0:T(8,128)(2,1)} async-done(((bf16[1024,512]{1,0:T(8,128)(2,1)}), bf16[256,512]{1,0:T(8,128)(2,1)}) %reduce-scatter.12.cloned.1.call-update) | async-done | bytes 262160 | tf_op jit(solution)/shard_map/reduce_scatter | solution.py:429
  392.2 2.4 convolution_convert_fusion
  398.9 20.1 %reduce-scatter.14.cloned.1.call-done = bf16[128,1024]{1,0:T(8,128)(2,1)} async-done(((bf16[512,1024]{1,0:T(8,128)(2,1)}), bf16[128,1024]{1,0:T(8,128)(2,1)}) %reduce-scatter.14.cloned.1.call-update) | async-done | bytes 262160 | tf_op jit(solution)/shard_map/reduce_scatter | solution.py:429
  419.6 2.5 convert_add_fusion
  426.7 2.9 collective-permute-done.62
  432.8 43.2 %psum.7 = f32[12288]{0:T(1024)S(1)} all-reduce(f32[12288]{0:T(1024)S(1)} %bitcast_dynamic-update-slice_fusion), channel_id=1, replica_groups=mesh['ctx'=8,'wsh'=4] {'ctx','wsh'}, use_global_device_ids=true, to_apply=%region_8.9 | all-reduce | flops 12288 | bytes 98304 | tf_op jit(solution)/shard_map/psum | solution.py:456
  477.4 2.5 fusion.9
  479.9 12.9 %all-gather.4 = bf16[256,1024]{1,0:T(8,128)(2,1)S(1)} all-gather(bf16[32,1024]{1,0:T(8,128)(2,1)} %reduce-scatter.10.cloned.1.call-done), channel_id=6, replica_groups=mesh['ctx'=8,'wsh'=4] {'ctx'}, dimensions={0}, use_global_device_ids=true | all-gather | bytes 589824 | tf_op jit(solution)/shard_map/all_gather | solution.py:432
  493.9 3.1 copy.115
  497.0 3.3 copy.135
  505.5 4.7 reshape.154
  510.3 4.6 copy.120
  514.9 5.8 %copy.141 = f32[32,8,32,128]{3,1,2,0:T(8,128)} copy(f32[32,8,32,128]{3,2,1,0:T(8,128)S(1)} %bitcast.158) | data formatting | bytes 8388608
  520.7 6.9 %all-gather.24.cloned.1.call-done = bf16[1024,1024]{1,0:T(8,128)(2,1)} async-done(((bf16[128,1024]{1,0:T(8,128)(2,1)}), bf16[1024,1024]{1,0:T(8,128)(2,1)}) %all-gather.24.cloned.1.call-update) | async-done | bytes 2097168 | tf_op jit(solution)/shard_map/all_gather | solution.py:432
  527.6 4.1 reshape.165
  (399 shorter events, 146.3 us)
Async XLA Ops:
  7.3 130.3 %all-gather.18.cloned.1.call-start = ((), (), s32[]{:S(2)}) async-start(), calls=%async_computation.12 | async-start | bytes 2359296 | tf_op jit(solution)/shard_map/all_gather | solution.py:352
  20.3 155.8 %all-gather.14.cloned.1.call-start = ((), (), s32[]{:S(2)}) async-start(), calls=%async_computation.5 | async-start | bytes 1310720 | tf_op jit(solution)/shard_map/all_gather | solution.py:349
  20.3 55.0 %collective-permute-start = (bf16[256,1024]{1,0:T(8,128)(2,1)}, bf16[256,1024]{1,0:T(8,128)(2,1)}, u32[]{:S(2)}, u32[]{:S(2)}) collective-permute-start(bf16[256,1024]{1,0:T(8,128)(2,1)} %bitcast.168), channel_id=1, source_target_pairs={{0,4},{4,0},{8,12},{12,8},{16,20},{20,16},{24,28},{28,24},{1,5},{5... | collective-permute-start | bytes 1572872 | tf_op jit(solution)/shard_map/ppermute | solution.py:249
  24.5 40.3 %collective-permute-start.1 = (bf16[256,1024]{1,0:T(8,128)(2,1)}, bf16[256,1024]{1,0:T(8,128)(2,1)}, u32[]{:S(2)}, u32[]{:S(2)}) collective-permute-start(bf16[256,1024]{1,0:T(8,128)(2,1)} %bitcast.169), channel_id=1, source_target_pairs={{0,8},{4,12},{8,0},{12,4},{16,24},{20,28},{24,16},{28,20},{1,9},{5... | collective-permute-start | bytes 1572872 | tf_op jit(solution)/shard_map/ppermute | solution.py:249
  25.7 47.0 %collective-permute-start.3 = (bf16[256,1024]{1,0:T(8,128)(2,1)}, bf16[256,1024]{1,0:T(8,128)(2,1)S(1)}, u32[]{:S(2)}, u32[]{:S(2)}) collective-permute-start(bf16[256,1024]{1,0:T(8,128)(2,1)} %bitcast.170), channel_id=1, source_target_pairs={{0,16},{4,20},{8,24},{12,28},{16,0},{20,4},{24,8},{28,12},{1,17},{... | collective-permute-start | bytes 1572872 | tf_op jit(solution)/shard_map/ppermute | solution.py:249
  33.3 150.2 %all-gather.16.cloned.1.call-start = ((), (), s32[]{:S(2)}) async-start(), calls=%async_computation.6 | async-start | bytes 1310720 | tf_op jit(solution)/shard_map/all_gather | solution.py:351
  64.8 17.6 %collective-permute-start.2 = (bf16[256,1024]{1,0:T(8,128)(2,1)}, bf16[256,1024]{1,0:T(8,128)(2,1)}, u32[]{:S(2)}, u32[]{:S(2)}) collective-permute-start(bf16[256,1024]{1,0:T(8,128)(2,1)} %collective-permute-done.1), channel_id=1, source_target_pairs={{0,4},{4,0},{8,12},{12,8},{16,20},{20,16},{24,28},{28,24},{1,5},{5... | collective-permute-start | bytes 1572872 | tf_op jit(solution)/shard_map/ppermute | solution.py:249
  72.4 8.1 %collective-permute-start.5 = (bf16[128,1024]{1,0:T(8,128)(2,1)S(1)}, bf16[128,1024]{1,0:T(8,128)(2,1)S(1)}, u32[]{:S(2)}, u32[]{:S(2)}) collective-permute-start(bf16[128,1024]{1,0:T(8,128)(2,1)S(1)} %slice.396), channel_id=1, source_target_pairs={{0,16},{4,20},{8,24},{12,28},{16,0},{20,4},{24,8},{28,12},{1,17},{... | collective-permute-start | bytes 786440 | tf_op jit(solution)/shard_map/ppermute | solution.py:249
  74.8 10.4 %collective-permute-start.4 = (bf16[256,1024]{1,0:T(8,128)(2,1)S(1)}, bf16[256,1024]{1,0:T(8,128)(2,1)S(1)}, u32[]{:S(2)}, u32[]{:S(2)}) collective-permute-start(bf16[256,1024]{1,0:T(8,128)(2,1)S(1)} %collective-permute-done.3), channel_id=1, source_target_pairs={{0,4},{4,0},{8,12},{12,8},{16,20},{20,16},{24,28},{28,24},{1,5},{5... | collective-permute-start | bytes 1572872 | tf_op jit(solution)/shard_map/ppermute | solution.py:249
  130.0 10.8 %collective-permute-start.10 = (bf16[256,128]{1,0:T(8,128)(2,1)S(1)}, bf16[256,128]{1,0:T(8,128)(2,1)S(1)}, u32[]{:S(2)}, u32[]{:S(2)}) collective-permute-start(bf16[256,128]{1,0:T(8,128)(2,1)S(1)} %get-tuple-element.156), channel_id=1, source_target_pairs={{0,12},{4,8},{8,4},{12,0},{16,28},{20,24},{24,20},{28,16},{1,13},{... | collective-permute-start | bytes 196616 | tf_op jit(solution)/shard_map/ppermute | solution.py:249
  131.9 8.9 %collective-permute-start.11 = (bf16[256,128]{1,0:T(8,128)(2,1)S(1)}, bf16[256,128]{1,0:T(8,128)(2,1)S(1)}, u32[]{:S(2)}, u32[]{:S(2)}) collective-permute-start(bf16[256,128]{1,0:T(8,128)(2,1)S(1)} %get-tuple-element.157), channel_id=1, source_target_pairs={{0,16},{4,20},{8,24},{12,28},{16,0},{20,4},{24,8},{28,12},{1,17},{... | collective-permute-start | bytes 196616 | tf_op jit(solution)/shard_map/ppermute | solution.py:249
  146.4 13.9 %collective-permute-start.16 = (bf16[256,1024]{1,0:T(8,128)(2,1)}, bf16[256,1024]{1,0:T(8,128)(2,1)S(1)}, u32[]{:S(2)}, u32[]{:S(2)}) collective-permute-start(bf16[256,1024]{1,0:T(8,128)(2,1)} %get-tuple-element.43), channel_id=1, source_target_pairs={{0,8},{4,12},{8,0},{12,4},{16,24},{20,28},{24,16},{28,20},{1,9},{5... | collective-permute-start | bytes 1572872 | tf_op jit(solution)/shard_map/ppermute | solution.py:249
  147.4 15.0 %collective-permute-start.18 = (bf16[256,1024]{1,0:T(8,128)(2,1)}, bf16[256,1024]{1,0:T(8,128)(2,1)S(1)}, u32[]{:S(2)}, u32[]{:S(2)}) collective-permute-start(bf16[256,1024]{1,0:T(8,128)(2,1)} %get-tuple-element.43), channel_id=1, source_target_pairs={{0,16},{4,20},{8,24},{12,28},{16,0},{20,4},{24,8},{28,12},{1,17},{... | collective-permute-start | bytes 1572872 | tf_op jit(solution)/shard_map/ppermute | solution.py:249
  147.9 17.2 %collective-permute-start.15 = (bf16[256,1024]{1,0:T(8,128)(2,1)}, bf16[256,1024]{1,0:T(8,128)(2,1)}, u32[]{:S(2)}, u32[]{:S(2)}) collective-permute-start(bf16[256,1024]{1,0:T(8,128)(2,1)} %get-tuple-element.43), channel_id=1, source_target_pairs={{0,4},{4,0},{8,12},{12,8},{16,20},{20,16},{24,28},{28,24},{1,5},{5... | collective-permute-start | bytes 1572872 | tf_op jit(solution)/shard_map/ppermute | solution.py:249
  149.2 203.2 %reduce-scatter.8.cloned.1.call-start = ((), (), s32[]{:S(2)}) async-start(), calls=%async_computation.8 | async-start | bytes 2359296 | tf_op jit(solution)/shard_map/reduce_scatter | solution.py:438
  160.4 10.9 %collective-permute-start.17 = (bf16[256,1024]{1,0:T(8,128)(2,1)S(1)}, bf16[256,1024]{1,0:T(8,128)(2,1)S(1)}, u32[]{:S(2)}, u32[]{:S(2)}) collective-permute-start(bf16[256,1024]{1,0:T(8,128)(2,1)S(1)} %collective-permute-done.16), channel_id=1, source_target_pairs={{0,4},{4,0},{8,12},{12,8},{16,20},{20,16},{24,28},{28,24},{1,5},{5... | collective-permute-start | bytes 1572872 | tf_op jit(solution)/shard_map/ppermute | solution.py:249
  161.0 8.1 %collective-permute-start.20 = (bf16[128,1024]{1,0:T(8,128)(2,1)S(1)}, bf16[128,1024]{1,0:T(8,128)(2,1)S(1)}, u32[]{:S(2)}, u32[]{:S(2)}) collective-permute-start(bf16[128,1024]{1,0:T(8,128)(2,1)S(1)} %slice.424), channel_id=1, source_target_pairs={{0,16},{4,20},{8,24},{12,28},{16,0},{20,4},{24,8},{28,12},{1,17},{... | collective-permute-start | bytes 786440 | tf_op jit(solution)/shard_map/ppermute | solution.py:249
  164.5 8.4 %collective-permute-start.19 = (bf16[256,1024]{1,0:T(8,128)(2,1)S(1)}, bf16[256,1024]{1,0:T(8,128)(2,1)S(1)}, u32[]{:S(2)}, u32[]{:S(2)}) collective-permute-start(bf16[256,1024]{1,0:T(8,128)(2,1)S(1)} %collective-permute-done.18), channel_id=1, source_target_pairs={{0,4},{4,0},{8,12},{12,8},{16,20},{20,16},{24,28},{28,24},{1,5},{5... | collective-permute-start | bytes 1572872 | tf_op jit(solution)/shard_map/ppermute | solution.py:249
  194.6 11.4 %collective-permute-start.25 = (bf16[128,1024]{1,0:T(8,128)(2,1)S(1)}, bf16[128,1024]{1,0:T(8,128)(2,1)S(1)}, u32[]{:S(2)}, u32[]{:S(2)}) collective-permute-start(bf16[128,1024]{1,0:T(8,128)(2,1)S(1)} %slice.592), channel_id=1, source_target_pairs={{0,8},{4,12},{8,0},{12,4},{16,24},{20,28},{24,16},{28,20},{1,9},{5... | collective-permute-start | bytes 786440 | tf_op jit(solution)/shard_map/ppermute | solution.py:249
  195.3 10.9 %collective-permute-start.32 = (bf16[128,1024]{1,0:T(8,128)(2,1)S(1)}, bf16[128,1024]{1,0:T(8,128)(2,1)S(1)}, u32[]{:S(2)}, u32[]{:S(2)}) collective-permute-start(bf16[128,1024]{1,0:T(8,128)(2,1)S(1)} %slice.591), channel_id=1, source_target_pairs={{0,16},{4,20},{8,24},{12,28},{16,0},{20,4},{24,8},{28,12},{1,17},{... | collective-permute-start | bytes 786440 | tf_op jit(solution)/shard_map/ppermute | solution.py:249
  200.6 11.0 %collective-permute-start.28 = (bf16[128,1024]{1,0:T(8,128)(2,1)S(1)}, bf16[128,1024]{1,0:T(8,128)(2,1)S(1)}, u32[]{:S(2)}, u32[]{:S(2)}) collective-permute-start(bf16[128,1024]{1,0:T(8,128)(2,1)S(1)} %fusion.17), channel_id=1, source_target_pairs={{0,8},{4,12},{8,0},{12,4},{16,24},{20,28},{24,16},{28,20},{1,9},{5... | collective-permute-start | bytes 786440 | tf_op jit(solution)/shard_map/ppermute | solution.py:249
  201.0 10.8 %collective-permute-start.31 = (bf16[128,1024]{1,0:T(8,128)(2,1)S(1)}, bf16[128,1024]{1,0:T(8,128)(2,1)S(1)}, u32[]{:S(2)}, u32[]{:S(2)}) collective-permute-start(bf16[128,1024]{1,0:T(8,128)(2,1)S(1)} %fusion.16), channel_id=1, source_target_pairs={{0,16},{4,20},{8,24},{12,28},{16,0},{20,4},{24,8},{28,12},{1,17},{... | collective-permute-start | bytes 786440 | tf_op jit(solution)/shard_map/ppermute | solution.py:249
  216.9 12.5 %collective-permute-start.34 = (bf16[256,1024]{1,0:T(8,128)(2,1)}, bf16[256,1024]{1,0:T(8,128)(2,1)S(1)}, u32[]{:S(2)}, u32[]{:S(2)}) collective-permute-start(bf16[256,1024]{1,0:T(8,128)(2,1)} %get-tuple-element.46), channel_id=1, source_target_pairs={{0,8},{4,12},{8,0},{12,4},{16,24},{20,28},{24,16},{28,20},{1,9},{5... | collective-permute-start | bytes 1572872 | tf_op jit(solution)/shard_map/ppermute | solution.py:249
  217.7 15.0 %collective-permute-start.36 = (bf16[256,1024]{1,0:T(8,128)(2,1)}, bf16[256,1024]{1,0:T(8,128)(2,1)S(1)}, u32[]{:S(2)}, u32[]{:S(2)}) collective-permute-start(bf16[256,1024]{1,0:T(8,128)(2,1)} %get-tuple-element.46), channel_id=1, source_target_pairs={{0,16},{4,20},{8,24},{12,28},{16,0},{20,4},{24,8},{28,12},{1,17},{... | collective-permute-start | bytes 1572872 | tf_op jit(solution)/shard_map/ppermute | solution.py:249
  218.3 16.5 %collective-permute-start.33 = (bf16[256,1024]{1,0:T(8,128)(2,1)}, bf16[256,1024]{1,0:T(8,128)(2,1)S(1)}, u32[]{:S(2)}, u32[]{:S(2)}) collective-permute-start(bf16[256,1024]{1,0:T(8,128)(2,1)} %get-tuple-element.46), channel_id=1, source_target_pairs={{0,4},{4,0},{8,12},{12,8},{16,20},{20,16},{24,28},{28,24},{1,5},{5... | collective-permute-start | bytes 1572872 | tf_op jit(solution)/shard_map/ppermute | solution.py:249
  229.4 12.2 %collective-permute-start.35 = (bf16[256,1024]{1,0:T(8,128)(2,1)S(1)}, bf16[256,1024]{1,0:T(8,128)(2,1)S(1)}, u32[]{:S(2)}, u32[]{:S(2)}) collective-permute-start(bf16[256,1024]{1,0:T(8,128)(2,1)S(1)} %collective-permute-done.34), channel_id=1, source_target_pairs={{0,4},{4,0},{8,12},{12,8},{16,20},{20,16},{24,28},{28,24},{1,5},{5... | collective-permute-start | bytes 1572872 | tf_op jit(solution)/shard_map/ppermute | solution.py:249
  255.7 8.6 %collective-permute-start.41 = (bf16[256,1024]{1,0:T(8,128)(2,1)S(1)}, bf16[256,1024]{1,0:T(8,128)(2,1)S(1)}, u32[]{:S(2)}, u32[]{:S(2)}) collective-permute-start(bf16[256,1024]{1,0:T(8,128)(2,1)S(1)} %get-tuple-element.129), channel_id=1, source_target_pairs={{0,4},{4,0},{8,12},{12,8},{16,20},{20,16},{24,28},{28,24},{1,5},{5... | collective-permute-start | bytes 1572872 | tf_op jit(solution)/shard_map/ppermute | solution.py:249
  256.7 11.0 %collective-permute-start.43 = (bf16[128,1024]{1,0:T(8,128)(2,1)S(1)}, bf16[128,1024]{1,0:T(8,128)(2,1)S(1)}, u32[]{:S(2)}, u32[]{:S(2)}) collective-permute-start(bf16[128,1024]{1,0:T(8,128)(2,1)S(1)} %slice.590), channel_id=1, source_target_pairs={{0,8},{4,12},{8,0},{12,4},{16,24},{20,28},{24,16},{28,20},{1,9},{5... | collective-permute-start | bytes 786440 | tf_op jit(solution)/shard_map/ppermute | solution.py:249
  257.4 10.3 %collective-permute-start.50 = (bf16[128,1024]{1,0:T(8,128)(2,1)S(1)}, bf16[128,1024]{1,0:T(8,128)(2,1)S(1)}, u32[]{:S(2)}, u32[]{:S(2)}) collective-permute-start(bf16[128,1024]{1,0:T(8,128)(2,1)S(1)} %slice.589), channel_id=1, source_target_pairs={{0,16},{4,20},{8,24},{12,28},{16,0},{20,4},{24,8},{28,12},{1,17},{... | collective-permute-start | bytes 786440 | tf_op jit(solution)/shard_map/ppermute | solution.py:249
  262.1 11.1 %collective-permute-start.46 = (bf16[128,1024]{1,0:T(8,128)(2,1)S(1)}, bf16[128,1024]{1,0:T(8,128)(2,1)S(1)}, u32[]{:S(2)}, u32[]{:S(2)}) collective-permute-start(bf16[128,1024]{1,0:T(8,128)(2,1)S(1)} %fusion.15), channel_id=1, source_target_pairs={{0,8},{4,12},{8,0},{12,4},{16,24},{20,28},{24,16},{28,20},{1,9},{5... | collective-permute-start | bytes 786440 | tf_op jit(solution)/shard_map/ppermute | solution.py:249
  262.5 10.8 %collective-permute-start.49 = (bf16[128,1024]{1,0:T(8,128)(2,1)S(1)}, bf16[128,1024]{1,0:T(8,128)(2,1)S(1)}, u32[]{:S(2)}, u32[]{:S(2)}) collective-permute-start(bf16[128,1024]{1,0:T(8,128)(2,1)S(1)} %fusion.14), channel_id=1, source_target_pairs={{0,16},{4,20},{8,24},{12,28},{16,0},{20,4},{24,8},{28,12},{1,17},{... | collective-permute-start | bytes 786440 | tf_op jit(solution)/shard_map/ppermute | solution.py:249
  281.1 8.4 %collective-permute-start.51 = (bf16[256,128]{1,0:T(8,128)(2,1)}, bf16[256,128]{1,0:T(8,128)(2,1)S(1)}, u32[]{:S(2)}, u32[]{:S(2)}) collective-permute-start(bf16[256,128]{1,0:T(8,128)(2,1)} %get-tuple-element.51), channel_id=1, source_target_pairs={{0,4},{4,0},{8,12},{12,8},{16,20},{20,16},{24,28},{28,24},{1,5},{5... | collective-permute-start | bytes 196616 | tf_op jit(solution)/shard_map/ppermute | solution.py:249
  283.5 8.7 %collective-permute-start.53 = (bf16[256,128]{1,0:T(8,128)(2,1)}, bf16[256,128]{1,0:T(8,128)(2,1)S(1)}, u32[]{:S(2)}, u32[]{:S(2)}) collective-permute-start(bf16[256,128]{1,0:T(8,128)(2,1)} %get-tuple-element.53), channel_id=1, source_target_pairs={{0,12},{4,8},{8,4},{12,0},{16,28},{20,24},{24,20},{28,16},{1,13},{... | collective-permute-start | bytes 196616 | tf_op jit(solution)/shard_map/ppermute | solution.py:249
  289.4 71.6 %reduce-scatter.6.cloned.1.call-start = ((), (), s32[]{:S(2)}) async-start(), calls=%async_computation.7 | async-start | bytes 983040 | tf_op jit(solution)/shard_map/reduce_scatter | solution.py:429
  339.8 50.6 %reduce-scatter.12.cloned.1.call-start = ((), (), s32[]{:S(2)}) async-start(), calls=%async_computation.10 | async-start | bytes 1310720 | tf_op jit(solution)/shard_map/reduce_scatter | solution.py:429
  346.0 73.0 %reduce-scatter.14.cloned.1.call-start = ((), (), s32[]{:S(2)}) async-start(), calls=%async_computation.11 | async-start | bytes 1310720 | tf_op jit(solution)/shard_map/reduce_scatter | solution.py:429
  352.4 127.5 %reduce-scatter.10.cloned.1.call-start = ((), (), s32[]{:S(2)}) async-start(), calls=%async_computation.9 | async-start | bytes 327680 | tf_op jit(solution)/shard_map/reduce_scatter | solution.py:429
  353.1 140.8 %all-gather.20.cloned.1.call-start = ((), (), s32[]{:S(2)}) async-start(), calls=%async_computation.13 | async-start | bytes 1769472 | tf_op jit(solution)/shard_map/all_gather | solution.py:432
  361.0 144.5 %all-gather.22.cloned.1.call-start = ((), (), s32[]{:S(2)}) async-start(), calls=%async_computation.14 | async-start | bytes 2359296 | tf_op jit(solution)/shard_map/all_gather | solution.py:432
  390.4 137.3 %all-gather.24.cloned.1.call-start = ((), (), s32[]{:S(2)}) async-start(), calls=%async_computation.15 | async-start | bytes 2359296 | tf_op jit(solution)/shard_map/all_gather | solution.py:432
  397.8 79.5 %collective-permute-start.58 = (bf16[256,1024]{1,0:T(8,128)(2,1)}, bf16[256,1024]{1,0:T(8,128)(2,1)}, u32[]{:S(2)}, u32[]{:S(2)}) collective-permute-start(bf16[256,1024]{1,0:T(8,128)(2,1)} %get-tuple-element.122), channel_id=1, source_target_pairs={{0,4},{4,0},{8,12},{12,8},{16,20},{20,16},{24,28},{28,24},{1,5},{5... | collective-permute-start | bytes 1572872 | tf_op jit(solution)/shard_map/ppermute | solution.py:249
  398.4 21.2 %collective-permute-start.64 = (bf16[256,1024]{1,0:T(8,128)(2,1)}, bf16[256,1024]{1,0:T(8,128)(2,1)}, u32[]{:S(2)}, u32[]{:S(2)}) collective-permute-start(bf16[256,1024]{1,0:T(8,128)(2,1)} %get-tuple-element.119), channel_id=1, source_target_pairs={{0,4},{4,0},{8,12},{12,8},{16,20},{20,16},{24,28},{28,24},{1,5},{5... | collective-permute-start | bytes 1572872 | tf_op jit(solution)/shard_map/ppermute | solution.py:249
  398.4 21.2 %collective-permute-start.61 = (bf16[256,1024]{1,0:T(8,128)(2,1)}, bf16[256,1024]{1,0:T(8,128)(2,1)}, u32[]{:S(2)}, u32[]{:S(2)}) collective-permute-start(bf16[256,1024]{1,0:T(8,128)(2,1)} %get-tuple-element.120), channel_id=1, source_target_pairs={{0,4},{4,0},{8,12},{12,8},{16,20},{20,16},{24,28},{28,24},{1,5},{5... | collective-permute-start | bytes 1572872 | tf_op jit(solution)/shard_map/ppermute | solution.py:249
  398.9 20.7 %collective-permute-start.59 = (bf16[256,1024]{1,0:T(8,128)(2,1)S(1)}, bf16[256,1024]{1,0:T(8,128)(2,1)}, u32[]{:S(2)}, u32[]{:S(2)}) collective-permute-start(bf16[256,1024]{1,0:T(8,128)(2,1)S(1)} %get-tuple-element.121), channel_id=1, source_target_pairs={{0,4},{4,0},{8,12},{12,8},{16,20},{20,16},{24,28},{28,24},{1,5},{5... | collective-permute-start | bytes 1572872 | tf_op jit(solution)/shard_map/ppermute | solution.py:249
  425.4 51.9 %collective-permute-start.60 = (bf16[128,1024]{1,0:T(8,128)(2,1)}, bf16[128,1024]{1,0:T(8,128)(2,1)S(1)}, u32[]{:S(2)}, u32[]{:S(2)}) collective-permute-start(bf16[128,1024]{1,0:T(8,128)(2,1)} %slice.588), channel_id=1, source_target_pairs={{0,8},{4,12},{8,0},{12,4},{16,24},{20,28},{24,16},{28,20},{1,9},{5... | collective-permute-start | bytes 786440 | tf_op jit(solution)/shard_map/ppermute | solution.py:249
  426.5 50.9 %collective-permute-start.67 = (bf16[128,1024]{1,0:T(8,128)(2,1)}, bf16[128,1024]{1,0:T(8,128)(2,1)}, u32[]{:S(2)}, u32[]{:S(2)}) collective-permute-start(bf16[128,1024]{1,0:T(8,128)(2,1)} %slice.587), channel_id=1, source_target_pairs={{0,16},{4,20},{8,24},{12,28},{16,0},{20,4},{24,8},{28,12},{1,17},{... | collective-permute-start | bytes 786440 | tf_op jit(solution)/shard_map/ppermute | solution.py:249
  430.4 46.9 %collective-permute-start.63 = (bf16[128,1024]{1,0:T(8,128)(2,1)}, bf16[128,1024]{1,0:T(8,128)(2,1)S(1)}, u32[]{:S(2)}, u32[]{:S(2)}) collective-permute-start(bf16[128,1024]{1,0:T(8,128)(2,1)} %fusion.11), channel_id=1, source_target_pairs={{0,8},{4,12},{8,0},{12,4},{16,24},{20,28},{24,16},{28,20},{1,9},{5... | collective-permute-start | bytes 786440 | tf_op jit(solution)/shard_map/ppermute | solution.py:249
  431.6 45.7 %collective-permute-start.66 = (bf16[128,1024]{1,0:T(8,128)(2,1)S(1)}, bf16[128,1024]{1,0:T(8,128)(2,1)S(1)}, u32[]{:S(2)}, u32[]{:S(2)}) collective-permute-start(bf16[128,1024]{1,0:T(8,128)(2,1)S(1)} %fusion.10), channel_id=1, source_target_pairs={{0,16},{4,20},{8,24},{12,28},{16,0},{20,4},{24,8},{28,12},{1,17},{... | collective-permute-start | bytes 786440 | tf_op jit(solution)/shard_map/ppermute | solution.py:249
  (71 other events, 959.0 us)
Sparse Core Ops, SparseCore 0:
  20.4 35.7 all-gather.17
  57.7 27.2 all-gather.13
  149.3 27.1 all-gather.15
  289.5 40.8 reduce-scatter.7
  339.9 21.0 reduce-scatter.5
  363.8 26.5 reduce-scatter.11
  393.2 25.7 reduce-scatter.13
  421.4 16.1 reduce-scatter.9
  439.5 28.6 all-gather.19
  469.9 28.3 all-gather.21
  500.1 27.4 all-gather.23

commit v2 on v1

v2 whole, which is shorter than its diff:
```python
import functools
import math

import jax
import jax.numpy as jnp
from jax import lax
from jax.experimental import pallas as pl
from jax.experimental.pallas import tpu as pltpu
from jax.sharding import PartitionSpec as P

HEADS = 16
LANES = 128
EXTRA = 16
BF = jnp.bfloat16
F32 = jnp.float32
MIB = 1024 * 1024
IN_VMEM = pl.BlockSpec(memory_space=pltpu.VMEM)
IN_SMEM = pl.BlockSpec(memory_space=pltpu.SMEM)


def dot(a, b):
    return lax.dot_general(a, b, (((1,), (0,)), ((), ())), preferred_element_type=F32)


def dot_nt(a, b):
    return lax.dot_general(a, b, (((1,), (1,)), ((), ())), preferred_element_type=F32)


def dot_tn(a, b):
    return lax.dot_general(a, b, (((0,), (0,)), ((), ())), preferred_element_type=F32)


def struct(shape, dtype):
    return jax.ShapeDtypeStruct(shape, dtype)


def micros(us):
    return pl.CostEstimate(flops=int(us * 1e9), bytes_accessed=0, transcendentals=0)


def params(limit):
    return pltpu.CompilerParams(vmem_limit_bytes=min(limit, 60 * MIB))


def after(value, *others):
    return lax.optimization_barrier((value, others))[0]


def bytes_of(arrays):
    return sum(math.prod(a.shape) * a.dtype.itemsize for a in arrays)


def call(kernel, scalars, arrays, out_shape, us, name, scratch=(), room=6):
    limit = 60 * MIB if room is None else bytes_of(arrays) + bytes_of(out_shape) + bytes_of(scratch) + room * MIB
    return pl.pallas_call(
        kernel,
        in_specs=[IN_SMEM] * len(scalars) + [IN_VMEM] * len(arrays),
        out_specs=[IN_VMEM] * len(out_shape),
        out_shape=out_shape,
        scratch_shapes=list(scratch),
        compiler_params=params(limit),
        cost_estimate=micros(us),
        name=name,
    )(*scalars, *arrays)


def block_at(index, size):
    return pl.ds(pl.multiple_of(index * size, size), size)


def as_row(column):
    return jnp.broadcast_to(column, (column.shape[0], LANES)).T[0:1, :]


def add_up(parts):
    total = parts[0].astype(F32)
    for part in parts[1:]:
        total = total + part.astype(F32)
    return total


def pack_kernel(first_ref, q_ref, k_ref, v_ref, *refs):
    vectors, out_ref = refs[:-1], refs[-1]
    depth, wide = q_ref.shape[0], out_ref.shape[1] // 3
    lanes = pl.ds(pl.multiple_of(first_ref[0], LANES), wide)
    for i, ref in enumerate((q_ref, k_ref, v_ref)):
        out_ref[:depth, i * wide : (i + 1) * wide] = ref[:, lanes]
    rows = jnp.concatenate([ref[...].astype(F32) for ref in vectors], axis=0)
    per = 3 * wide // LANES
    height = out_ref.shape[0] - depth
    if rows.shape[0] < height * per:
        rows = jnp.concatenate([rows, jnp.zeros((height * per - rows.shape[0], LANES), F32)], axis=0)
    packed = [
        jnp.concatenate([rows[i * per + j : i * per + j + 1, :] for j in range(per)], axis=1) for i in range(height)
    ]
    out_ref[depth:, :] = jnp.concatenate(packed, axis=0).astype(BF)


def unpack_kernel(count, shard_ref, *refs):
    packs, (vec_ref, inner_ref) = refs[:count], refs[count:]
    depth = vec_ref.shape[1] // count
    vec_ref[...] = jnp.zeros_like(vec_ref)
    inner_ref[...] = jnp.zeros_like(inner_ref)
    for r, pack in enumerate(packs):
        at = shard_ref[r]
        wide = pack.shape[1] // LANES
        rows = pack[depth:, :].astype(F32)

        def piece(i):
            return rows[i // wide : i // wide + 1, i % wide * LANES : (i % wide + 1) * LANES]

        per = depth // LANES
        for i in range(8):
            for j in range(per):
                vec_ref[i : i + 1, block_at(at * per + j, LANES)] = piece(i * per + j)
        for j in range(inner_ref.shape[1] // LANES):
            inner_ref[block_at(at, 8), j * LANES : (j + 1) * LANES] = jnp.broadcast_to(piece(8 * per + j), (8, LANES))


def project_kernel(count, shards, cols, scale, shard_ref, place_ref, starts_ref, *refs):
    pieces, packs = refs[:count], refs[count : count + shards]
    bias_ref, w_ref, q_ref, k_ref, v_ref, qt_ref, kt_ref = refs[count + shards :]
    depth = w_ref.shape[0] // shards
    for r, pack in enumerate(packs):
        w_ref[block_at(shard_ref[r], depth), :] = pack[:depth, :]
    weight = w_ref[...]
    documents = starts_ref.shape[0]
    row = 0
    for p, piece in enumerate(pieces):
        rows = piece.shape[0]
        at = slice(row, row + rows)
        raw = dot(piece[...], weight)
        q_ref[at, :] = ((raw[:, :cols] + bias_ref[0:1, :]) * scale).astype(BF)
        k_ref[at, :] = raw[:, cols : 2 * cols].astype(BF)
        v_ref[at, :] = (raw[:, 2 * cols :] + bias_ref[1:2, :]).astype(BF)
        place = place_ref[p] + lax.broadcasted_iota(jnp.int32, (rows, LANES), 0)
        segment = jnp.full((rows, LANES), -1, jnp.int32)
        for j in range(documents):
            segment = segment + (starts_ref[j] <= place).astype(jnp.int32)
        lane = lax.broadcasted_iota(jnp.int32, (rows, LANES), 1)
        same = segment == lane
        qt_ref[at, :] = jnp.where(same | (lane >= documents), 0.0, -1e30).astype(BF)
        kt_ref[at, :] = jnp.where(same, 1.0, 0.0).astype(BF)
        row += rows


def head_lanes(rows, wide, h, size):
    lane = lax.broadcasted_iota(jnp.int32, (rows, wide), 1)
    return (lane >= h * size) & (lane < (h + 1) * size)


def attend_kernel(heads, size, q_ref, qt_ref, k_ref, kt_ref, v_ref, low_ref, o_ref, lse_ref):
    rows, wide = q_ref.shape
    keys = jnp.concatenate([k_ref[...], kt_ref[...]], axis=1)
    query, tail = q_ref[...], qt_ref[...]
    out = jnp.zeros((rows, wide), F32)
    for h in range(heads):
        mine = head_lanes(rows, wide, h, size)
        scores = dot_nt(jnp.concatenate([jnp.where(mine, query, jnp.zeros_like(query)), tail], axis=1), keys)
        top = jnp.max(scores, axis=1, keepdims=True)
        probs = jnp.exp(scores - top)
        total = jnp.sum(probs, axis=1, keepdims=True)
        out = jnp.where(mine, dot(probs.astype(BF), v_ref[...]) / total, out)
        lse_ref[h : h + 1, :] = as_row(top + jnp.log(total))
    o_ref[...] = out
    low_ref[...] = out.astype(BF)


def attend(q, qt, k, kt, v, rows, heads, size):
    length, wide = q.shape
    part = pl.BlockSpec((rows, wide), lambda i: (i, 0))
    whole = pl.BlockSpec((length, wide), lambda i: (0, 0))
    tail = pl.BlockSpec((length, LANES), lambda i: (0, 0))
    return pl.pallas_call(
        functools.partial(attend_kernel, heads, size),
        grid=(length // rows,),
        in_specs=[part, pl.BlockSpec((rows, LANES), lambda i: (i, 0)), whole, tail, whole],
        out_specs=[part, part, pl.BlockSpec((8, rows), lambda i: (0, i))],
        out_shape=[struct((length, wide), BF), struct((length, wide), F32), struct((8, length), F32)],
        compiler_params=params(8 * MIB + 20 * rows * length + 8 * bytes_of([q])),
        cost_estimate=micros(18),
        name="attend",
    )(q, qt, k, kt, v)


def attend_back_kernel(
    heads, size, scale, q_ref, qt_ref, k_ref, kt_ref, v_ref, mg_ref, o_ref, lse_ref, out_ref, kx, dk_acc, dv_acc
):
    step = pl.program_id(0)
    rows, wide = q_ref.shape

    @pl.when(step == 0)
    def _():
        dk_acc[...] = jnp.zeros_like(dk_acc)
        dv_acc[...] = jnp.zeros_like(dv_acc)
        kx[...] = k_ref[...].astype(F32).T.astype(BF)

    keys = jnp.concatenate([k_ref[...], kt_ref[...]], axis=1)
    query, tail, mg = q_ref[...], qt_ref[...], mg_ref[...]
    spread = mg.astype(F32) * o_ref[...]
    turned = []
    for h in range(heads):
        mine = head_lanes(rows, wide, h, size)
        query_h = jnp.where(mine, query, jnp.zeros_like(query))
        mg_h = jnp.where(mine, mg, jnp.zeros_like(mg))
        row_terms = as_row(jnp.sum(jnp.where(mine, spread, 0.0), axis=1, keepdims=True))
        scores = dot_nt(keys, jnp.concatenate([query_h, tail], axis=1))
        probs = jnp.exp(scores - lse_ref[h : h + 1, :])
        dv_acc[...] += dot(probs.astype(BF), mg_h)
        grads = (probs * (dot_nt(v_ref[...], mg_h) - row_terms)).astype(BF)
        dk_acc[...] += dot(grads, query_h)
        turned.append(dot(kx[h * size : (h + 1) * size, :], grads))
    if heads * size < wide:
        turned.append(jnp.zeros((wide - heads * size, rows), F32))
    at = block_at(step, rows)
    out_ref[at, :wide] = (jnp.concatenate(turned, axis=0).T * scale).astype(BF)

    @pl.when(step == pl.num_programs(0) - 1)
    def _():
        out_ref[:, wide : 2 * wide] = dk_acc[...].astype(BF)
        out_ref[:, 2 * wide :] = dv_acc[...].astype(BF)


def attend_back(q, qt, k, kt, v, mg, o, lse, rows, heads, size, scale):
    length, wide = q.shape
    part = pl.BlockSpec((rows, wide), lambda i: (i, 0))
    whole = pl.BlockSpec((length, wide), lambda i: (0, 0))
    tail = pl.BlockSpec((length, LANES), lambda i: (0, 0))
    return pl.pallas_call(
        functools.partial(attend_back_kernel, heads, size, scale),
        grid=(length // rows,),
        in_specs=[
            part, pl.BlockSpec((rows, LANES), lambda i: (i, 0)), whole, tail, whole, part, part,
            pl.BlockSpec((8, rows), lambda i: (0, i)),
        ],
        out_specs=pl.BlockSpec((length, 3 * wide), lambda i: (0, 0)),
        out_shape=struct((length, 3 * wide), BF),
        scratch_shapes=[
            pltpu.VMEM((wide, length), BF), pltpu.VMEM((length, wide), F32), pltpu.VMEM((length, wide), F32)
        ],
        compiler_params=params(60 * MIB),
        cost_estimate=micros(27),
        name="attend_back",
    )(q, qt, k, kt, v, mg, o, lse)


def normalize(source):
    mean = jnp.mean(source, axis=-1, keepdims=True)
    centered = source - mean
    root = lax.rsqrt(jnp.mean(centered * centered, axis=-1, keepdims=True) + 1e-05)
    return centered * root, root


def norm_back(normed, root, grad, gain):
    scaled = grad * gain
    mean = jnp.mean(scaled, axis=-1, keepdims=True)
    mix = jnp.mean(scaled * normed, axis=-1, keepdims=True)
    return root * (scaled - mean - normed * mix)


def column_sums(sums_ref, rows):
    sums_ref[...] = jnp.zeros_like(sums_ref)
    for i, row in enumerate(rows):
        sums_ref[i : i + 1, :] = jnp.sum(row, axis=0, keepdims=True)


def collected(refs, whole, halves):
    full = add_up([r[...] for r in refs[:whole]])
    if not halves:
        return full
    upper = add_up([r[...] for r in refs[whole : whole + halves]])
    lower = add_up([r[...] for r in refs[whole + halves : whole + 2 * halves]])
    return full + jnp.concatenate([upper, lower], axis=0)


def first_norm_kernel(count, offs_ref, x_ref, wo_ref, vec_ref, *refs):
    blocks, (hidden_ref, low_ref, normed_ref, root_ref) = refs[:count], refs[count:]
    wide = wo_ref.shape[0] // count
    out = x_ref[...].astype(F32) + vec_ref[2:3, :]
    for r, block in enumerate(blocks):
        out = out + dot(block[...], wo_ref[block_at(offs_ref[r], wide), :])
    normed, root = normalize(out)
    hidden = normed * vec_ref[3:4, :] + vec_ref[4:5, :]
    hidden_ref[...] = hidden
    low_ref[...] = hidden.astype(BF)
    normed_ref[...] = normed
    root_ref[...] = root


def second_norm_kernel(whole, halves, hidden_ref, vec_ref, cot_ref, *refs):
    parts, (res_ref, resid_ref, low_ref, sums_ref) = refs[:-4], refs[-4:]
    normed, root = normalize(hidden_ref[...] + collected(parts, whole, halves) + vec_ref[5:6, :])
    gain = vec_ref[6:7, :]
    res_ref[...] = (normed * gain + vec_ref[7:8, :]).astype(BF)
    grad = cot_ref[...].astype(F32)
    resid = norm_back(normed, root, grad, gain)
    resid_ref[...] = resid
    low = resid.astype(BF)
    low_ref[...] = low
    column_sums(sums_ref, [low.astype(F32), grad * normed, grad])


def first_back_kernel(count, whole, halves, offs_ref, resid_ref, normed_ref, root_ref, vec_ref, wo_ref, *refs):
    parts = refs[: whole + 2 * halves]
    first_ref, low_ref, sums_ref, *outs = refs[whole + 2 * halves :]
    wide = wo_ref.shape[0] // count
    grad = resid_ref[...] + collected(parts, whole, halves)
    normed = normed_ref[...]
    first = norm_back(normed, root_ref[...], grad, vec_ref[3:4, :])
    first_ref[...] = first
    low = first.astype(BF)
    low_ref[...] = low
    for r in range(count):
        outs[r][...] = dot_nt(low, wo_ref[block_at(offs_ref[r], wide), :]).astype(BF)
    column_sums(sums_ref, [low.astype(F32), grad * normed, grad])


def input_kernel(whole, halves, first_ref, *refs):
    parts, out_ref = refs[:-1], refs[-1]
    out_ref[...] = (first_ref[...] + collected(parts, whole, halves)).astype(BF)


def assemble_kernel(shards, strip, shard_ref, ids_ref, *refs):
    slabs, out_ref = refs[:-1], refs[-1]
    per = slabs[0].shape[0] // (shards * strip)
    depth = out_ref.shape[0] // shards
    for i, slab in enumerate(slabs):
        for b in range(per):
            for r in range(shards):
                row = pl.multiple_of(shard_ref[r] * depth + ids_ref[i * per + b] * strip, strip)
                out_ref[pl.ds(row, strip), :] = slab[(b * shards + r) * strip : (b * shards + r + 1) * strip, :]


def gelu_pair(source):
    bell = 0.5 * (1.0 + lax.erf(source * (0.5**0.5)))
    slope = bell + source * jnp.exp(-0.5 * source * source) * ((2.0 * jnp.pi) ** -0.5)
    return source * bell, slope


def forward_kernel(count, inner_ref, bias_ref, outer_ref, *refs):
    for p in range(count):
        act, slope = gelu_pair(dot(refs[p][...], inner_ref[...]) + bias_ref[...])
        low = act.astype(BF)
        refs[count + p][...] = low
        refs[2 * count + p][...] = slope.astype(BF)
        refs[3 * count + p][...] = dot(low, outer_ref[...]).astype(BF)


def backward_kernel(count, inner_ref, outer_ref, *refs):
    total = jnp.zeros((1, inner_ref.shape[1]), F32)
    for p in range(count):
        grad = (dot_nt(refs[p][...], outer_ref[...]) * refs[count + p][...].astype(F32)).astype(BF)
        refs[2 * count + p][...] = grad
        refs[3 * count + p][...] = dot_nt(grad, inner_ref[...]).astype(BF)
        total = total + jnp.sum(grad.astype(F32), axis=0, keepdims=True)
    refs[-1][...] = total


def products_kernel(count, shard_ref, *refs):
    acts, grads, hidden, inner = [refs[i * count : (i + 1) * count] for i in range(4)]
    *outs, out_ref, outer_acc, inner_acc = refs[4 * count :]
    for p in range(count):
        term = dot_tn(acts[p][...], grads[p][...])
        if p == 0:
            outer_acc[...] = term
        else:
            outer_acc[...] += term
    for r, out in enumerate(outs):
        out[...] = outer_acc[block_at(shard_ref[r], out.shape[0]), :].astype(BF)
    for p in range(count):
        term = dot_tn(hidden[p][...], inner[p][...])
        if p == 0:
            inner_acc[...] = term
        else:
            inner_acc[...] += term
    out_ref[...] = inner_acc[...].astype(BF)


def inner_outer_kernel(inner_ref, *refs):
    parts, out_ref = refs[:-1], refs[-1]
    total = add_up([r[...] for r in parts])
    units = total.shape[0]
    out_ref[:units, :] = total.astype(BF)
    times = out_ref.shape[1] // inner_ref.shape[1]
    rows = inner_ref.shape[0] // times
    for i in range(times):
        out_ref[units:, i * inner_ref.shape[1] : (i + 1) * inner_ref.shape[1]] = inner_ref[i * rows : (i + 1) * rows, :]


def finish_forward_kernel(units, all_ref, outer_ref, inner_ref):
    count, height, width = all_ref.shape
    rows = height - units
    times = inner_ref.shape[0] // rows
    share = width // times
    stretch = units * count
    for c in range(count):
        outer_ref[c * units : (c + 1) * units, :] = all_ref[c, :units, :].astype(F32)
        for i in range(times):
            for s in range(share // units):
                inner_ref[i * rows : (i + 1) * rows, s * stretch + c * units : s * stretch + (c + 1) * units] = all_ref[
                    c, units:, i * share + s * units : i * share + (s + 1) * units
                ].astype(F32)


def last_sum_kernel(count, *refs):
    packs, wos, out_ref = refs[:count], refs[count : 2 * count], refs[-1]
    total = add_up([r[...] for r in packs]).astype(BF)
    height = total.shape[0]
    for i in range(total.shape[1] // LANES):
        out_ref[i * height : (i + 1) * height, :] = total[:, i * LANES : (i + 1) * LANES]
    total = add_up([r[...] for r in wos]).astype(BF)
    base = total.shape[1] // LANES
    strip = total.shape[0]
    for i in range(base):
        row = height * 3 + i * strip
        out_ref[row : row + strip, :] = total[:, i * LANES : (i + 1) * LANES]


def into_kernel(factor, triple_ref, w_ref, *outs):
    rows = outs[0].shape[0]
    for r, out in enumerate(outs):
        term = dot_nt(triple_ref[r * rows : (r + 1) * rows, :], w_ref[...])
        out[...] = (term if factor == 1.0 else term * factor).astype(BF)


def qkv_product_kernel(count, shard_ref, triple_ref, one_ref, two_ref, inner_ref, *refs):
    pieces, outs, (acc, bias) = refs[:count], refs[count:-2], refs[-2:]
    row = 0
    bias[...] = jnp.zeros_like(bias)
    bias[0:1, :] = jnp.sum(triple_ref[...].astype(F32), axis=0, keepdims=True)
    for p, piece in enumerate(pieces):
        rows = piece.shape[0]
        term = dot_tn(piece[...], triple_ref[row : row + rows, :])
        if p == 0:
            acc[...] = term
        else:
            acc[...] += term
        row += rows
    depth = acc.shape[0] // len(outs)
    units = inner_ref.shape[1]
    for r, out in enumerate(outs):
        at = shard_ref[r]
        out[:depth, :] = acc[block_at(at, depth), :].astype(BF)
        for i in range(3):
            bias[1 + i : 2 + i, :depth] = one_ref[i : i + 1, block_at(at, depth)]
            bias[4 + i : 5 + i, :depth] = two_ref[i : i + 1, block_at(at, depth)]
        bias[7:8, 2 * LANES : 2 * LANES + units] = inner_ref[pl.ds(at, 1), :]
        out[depth:, :] = bias[...].astype(BF)


def finish_kernel(shard_ref, offs_ref, *refs):
    pieces, (q_ref, k_ref, v_ref, wo_ref, vec_ref, inner_ref, bias) = refs[:-7], refs[-7:]
    depth = q_ref.shape[0]
    height = depth + EXTRA
    cols = LANES
    total = None
    for r, block in enumerate(Cube.blocks(pieces)):
        block = jnp.concatenate([p[...] for p in block], axis=0)
        lanes = block_at(offs_ref[r], cols)
        for i, out in enumerate((q_ref, k_ref, v_ref)):
            out[:, lanes] = block[i * height : i * height + depth, :].astype(F32)
        tails = [block[i * height + depth : (i + 1) * height, :].astype(F32) for i in range(3)]
        bias[0:8, lanes] = jnp.broadcast_to(tails[0][0:1, :], (8, cols))
        bias[8:16, lanes] = jnp.broadcast_to(tails[2][0:1, :], (8, cols))
        inner_ref[:, lanes] = jnp.broadcast_to(tails[2][7:8, :], (8, cols))
        tail = jnp.concatenate(tails, axis=1)
        total = tail if total is None else total + tail
        strip = (block.shape[0] - 3 * height) * LANES // wo_ref.shape[1]
        for i in range(wo_ref.shape[1] // LANES):
            row = 3 * height + i * strip
            wo_ref[block_at(offs_ref[r], strip), i * LANES : (i + 1) * LANES] = block[row : row + strip, :].astype(F32)
    mine = block_at(shard_ref[0], depth)
    vec_ref[0:1, :] = bias[0:1, mine]
    vec_ref[1:2, :] = bias[8:9, mine]
    vec_ref[2:8, :] = total[1:7, :depth]


def flip(source, bit):
    return lax.ppermute(source, "ctx", [(i, i ^ bit) for i in range(8)])


def shard_flip(source, bit, shards):
    return lax.ppermute(source, "wsh", [(i, i ^ bit) for i in range(shards)])


class Cube:
    def __init__(self):
        self.count = 8

    def at(self, r):
        return lax.axis_index("ctx") ^ r

    def gather(self, own, work=None, early=(), late=()):
        half = own.shape[0] // 32 * 16
        side, down, core = flip(own, 2), flip(own, 4), flip(own, 1)
        if work is not None:
            first = work([own, core])
        side, down, core = after((side, down, core), *([first] if work is not None else early))
        far_a, far_b = flip(side[:half], 4), flip(down[half:], 2)
        side1, down1 = flip(side, 1), flip(down, 1)
        if work is not None:
            second = work([side, side1, down, down1])
        far_a, far_b = after((far_a, far_b), *([second] if work is not None else late))
        far1_a, far1_b = flip(far_a, 1), flip(far_b, 1)
        pieces = [own, core, side, side1, down, down1, far_a, far_b, far1_a, far1_b]
        if work is None:
            return pieces
        third = work(pieces[6:])
        return pieces, [[*a, *b, *c] for a, b, c in zip(first, second, third)]

    def gather_slab(self, own, first, second):
        pair = jnp.concatenate([own, after(flip(own, 2), first)], axis=0)
        four = jnp.concatenate([pair, after(flip(pair, 4), second)], axis=0)
        return [four, flip(four, 1)]

    slab_order = (0, 2, 4, 6, 1, 3, 5, 7)

    def scatter_slab(self, keep, send):
        def fold(half, other):
            return half.astype(F32) + other.astype(F32)

        four = fold(keep, flip(send, 1)).astype(BF)
        half = four.shape[0] // 2
        two = fold(four[:half], flip(four[half:], 2)).astype(BF)
        half = half // 2
        return fold(two[:half], flip(two[half:], 4)).astype(BF)

    def places(self, rows):
        own = [self.at(r) * rows for r in range(8)]
        half = rows // 2
        return own[:6] + [own[6], own[6] + half, own[7], own[7] + half]

    @staticmethod
    def blocks(pieces):
        return [(p,) for p in pieces[:6]] + [(pieces[6], pieces[7]), (pieces[8], pieces[9])]

    def scatter(self, pieces):
        own, core, side, side1, down, down1, far_a, far_b, far1_a, far1_b = pieces
        half = own.shape[0] // 2
        far_a = (far_a.astype(F32) + flip(far1_a, 1).astype(F32)).astype(BF)
        over_side = flip(far_a, 2)
        far_b = (far_b.astype(F32) + flip(far1_b, 1).astype(F32)).astype(BF)
        over_down = flip(far_b, 4)
        side = side.astype(F32) + flip(side1, 1).astype(F32)
        down = down.astype(F32) + flip(down1, 1).astype(F32)
        side_a = flip(side[:half].astype(BF), 2)
        down_b = flip(down[half:].astype(BF), 4)
        side_b = flip((side[half:] + over_down.astype(F32)).astype(BF), 2)
        down_a = flip((down[:half] + over_side.astype(F32)).astype(BF), 4)
        return [own, flip(core, 1), side_a, down_a, side_b, down_b], 2, 2, (over_side, over_down)

    def exchange(self, blocks):
        return [blocks[0]] + [flip(blocks[r], r) for r in range(1, 8)]


class Line:
    def __init__(self, count):
        self.count = count

    def at(self, r):
        return jnp.int32(r)

    def gather(self, own, work=None, early=(), late=()):
        pieces = list(lax.all_gather(own, "ctx", axis=0, tiled=False))
        if work is None:
            return pieces
        groups = [work(group) for group in grouped(pieces, 4)]
        return pieces, [[piece for part in parts for piece in part] for parts in zip(*groups)]

    def places(self, rows):
        return [jnp.int32(r * rows) for r in range(self.count)]

    def scatter(self, pieces):
        whole = jnp.concatenate(pieces, axis=0)
        return [lax.psum_scatter(whole, "ctx", scatter_dimension=0, tiled=True)], 1, 0, ()

    def exchange(self, blocks):
        return list(lax.all_to_all(jnp.stack(blocks), "ctx", 0, 0, tiled=False))


def grouped(items, size):
    return [items[i : i + size] for i in range(0, len(items), size)]


def local(
    tokens, starts, query_weight, key_weight, value_weight, output_weight, inner_weight, outer_weight,
    query_bias, value_bias, output_bias, first_gain, first_shift, inner_bias, outer_bias,
    second_gain, second_shift, cotangent,
):
    count, shards = lax.axis_size("ctx"), lax.axis_size("wsh")
    net = Cube() if count == 8 else Line(count)
    me, shard = lax.axis_index("ctx"), lax.axis_index("wsh")
    x = tokens[0]
    rows, width = x.shape
    length = rows * count
    size = width // HEADS
    heads = max(1, HEADS // count)
    copies = max(1, count // HEADS)
    cols = heads * size
    wide = -(-cols // LANES) * LANES
    depth = width // shards
    units = outer_weight.shape[0] // count
    strip = depth // count
    scale = size**-0.5
    shard_ids = jnp.stack([shard ^ r for r in range(shards)])
    offs = jnp.stack([net.at(r) // copies for r in range(0, count, copies)])
    places = jnp.stack(net.places(rows))

    first_col = me // copies * cols

    def own_columns(w):
        return jnp.pad(lax.dynamic_slice_in_dim(w, first_col, cols, 1), ((0, 0), (0, wide - cols)))

    weights, lane = [query_weight, key_weight, value_weight], first_col
    if cols % LANES:
        weights, lane = [own_columns(w) for w in weights], jnp.int32(0)
    vectors = [query_bias, value_bias, output_bias, first_gain, first_shift, outer_bias, second_gain,
               second_shift, inner_bias]
    vectors = [v.reshape(-1, LANES) for v in vectors]
    height = -(-sum(v.shape[0] for v in vectors) * LANES // (24 * wide)) * 8
    (pack,) = call(
        pack_kernel, [lane[None]], [*weights, *vectors], [struct((depth + height, 3 * wide), BF)], 2, "pack"
    )
    packs = [pack] + [shard_flip(pack, r, shards) for r in range(1, shards)]
    vec, inner_all = call(
        functools.partial(unpack_kernel, shards), [shard_ids], packs,
        [struct((8, width), F32), struct((8 * shards, inner_bias.shape[0]), F32)], 2, "unpack",
    )
    pieces = net.gather(x, early=[pack], late=[vec])
    wo_own = lax.dynamic_slice_in_dim(output_weight, me * strip, strip, 0)
    wo_own = after(wo_own, pieces[6:8])
    wo_parts = [wo_own] + [shard_flip(wo_own, r, shards) for r in range(1, shards)]
    bias = jnp.pad(lax.dynamic_slice(vec, (0, first_col), (8, cols)), ((0, 0), (0, wide - cols)))
    inner_b = lax.dynamic_slice_in_dim(inner_all[::8], me * units, units, 1).reshape(1, -1)

    qkv_rows = []
    done = 0
    for group in grouped(pieces, 10):
        group_rows = sum(p.shape[0] for p in group)
        sheet = struct((group_rows, wide), BF)
        tail = struct((group_rows, LANES), BF)
        qkv, *made = call(
            functools.partial(project_kernel, len(group), shards, wide, scale),
            [shard_ids, places[done : done + len(group)], starts[0]],
            [*group, *packs, bias],
            [struct((width, 3 * wide), BF), sheet, sheet, sheet, tail, tail],
            4, "project",
        )
        qkv_rows.append(made)
        done += len(group)
    q, k, v, qt, kt = [made[0] if len(made) == 1 else jnp.concatenate(made) for made in zip(*qkv_rows)]

    inner_own = jnp.concatenate(
        [lax.dynamic_slice_in_dim(inner_weight, s * units * count + me * units, units, 1) for s in range(shards)],
        axis=1,
    )
    outer_own = lax.dynamic_slice_in_dim(outer_weight, me * units, units, 0)
    inner_own, outer_own = after((inner_own, outer_own), packs, pieces[6:8])
    inner = lax.all_gather(inner_own, "wsh", axis=0, tiled=True)
    outer = lax.all_gather(outer_own, "wsh", axis=0, tiled=True)
    mixed_low, mixed, lse = attend(q, qt, k, kt, v, rows, heads, size)
    if isinstance(net, Cube):
        ids = jnp.stack([net.at(r) for r in net.slab_order])
        slabs = net.gather_slab(jnp.concatenate(wo_parts, axis=0), q, mixed_low)
        (wo,) = call(
            functools.partial(assemble_kernel, shards, strip), [shard_ids, ids], slabs,
            [struct((width, width), BF)], 2, "assemble",
        )
    else:
        wo_slab = jnp.zeros((shards, strip, width), BF)
        for r in range(shards):
            wo_slab = lax.dynamic_update_slice(wo_slab, wo_parts[r][None], (shard ^ r, jnp.int32(0), jnp.int32(0)))
        wo = lax.all_gather(wo_slab, "ctx", axis=0, tiled=False)
        wo = wo.transpose(1, 0, 2, 3).reshape(width, width)

    blocks = net.exchange([mixed_low[r * rows : (r + 1) * rows, :cols] for r in range(count)])[::copies]
    groups = len(blocks)
    full, low_full, tall = struct((rows, width), F32), struct((rows, width), BF), struct((rows, 1), F32)
    sums = struct((8, width), F32)
    hidden, hidden_low, normed, root = call(
        functools.partial(first_norm_kernel, groups), [offs], [x, wo, vec, *blocks],
        [full, low_full, full, tall], 5, "first_norm",
    )

    def forward(group):
        sizes = [p.shape[0] for p in group]
        mids = [struct((s, units * shards), BF) for s in sizes]
        made = call(
            functools.partial(forward_kernel, len(group)), [], [inner, inner_b, outer, *group],
            mids + mids + [struct((s, width), BF) for s in sizes], 1.5 * sum(sizes) / 256, "forward",
        )
        n = len(group)
        return made[:n], made[n : 2 * n], made[2 * n :]

    hidden_all, (acts, slopes, branch) = net.gather(hidden_low, forward)
    parts, n_whole, n_half, _ = net.scatter(branch)
    result, resid, branch_grad, sums_two = call(
        functools.partial(second_norm_kernel, n_whole, n_half), [], [hidden, vec, cotangent[0], *parts],
        [low_full, full, low_full, sums], 4, "second_norm",
    )

    inner_sums, waiting = [], list(slopes)

    def backward(group):
        sizes = [p.shape[0] for p in group]
        n = len(group)
        slope, waiting[:n] = waiting[:n], []
        made = call(
            functools.partial(backward_kernel, n), [], [inner, outer, *group, *slope],
            [struct((s, units * shards), BF) for s in sizes]
            + [struct((s, width), BF) for s in sizes]
            + [struct((1, units * shards), F32)],
            1.5 * sum(sizes) / 256, "backward",
        )
        inner_sums.append(made[-1])
        return made[:n], made[n:-1]

    grad_all, (inner_grads, hidden_grads) = net.gather(branch_grad, backward)
    parts, n_whole, n_half, moved = net.scatter(hidden_grads)
    *outer_parts, inner_wg = call(
        functools.partial(products_kernel, len(acts)), [shard_ids],
        [*after(acts, moved), *grad_all, *hidden_all, *inner_grads],
        [struct((units, width), BF)] * shards + [struct((width, units * shards), BF)], 12, "products",
        [pltpu.VMEM((units * shards, width), F32), pltpu.VMEM((width, units * shards), F32)], None,
    )
    parts = after(parts, inner_wg)
    outer_parts = [outer_parts[0]] + [shard_flip(outer_parts[r], r, shards) for r in range(1, shards)]
    inner_own_grad = lax.psum_scatter(inner_wg, "wsh", scatter_dimension=0, tiled=True)

    first, attn_grad, sums_one, *mixed_grads = call(
        functools.partial(first_back_kernel, groups, n_whole, n_half), [offs],
        [resid, normed, root, vec, wo, *parts],
        [full, low_full, sums] + [struct((rows, cols), BF)] * groups, 5, "first_back",
    )
    if copies > 1:
        mixed_grads = [b for b in mixed_grads for _ in range(copies)]
    exchanged = net.exchange(mixed_grads)
    mixed_grad = jnp.concatenate(exchanged, axis=0)
    mixed_grad = jnp.pad(mixed_grad, ((0, 0), (0, wide - cols)))

    order = [0, 4, 2, 6, 1, 5, 3, 7] if isinstance(net, Cube) else list(range(count))
    halves = 2 if isinstance(net, Cube) else 1
    ids = jnp.stack([net.at(r) for r in order])

    def mixed_product(offs_ref, ids_ref, low_ref, *refs):
        outs, acc = refs[groups:-1], refs[-1]
        for r, block in enumerate(refs[:groups]):
            acc[block_at(offs_ref[r], cols), :] = dot_tn(block[...], low_ref[...])
        per = count // halves
        for i in range(count):
            for s in range(shards):
                row = (i % per * shards + s) * strip
                at = pl.multiple_of(s * depth + ids_ref[i] * strip, strip)
                outs[i // per][row : row + strip, :] = acc[pl.ds(at, strip), :].astype(BF)

    wo_grad = call(
        mixed_product, [offs, ids], [after(attn_grad, exchanged[1]), *blocks],
        [struct((width // halves, width), BF)] * halves, 4, "mixed_product", [pltpu.VMEM((width, width), F32)],
    )
    if isinstance(net, Cube):
        wo_grad = net.scatter_slab(*wo_grad)
    else:
        wo_grad = lax.psum_scatter(wo_grad[0], "ctx", scatter_dimension=0, tiled=True)
    wo_parts = [lax.dynamic_slice_in_dim(wo_grad, (shard ^ r) * strip, strip, 0) for r in range(shards)]
    wo_parts = [wo_parts[0]] + [shard_flip(wo_parts[r], r, shards) for r in range(1, shards)]
    triple = attend_back(q, qt, k, kt, v, mixed_grad, mixed, lse, rows, heads, size, scale)
    (forward_own,) = call(
        inner_outer_kernel, [], [inner_own_grad, *after(outer_parts, triple)],
        [struct((units + depth * units * shards // width, width), BF)], 2, "pack_forward",
    )
    forward_all = lax.all_gather(forward_own, "ctx", axis=0, tiled=False)
    inner_sum = add_up(inner_sums).reshape(shards, units)
    qkv_pack = struct((depth + EXTRA, 3 * wide), BF)
    packs = call(
        functools.partial(qkv_product_kernel, len(pieces)), [shard_ids],
        [triple, sums_one, sums_two, inner_sum, *pieces], [qkv_pack] * shards, 5, "qkv_product",
        [pltpu.VMEM((width, 3 * wide), F32), pltpu.VMEM((EXTRA, 3 * wide), F32)], None,
    )
    into = call(
        functools.partial(into_kernel, 1.0 / copies), [], [after(triple, packs), qkv], [low_full] * count, 3, "into",
    )
    if isinstance(net, Cube):
        half = rows // 2
        into = [*into[:6]] + [into[6][:half], into[6][half:], into[7][:half], into[7][half:]]
    parts, n_whole, n_half, _ = net.scatter(into)
    (input_grad,) = call(
        functools.partial(input_kernel, n_whole, n_half), [], [first, *parts], [low_full], 2, "input_sum"
    )
    packs = [packs[0]] + [shard_flip(packs[r], r, shards) for r in range(1, shards)]
    if isinstance(net, Cube):
        (last_own,) = call(
            functools.partial(last_sum_kernel, shards), [], [*packs, *wo_parts],
            [struct((3 * (depth + EXTRA) + strip * width // LANES, LANES), BF)], 2, "last_sum",
        )
        square = struct((depth, width), F32)
        query_out, key_out, value_out, wo_out, vecs, inner_vec = call(
            finish_kernel, [shard_ids, offs], net.gather(last_own),
            [square, square, square, square, struct((8, depth), F32), struct((8, units * count), F32)], 4, "finish",
            [pltpu.VMEM((16, width), F32)],
        )
        outer_out, inner_out = call(
            functools.partial(finish_forward_kernel, units), [], [forward_all],
            [struct((units * count, width), F32), struct((depth, units * count * shards), F32)], 6, "finish_forward",
        )
        vecs = [vecs[i] for i in range(8)]
        inner_vec = inner_vec[0]
    else:

        def everywhere(parts):
            return lax.all_gather(add_up(parts).astype(BF), "ctx", axis=0, tiled=False).astype(F32)

        wo_out = everywhere(wo_parts).reshape(depth, width)
        gathered = everywhere(packs)
        out3 = gathered[::copies, :depth].reshape(-1, depth, 3, wide)[..., :cols]
        query_out, key_out, value_out = out3.transpose(2, 1, 0, 3).reshape(3, depth, width)
        tail = gathered[:, depth:]
        both = tail[::copies, 0].reshape(-1, 3, wide)[..., :cols].transpose(1, 0, 2).reshape(3, width)
        both = lax.dynamic_slice_in_dim(both, shard * depth, depth, 1)
        six = jnp.sum(tail[:, 1:7, :depth], axis=0)
        vecs = [both[0], both[2]] + [six[i] for i in range(6)]
        inner_vec = tail[:, 7, 2 * wide : 2 * wide + units].reshape(-1)
        forward_all = forward_all.astype(F32)
        outer_out = forward_all[:, :units].reshape(-1, width)
        times = width // (units * shards)
        inner_out = forward_all[:, units:].reshape(count, depth // times, times, shards, units)
        inner_out = inner_out.transpose(2, 1, 3, 0, 4).reshape(depth, -1)
    return (
        result[None], input_grad[None], query_out, key_out, value_out, wo_out, inner_out, outer_out,
        vecs[0], vecs[1], vecs[2], vecs[3], vecs[4], inner_vec, vecs[5], vecs[6], vecs[7],
    )


def solution(mesh):
    sheet, matrix, vector = P("wsh", "ctx", None), P("wsh", None), P("wsh")
    return jax.shard_map(
        local,
        mesh=mesh,
        in_specs=(sheet, matrix) + (matrix,) * 6 + (vector,) * 9 + (sheet,),
        out_specs=(sheet, sheet) + (matrix,) * 6 + (vector,) * 9,
        check_vma=False,
    )
```

time: 545 us -> 387 us (0.71)
  blocking collectives: 94.7 us -> 0 us
  local copies, waits for them, and re-layouts: 99.9 us -> 45.3 us
  matrix products: 43.3 us -> 0 us
  Pallas kernels: 61.8 us -> 103 us
  starting transfers between devices: 63 us -> 94.4 us
  waiting for transfers between devices: 134 us -> 113 us
  other arithmetic: 25.9 us -> 8.96 us
    reduce_scatter x5 -> x1, waiting for transfers between devices: 57.2 us -> 0.02 us  [local(): lax.psum_scatter(inner_wg, 'wsh', scatter_dimension=0, tiled=True)]
    all_gather x4 -> x0, blocking collectives: 51.5 us -> none  [the longest x1 15.8 us: local(): qkv = lax.all_gather(qkv_own, 'wsh', axis=0, tiled=True)]
    dot_general x9 -> x0, matrix products: 43.3 us -> none  [the longest x3 17.9 us: dot_tn(): lax.dot_general(a, b, (((0,), (0,)), ((), ())), preferred_element_type=F32)]
    psum x1 -> x0, blocking collectives: 43.2 us -> none  [local(): vecs = lax.psum(vecs, ('ctx', 'wsh'))]
    pallas_call x5 -> x24, Pallas kernels: 61.8 us -> 103 us  [the longest x22 61.1 us: call(): pl.pallas_call(kernel, in_specs=[IN_SMEM] * len(scalars) + [IN_VMEM] * le...]
    ppermute x68 -> x89, waiting for transfers between devices: 69.4 us -> 98.4 us  [flip(): return lax.ppermute(source, 'ctx', [(i, i ^ bit) for i in range(8)])]
    ppermute x0 -> x15, starting transfers between devices: none -> 15.9 us  [shard_flip(): return lax.ppermute(source, 'wsh', [(i, i ^ bit) for i in range(shards)])]
    ppermute x68 -> x89, starting transfers between devices: 62.3 us -> 78.1 us  [flip(): return lax.ppermute(source, 'ctx', [(i, i ^ bit) for i in range(8)])]
  transfers between devices with their start and end apart: 79 -> 108, of which waited for: 30 -> 37; matrix products, arithmetic and copies ran while one was open for 27% -> 6% of each run, Pallas kernels for 10% -> 25%
where the time goes in v2:
time: 387 us; the launch traced here: 380 us
  waiting for transfers between devices  113 us (29%)
  Pallas kernels  103 us (27%)
  starting transfers between devices  94.4 us (24%)
  local copies, waits for them, and re-layouts  45.3 us (12%)
  between operations  15.6 us (4%)
  other arithmetic  8.96 us (2%)
    ppermute x89, waiting for transfers between devices, flip(): return lax.ppermute(source, 'ctx', [(i, i ^ bit) for i in range(8)])  98.4 us
    ppermute x89, starting transfers between devices, flip(): return lax.ppermute(source, 'ctx', [(i, i ^ bit) for i in range(8)])  78.1 us
    pallas_call x22, Pallas kernels, call(): pl.pallas_call(kernel, in_specs=[IN_SMEM] * len(scalars) + [IN_VMEM] * le...  61.1 us
    unnamed x241, local copies, waits for them, and re-layouts  35.7 us
    pallas_call x1, Pallas kernels, attend_back(): pl.pallas_call(functools.partial(attend_back_kernel, heads, size, scale),...  27.2 us
    ppermute x15, starting transfers between devices, shard_flip(): return lax.ppermute(source, 'wsh', [(i, i ^ bit) for i in range(shards)])  15.9 us
    pallas_call x1, Pallas kernels, attend(): pl.pallas_call(functools.partial(attend_kernel, heads, size), grid=(lengt...  14.6 us
    all_gather x1, waiting for transfers between devices, local(): outer = lax.all_gather(outer_own, 'wsh', axis=0, tiled=True)  9.39 us
  transfers between devices with their start and end apart: 108, of which 37 were waited for; matrix products, arithmetic and copies ran while one was open for 6% of the time, Pallas kernels for 25%

profile of v2, /device:TPU:9, one launch (start us, length us, event | category | flops | bytes accessed | tf_op | source)
XLA Modules:
  0.0 380.0 jit_solution(465303270953456144)
XLA Ops:
  27.3 6.2 %collective-permute-done.1.refs_4_ = bf16[256,1024]{1,0:T(8,128)(2,1)S(1)} collective-permute-done((bf16[256,1024]{1,0:T(8,128)(2,1)}, bf16[256,1024]{1,0:T(8,128)(2,1)S(1)}, u32[]{:S(2)}, u32[]{:S(2)}) %collective-permute-start.1) | collective-permute-done | bytes 524320 | tf_op jit(solution)/shard_map/ppermute | solution.py:479
  41.3 2.0 collective-permute-start.10
  45.8 4.0 %collective-permute-start.14 = (bf16[128,1024]{1,0:T(8,128)(2,1)S(1)}, bf16[128,1024]{1,0:T(8,128)(2,1)S(1)}, u32[]{:S(2)}, u32[]{:S(2)}) collective-permute-start(bf16[128,1024]{1,0:T(8,128)(2,1)S(1)} %collective-permute-done.3.refs_6_), channel_id=1, source_target_pairs={{0,4},{4,0},{8,12},{12,8},{16,20},{20,16},{24,28},{28,24},{1,5},{5... | collective-permute-start | bytes 786440 | tf_op jit(solution)/shard_map/ppermute | solution.py:479
  49.8 2.2 collective-permute-start.15
  56.9 5.2 %project.1 = (bf16[1024,384]{1,0:T(8,128)(2,1)S(1)}, bf16[2048,128]{1,0:T(8,128)(2,1)S(1)}, bf16[2048,128]{1,0:T(8,128)(2,1)S(1)}, bf16[2048,128]{1,0:T(8,128)(2...) custom-call(s32[4]{0:T(128)S(1)} %pad_add_fusion.shard_ref, s32[10]{0:T(128)S(1)} %stack.122.place_ref, ...), custom_call_target="tpu_custom_call" | custom-call | flops 4000000000 | tf_op jit(solution)/shard_map/project/pallas_call | solution.py:55
  63.6 14.6 %attend.1 = (bf16[2048,128]{1,0:T(8,128)(2,1)S(1)}, f32[2048,128]{1,0:T(8,128)S(1)}, f32[8,2048]{1,0:T(8,128)S(1)}) custom-call(bf16[2048,128]{1,0:T(8,128)(2,1)S(1)} %get-tuple-element.181.q_ref, bf16[2048,128]{1,0:T(8,128)(2,1)S(1)} %get-tuple-element.183.qt_ref, bf16[2048,128]{1,0:T(8,128)(2,1)S(1)} %get-tuple-element.184.k_ref, ...), custom_call_target="tpu_custom_call" | custom-call | flops 17999998976 | tf_op jit(solution)/shard_map/attend/pallas_call | solution.py:174
  82.0 2.0 collective-permute-start.24
  84.5 1.8 collective-permute-start.22
  91.9 3.0 first_norm.1
  96.9 1.8 collective-permute-start.25
  100.2 9.4 %all-gather.7.cloned.1.call-done.outer_ref = bf16[512,1024]{1,0:T(8,128)(2,1)} async-done(((bf16[128,1024]{1,0:T(8,128)(2,1)}), bf16[512,1024]{1,0:T(8,128)(2,1)}) %all-gather.7.cloned.1.call-update) | async-done | bytes 1048592 | tf_op jit(solution)/shard_map/all_gather | solution.py:660
  112.3 1.8 forward.3
  117.7 3.3 forward.4
  126.7 2.1 forward.5
  133.3 9.5 %collective-permute-done.39 = bf16[128,1024]{1,0:T(8,128)(2,1)S(1)} collective-permute-done((bf16[128,1024]{1,0:T(8,128)(2,1)S(1)}, bf16[128,1024]{1,0:T(8,128)(2,1)S(1)}, u32[]{:S(2)}, u32[]{:S(2)}) %collective-permute-start.39) | collective-permute-done | bytes 262176 | tf_op jit(solution)/shard_map/ppermute | solution.py:479
  144.6 4.9 %collective-permute-done.40.refs_3_ = bf16[128,1024]{1,0:T(8,128)(2,1)S(1)} collective-permute-done((bf16[128,1024]{1,0:T(8,128)(2,1)S(1)}, bf16[128,1024]{1,0:T(8,128)(2,1)S(1)}, u32[]{:S(2)}, u32[]{:S(2)}) %collective-permute-start.40) | collective-permute-done | bytes 262176 | tf_op jit(solution)/shard_map/ppermute | solution.py:479
  150.6 1.7 second_norm.1
  153.3 2.5 collective-permute-start.45
  157.3 1.9 backward.3
  160.0 9.3 %collective-permute-done.48.refs_2_.refs_14_ = bf16[256,1024]{1,0:T(8,128)(2,1)S(1)} collective-permute-done((bf16[256,1024]{1,0:T(8,128)(2,1)S(1)}, bf16[256,1024]{1,0:T(8,128)(2,1)S(1)}, u32[]{:S(2)}, u32[]{:S(2)}) %collective-permute-start.48) | collective-permute-done | bytes 524320 | tf_op jit(solution)/shard_map/ppermute | solution.py:479
  172.7 2.7 backward.4
  181.1 3.0 backward.5
  189.2 9.8 %collective-permute-done.59 = bf16[128,1024]{1,0:T(8,128)(2,1)S(1)} collective-permute-done((bf16[128,1024]{1,0:T(8,128)(2,1)S(1)}, bf16[128,1024]{1,0:T(8,128)(2,1)S(1)}, u32[]{:S(2)}, u32[]{:S(2)}) %collective-permute-start.59) | collective-permute-done | bytes 262176 | tf_op jit(solution)/shard_map/ppermute | solution.py:479
  202.9 11.2 %products.1 = (bf16[128,1024]{1,0:T(8,128)(2,1)}, bf16[128,1024]{1,0:T(8,128)(2,1)}, bf16[128,1024]{1,0:T(8,128)(2,1)}, bf16[128,1024]{1,0:T(8,128)(2,1)}, bf16[1024,512]{1,0:T(8,128)(2,1)}) custom-call(s32[4]{0:T(128)} %copy-done.8, bf16[256,512]{1,0:T(8,128)(2,1)} %copy-done.88, bf16[256,512]{1,0:T(8,128)(2,1)} %copy-done.89, ...), custom_call_target="tpu_custom_call" | custom-call | flops 12000000000 | tf_op jit(solution)/shard_map/products/pallas_call | solution.py:55
  222.0 2.7 first_back.1
  225.7 2.7 collective-permute-start.65
  230.1 2.1 collective-permute-done.66
  236.0 2.6 collective-permute-done.69
  238.5 2.0 collective-permute-start.71
  240.6 3.0 collective-permute-done.71
  244.4 27.2 %attend_back.1.triple_ref = bf16[2048,384]{1,0:T(8,128)(2,1)} custom-call(bf16[2048,128]{1,0:T(8,128)(2,1)} %copy-done.81, bf16[2048,128]{1,0:T(8,128)(2,1)} %copy-done.84, bf16[2048,128]{1,0:T(8,128)(2,1)} %copy-done.82, bf16[2048,128]{1,0:T(8,128)(2,1)} %copy-done.85, bf16[2048,128]{1,0:T(8,128)(2,1)} %copy-done.83, bf16[2048,128]{1,0:T(8,128)(2,1)} %copy-done.114, ...), custom_call_target="tpu_custom_call" | custom-call | flops 27000000512 | tf_op jit(solution)/shard_map/attend_back/pallas_call | solution.py:229
  276.3 6.3 %qkv_product.1 = (bf16[272,384]{1,0:T(8,128)(2,1)}, bf16[272,384]{1,0:T(8,128)(2,1)}, bf16[272,384]{1,0:T(8,128)(2,1)}, bf16[272,384]{1,0:T(8,128)(2,1)}) custom-call(s32[4]{0:T(128)} %copy-done.8, bf16[2048,384]{1,0:T(8,128)(2,1)} %attend_back.1.triple_ref, f32[8,1024]{1,0:T(8,128)} %copy-done.112, f32[8,1024]{1,0:T(8,128)} %copy-done.110, ...), custom_call_target="tpu_custom_call" | custom-call | flops 5000000000 | tf_op jit(solution)/shard_map/qkv_product/pallas_call | solution.py:55
  284.2 2.4 into.1
  288.1 12.2 %collective-permute-done.87 = bf16[256,1024]{1,0:T(8,128)(2,1)S(1)} collective-permute-done((bf16[256,1024]{1,0:T(8,128)(2,1)S(1)}, bf16[256,1024]{1,0:T(8,128)(2,1)S(1)}, u32[]{:S(2)}, u32[]{:S(2)}) %collective-permute-start.87) | collective-permute-done | bytes 524320 | tf_op jit(solution)/shard_map/ppermute | solution.py:479
  301.2 1.7 slice.205
  304.5 2.1 collective-permute-start.84
  306.9 1.7 collective-permute-start.73
  309.8 6.9 %collective-permute-done.88 = bf16[128,1024]{1,0:T(8,128)(2,1)S(1)} collective-permute-done((bf16[128,1024]{1,0:T(8,128)(2,1)}, bf16[128,1024]{1,0:T(8,128)(2,1)S(1)}, u32[]{:S(2)}, u32[]{:S(2)}) %collective-permute-start.88) | collective-permute-done | bytes 262176 | tf_op jit(solution)/shard_map/ppermute | solution.py:479
  322.9 3.8 %collective-permute-done.85.refs_3_ = bf16[272,384]{1,0:T(8,128)(2,1)S(1)} collective-permute-done((bf16[272,384]{1,0:T(8,128)(2,1)}, bf16[272,384]{1,0:T(8,128)(2,1)S(1)}, u32[]{:S(2)}, u32[]{:S(2)}) %collective-permute-start.85) | collective-permute-done | bytes 208928 | tf_op jit(solution)/shard_map/ppermute | solution.py:483
  326.7 4.2 %collective-permute-start.72 = (bf16[256,1024]{1,0:T(8,128)(2,1)S(1)}, bf16[256,1024]{1,0:T(8,128)(2,1)S(1)}, u32[]{:S(2)}, u32[]{:S(2)}) collective-permute-start(bf16[256,1024]{1,0:T(8,128)(2,1)S(1)} %get-tuple-element.299), channel_id=1, source_target_pairs={{0,4},{4,0},{8,12},{12,8},{16,20},{20,16},{24,28},{28,24},{1,5},{5... | collective-permute-start | bytes 1572872 | tf_op jit(solution)/shard_map/ppermute | solution.py:479
  334.4 3.6 collective-permute-done.80
  340.0 3.9 %collective-permute-done.93.refs_4_ = bf16[1072,128]{1,0:T(8,128)(2,1)S(1)} collective-permute-done((bf16[1072,128]{1,0:T(8,128)(2,1)S(1)}, bf16[1072,128]{1,0:T(8,128)(2,1)S(1)}, u32[]{:S(2)}, u32[]{:S(2)}) %collective-permute-start.93) | collective-permute-done | bytes 274464 | tf_op jit(solution)/shard_map/ppermute | solution.py:479
  345.9 3.0 collective-permute-done.74.refs_2_
  349.1 9.5 %collective-permute-done.97.refs_6_ = bf16[528,128]{1,0:T(8,128)(2,1)S(1)} collective-permute-done((bf16[528,128]{1,0:T(8,128)(2,1)S(1)}, bf16[528,128]{1,0:T(8,128)(2,1)S(1)}, u32[]{:S(2)}, u32[]{:S(2)}) %collective-permute-start.97) | collective-permute-done | bytes 135200 | tf_op jit(solution)/shard_map/ppermute | solution.py:479
  358.6 2.5 collective-permute-start.95
  363.1 2.7 finish.1
  367.0 2.2 copy-done.10
  369.2 4.1 %finish_forward.1 = (f32[1024,1024]{1,0:T(8,128)}, f32[256,4096]{1,0:T(8,128)}) custom-call(bf16[8,256,1024]{2,1,0:T(8,128)(2,1)S(1)} %bitcast.52), custom_call_target="tpu_custom_call" | custom-call | flops 6000000000 | tf_op jit(solution)/shard_map/finish_forward/pallas_call | solution.py:55
  (495 shorter events, 133.5 us)
Async XLA Ops:
  7.2 93.0 %all-gather.5.cloned.1.call-start = ((), (), s32[]{:S(2)}) async-start(), calls=%async_computation.1 | async-start | bytes 1310720 | tf_op jit(solution)/shard_map/all_gather | solution.py:659
  7.3 17.9 %collective-permute-start.2 = (bf16[256,1024]{1,0:T(8,128)(2,1)}, bf16[256,1024]{1,0:T(8,128)(2,1)}, u32[]{:S(2)}, u32[]{:S(2)}) collective-permute-start(bf16[256,1024]{1,0:T(8,128)(2,1)} %bitcast.8.refs_0_.x_ref), channel_id=1, source_target_pairs={{0,4},{4,0},{8,12},{12,8},{16,20},{20,16},{24,28},{28,24},{1,5},{5... | collective-permute-start | bytes 1572872 | tf_op jit(solution)/shard_map/ppermute | solution.py:479
  17.8 18.0 %collective-permute-start.7 = (bf16[264,384]{1,0:T(8,128)(2,1)}, bf16[264,384]{1,0:T(8,128)(2,1)}, u32[]{:S(2)}, u32[]{:S(2)}) collective-permute-start(bf16[264,384]{1,0:T(8,128)(2,1)} %pack.1.refs_0_.refs_10_), channel_id=1, source_target_pairs={{0,3},{1,2},{2,1},{3,0},{4,7},{5,6},{6,5},{7,4},{8,11},{9,10},{10,... | collective-permute-start | bytes 608264 | tf_op jit(solution)/shard_map/ppermute | solution.py:483
  19.1 17.6 %collective-permute-start.6 = (bf16[264,384]{1,0:T(8,128)(2,1)}, bf16[264,384]{1,0:T(8,128)(2,1)}, u32[]{:S(2)}, u32[]{:S(2)}) collective-permute-start(bf16[264,384]{1,0:T(8,128)(2,1)} %pack.1.refs_0_.refs_10_), channel_id=1, source_target_pairs={{0,2},{1,3},{2,0},{3,1},{4,6},{5,7},{6,4},{7,5},{8,10},{9,11},{10,... | collective-permute-start | bytes 608264 | tf_op jit(solution)/shard_map/ppermute | solution.py:483
  20.1 13.4 %collective-permute-start.1 = (bf16[256,1024]{1,0:T(8,128)(2,1)}, bf16[256,1024]{1,0:T(8,128)(2,1)S(1)}, u32[]{:S(2)}, u32[]{:S(2)}) collective-permute-start(bf16[256,1024]{1,0:T(8,128)(2,1)} %bitcast.8.refs_0_.x_ref), channel_id=1, source_target_pairs={{0,16},{4,20},{8,24},{12,28},{16,0},{20,4},{24,8},{28,12},{1,17},{... | collective-permute-start | bytes 1572872 | tf_op jit(solution)/shard_map/ppermute | solution.py:479
  21.4 12.8 %collective-permute-start = (bf16[256,1024]{1,0:T(8,128)(2,1)}, bf16[256,1024]{1,0:T(8,128)(2,1)S(1)}, u32[]{:S(2)}, u32[]{:S(2)}) collective-permute-start(bf16[256,1024]{1,0:T(8,128)(2,1)} %bitcast.8.refs_0_.x_ref), channel_id=1, source_target_pairs={{0,8},{4,12},{8,0},{12,4},{16,24},{20,28},{24,16},{28,20},{1,9},{5... | collective-permute-start | bytes 1572872 | tf_op jit(solution)/shard_map/ppermute | solution.py:479
  25.2 11.5 %collective-permute-start.5 = (bf16[264,384]{1,0:T(8,128)(2,1)}, bf16[264,384]{1,0:T(8,128)(2,1)S(1)}, u32[]{:S(2)}, u32[]{:S(2)}) collective-permute-start(bf16[264,384]{1,0:T(8,128)(2,1)} %pack.1.refs_0_.refs_10_), channel_id=1, source_target_pairs={{0,1},{1,0},{2,3},{3,2},{4,5},{5,4},{6,7},{7,6},{8,9},{9,8},{10,11... | collective-permute-start | bytes 608264 | tf_op jit(solution)/shard_map/ppermute | solution.py:483
  37.9 18.9 %collective-permute-start.12 = (bf16[256,1024]{1,0:T(8,128)(2,1)S(1)}, bf16[256,1024]{1,0:T(8,128)(2,1)S(1)}, u32[]{:S(2)}, u32[]{:S(2)}) collective-permute-start(bf16[256,1024]{1,0:T(8,128)(2,1)S(1)} %collective-permute-done.refs_2_), channel_id=1, source_target_pairs={{0,4},{4,0},{8,12},{12,8},{16,20},{20,16},{24,28},{28,24},{1,5},{5... | collective-permute-start | bytes 1572872 | tf_op jit(solution)/shard_map/ppermute | solution.py:479
  39.3 17.5 %collective-permute-start.13 = (bf16[256,1024]{1,0:T(8,128)(2,1)S(1)}, bf16[256,1024]{1,0:T(8,128)(2,1)S(1)}, u32[]{:S(2)}, u32[]{:S(2)}) collective-permute-start(bf16[256,1024]{1,0:T(8,128)(2,1)S(1)} %collective-permute-done.1.refs_4_), channel_id=1, source_target_pairs={{0,4},{4,0},{8,12},{12,8},{16,20},{20,16},{24,28},{28,24},{1,5},{5... | collective-permute-start | bytes 1572872 | tf_op jit(solution)/shard_map/ppermute | solution.py:479
  44.9 64.8 %all-gather.7.cloned.1.call-start = ((), (), s32[]{:S(2)}) async-start(), calls=%async_computation.2 | async-start | bytes 1310720 | tf_op jit(solution)/shard_map/all_gather | solution.py:660
  63.1 16.7 %collective-permute-start.16 = (bf16[256,1024]{1,0:T(8,128)(2,1)S(1)}, bf16[256,1024]{1,0:T(8,128)(2,1)S(1)}, u32[]{:S(2)}, u32[]{:S(2)}) collective-permute-start(bf16[256,1024]{1,0:T(8,128)(2,1)S(1)} %get-tuple-element.351), channel_id=1, source_target_pairs={{0,16},{4,20},{8,24},{12,28},{16,0},{20,4},{24,8},{28,12},{1,17},{... | collective-permute-start | bytes 1572872 | tf_op jit(solution)/shard_map/ppermute | solution.py:479
  81.7 190.0 %reduce-scatter.2.cloned.1.call-start = ((), (), s32[]{:S(2)}) async-start(), calls=%async_computation.3 | async-start | bytes 1310720 | tf_op jit(solution)/shard_map/reduce_scatter | solution.py:728
  96.9 12.7 %collective-permute-start.25 = (bf16[256,1024]{1,0:T(8,128)(2,1)S(1)}, bf16[256,1024]{1,0:T(8,128)(2,1)S(1)}, u32[]{:S(2)}, u32[]{:S(2)}) collective-permute-start(bf16[256,1024]{1,0:T(8,128)(2,1)S(1)} %get-tuple-element.193.refs_0_.refs_20_), channel_id=1, source_target_pairs={{0,4},{4,0},{8,12},{12,8},{16,20},{20,16},{24,28},{28,24},{1,5},{5... | collective-permute-start | bytes 1572872 | tf_op jit(solution)/shard_map/ppermute | solution.py:479
  98.7 15.4 %collective-permute-start.28 = (bf16[256,1024]{1,0:T(8,128)(2,1)S(1)}, bf16[256,1024]{1,0:T(8,128)(2,1)S(1)}, u32[]{:S(2)}, u32[]{:S(2)}) collective-permute-start(bf16[256,1024]{1,0:T(8,128)(2,1)S(1)} %get-tuple-element.193.refs_0_.refs_20_), channel_id=1, source_target_pairs={{0,16},{4,20},{8,24},{12,28},{16,0},{20,4},{24,8},{28,12},{1,17},{... | collective-permute-start | bytes 1572872 | tf_op jit(solution)/shard_map/ppermute | solution.py:479
  99.1 15.0 %collective-permute-start.27 = (bf16[256,1024]{1,0:T(8,128)(2,1)S(1)}, bf16[256,1024]{1,0:T(8,128)(2,1)S(1)}, u32[]{:S(2)}, u32[]{:S(2)}) collective-permute-start(bf16[256,1024]{1,0:T(8,128)(2,1)S(1)} %get-tuple-element.193.refs_0_.refs_20_), channel_id=1, source_target_pairs={{0,8},{4,12},{8,0},{12,4},{16,24},{20,28},{24,16},{28,20},{1,9},{5... | collective-permute-start | bytes 1572872 | tf_op jit(solution)/shard_map/ppermute | solution.py:479
  125.7 18.9 %collective-permute-start.26 = (bf16[256,1024]{1,0:T(8,128)(2,1)S(1)}, bf16[256,1024]{1,0:T(8,128)(2,1)S(1)}, u32[]{:S(2)}, u32[]{:S(2)}) collective-permute-start(bf16[256,1024]{1,0:T(8,128)(2,1)S(1)} %get-tuple-element.195), channel_id=1, source_target_pairs={{0,4},{4,0},{8,12},{12,8},{16,20},{20,16},{24,28},{28,24},{1,5},{5... | collective-permute-start | bytes 1572872 | tf_op jit(solution)/shard_map/ppermute | solution.py:479
  129.7 14.9 %collective-permute-start.32 = (bf16[128,1024]{1,0:T(8,128)(2,1)S(1)}, bf16[128,1024]{1,0:T(8,128)(2,1)S(1)}, u32[]{:S(2)}, u32[]{:S(2)}) collective-permute-start(bf16[128,1024]{1,0:T(8,128)(2,1)S(1)} %slice.239), channel_id=1, source_target_pairs={{0,8},{4,12},{8,0},{12,4},{16,24},{20,28},{24,16},{28,20},{1,9},{5... | collective-permute-start | bytes 786440 | tf_op jit(solution)/shard_map/ppermute | solution.py:479
  130.6 12.2 %collective-permute-start.39 = (bf16[128,1024]{1,0:T(8,128)(2,1)S(1)}, bf16[128,1024]{1,0:T(8,128)(2,1)S(1)}, u32[]{:S(2)}, u32[]{:S(2)}) collective-permute-start(bf16[128,1024]{1,0:T(8,128)(2,1)S(1)} %add_convert_fusion.8), channel_id=1, source_target_pairs={{0,8},{4,12},{8,0},{12,4},{16,24},{20,28},{24,16},{28,20},{1,9},{5... | collective-permute-start | bytes 786440 | tf_op jit(solution)/shard_map/ppermute | solution.py:479
  131.5 12.7 %collective-permute-start.42 = (bf16[128,1024]{1,0:T(8,128)(2,1)S(1)}, bf16[128,1024]{1,0:T(8,128)(2,1)S(1)}, u32[]{:S(2)}, u32[]{:S(2)}) collective-permute-start(bf16[128,1024]{1,0:T(8,128)(2,1)S(1)} %add_convert_fusion.7), channel_id=1, source_target_pairs={{0,16},{4,20},{8,24},{12,28},{16,0},{20,4},{24,8},{28,12},{1,17},{... | collective-permute-start | bytes 786440 | tf_op jit(solution)/shard_map/ppermute | solution.py:479
  133.0 11.6 %collective-permute-start.44 = (bf16[128,1024]{1,0:T(8,128)(2,1)S(1)}, bf16[128,1024]{1,0:T(8,128)(2,1)S(1)}, u32[]{:S(2)}, u32[]{:S(2)}) collective-permute-start(bf16[128,1024]{1,0:T(8,128)(2,1)S(1)} %slice.238), channel_id=1, source_target_pairs={{0,16},{4,20},{8,24},{12,28},{16,0},{20,4},{24,8},{28,12},{1,17},{... | collective-permute-start | bytes 786440 | tf_op jit(solution)/shard_map/ppermute | solution.py:479
  155.8 13.6 %collective-permute-start.48 = (bf16[256,1024]{1,0:T(8,128)(2,1)S(1)}, bf16[256,1024]{1,0:T(8,128)(2,1)S(1)}, u32[]{:S(2)}, u32[]{:S(2)}) collective-permute-start(bf16[256,1024]{1,0:T(8,128)(2,1)S(1)} %get-tuple-element.224.refs_0_.refs_10_), channel_id=1, source_target_pairs={{0,16},{4,20},{8,24},{12,28},{16,0},{20,4},{24,8},{28,12},{1,17},{... | collective-permute-start | bytes 1572872 | tf_op jit(solution)/shard_map/ppermute | solution.py:479
  156.0 13.3 %collective-permute-start.47 = (bf16[256,1024]{1,0:T(8,128)(2,1)S(1)}, bf16[256,1024]{1,0:T(8,128)(2,1)S(1)}, u32[]{:S(2)}, u32[]{:S(2)}) collective-permute-start(bf16[256,1024]{1,0:T(8,128)(2,1)S(1)} %get-tuple-element.224.refs_0_.refs_10_), channel_id=1, source_target_pairs={{0,8},{4,12},{8,0},{12,4},{16,24},{20,28},{24,16},{28,20},{1,9},{5... | collective-permute-start | bytes 1572872 | tf_op jit(solution)/shard_map/ppermute | solution.py:479
  180.0 34.2 %collective-permute-start.46 = (bf16[256,1024]{1,0:T(8,128)(2,1)S(1)}, bf16[256,1024]{1,0:T(8,128)(2,1)S(1)}, u32[]{:S(2)}, u32[]{:S(2)}) collective-permute-start(bf16[256,1024]{1,0:T(8,128)(2,1)S(1)} %get-tuple-element.226), channel_id=1, source_target_pairs={{0,4},{4,0},{8,12},{12,8},{16,20},{20,16},{24,28},{28,24},{1,5},{5... | collective-permute-start | bytes 1572872 | tf_op jit(solution)/shard_map/ppermute | solution.py:479
  185.7 28.9 %collective-permute-start.52 = (bf16[128,1024]{1,0:T(8,128)(2,1)}, bf16[128,1024]{1,0:T(8,128)(2,1)S(1)}, u32[]{:S(2)}, u32[]{:S(2)}) collective-permute-start(bf16[128,1024]{1,0:T(8,128)(2,1)} %slice.237), channel_id=1, source_target_pairs={{0,8},{4,12},{8,0},{12,4},{16,24},{20,28},{24,16},{28,20},{1,9},{5... | collective-permute-start | bytes 786440 | tf_op jit(solution)/shard_map/ppermute | solution.py:479
  186.9 12.1 %collective-permute-start.59 = (bf16[128,1024]{1,0:T(8,128)(2,1)S(1)}, bf16[128,1024]{1,0:T(8,128)(2,1)S(1)}, u32[]{:S(2)}, u32[]{:S(2)}) collective-permute-start(bf16[128,1024]{1,0:T(8,128)(2,1)S(1)} %add_convert_fusion.6), channel_id=1, source_target_pairs={{0,8},{4,12},{8,0},{12,4},{16,24},{20,28},{24,16},{28,20},{1,9},{5... | collective-permute-start | bytes 786440 | tf_op jit(solution)/shard_map/ppermute | solution.py:479
  187.4 11.6 %collective-permute-start.62 = (bf16[128,1024]{1,0:T(8,128)(2,1)S(1)}, bf16[128,1024]{1,0:T(8,128)(2,1)S(1)}, u32[]{:S(2)}, u32[]{:S(2)}) collective-permute-start(bf16[128,1024]{1,0:T(8,128)(2,1)S(1)} %add_convert_fusion.5), channel_id=1, source_target_pairs={{0,16},{4,20},{8,24},{12,28},{16,0},{20,4},{24,8},{28,12},{1,17},{... | collective-permute-start | bytes 786440 | tf_op jit(solution)/shard_map/ppermute | solution.py:479
  188.9 27.3 %collective-permute-start.64 = (bf16[128,1024]{1,0:T(8,128)(2,1)S(1)}, bf16[128,1024]{1,0:T(8,128)(2,1)S(1)}, u32[]{:S(2)}, u32[]{:S(2)}) collective-permute-start(bf16[128,1024]{1,0:T(8,128)(2,1)S(1)} %slice.236), channel_id=1, source_target_pairs={{0,16},{4,20},{8,24},{12,28},{16,0},{20,4},{24,8},{28,12},{1,17},{... | collective-permute-start | bytes 786440 | tf_op jit(solution)/shard_map/ppermute | solution.py:479
  199.8 17.1 %collective-permute-start.63 = (bf16[128,1024]{1,0:T(8,128)(2,1)}, bf16[128,1024]{1,0:T(8,128)(2,1)S(1)}, u32[]{:S(2)}, u32[]{:S(2)}) collective-permute-start(bf16[128,1024]{1,0:T(8,128)(2,1)} %fusion.2), channel_id=1, source_target_pairs={{0,8},{4,12},{8,0},{12,4},{16,24},{20,28},{24,16},{28,20},{1,9},{5... | collective-permute-start | bytes 786440 | tf_op jit(solution)/shard_map/ppermute | solution.py:479
  201.7 15.2 %collective-permute-start.60 = (bf16[128,1024]{1,0:T(8,128)(2,1)}, bf16[128,1024]{1,0:T(8,128)(2,1)S(1)}, u32[]{:S(2)}, u32[]{:S(2)}) collective-permute-start(bf16[128,1024]{1,0:T(8,128)(2,1)} %fusion.3), channel_id=1, source_target_pairs={{0,16},{4,20},{8,24},{12,28},{16,0},{20,4},{24,8},{28,12},{1,17},{... | collective-permute-start | bytes 786440 | tf_op jit(solution)/shard_map/ppermute | solution.py:479
  214.1 152.8 %all-gather.9.cloned.1.call-start = ((), (), s32[]{:S(2)}) async-start(), calls=%async_computation.4 | async-start | bytes 4718592 | tf_op jit(solution)/shard_map/all_gather | solution.py:771
  214.2 57.5 %collective-permute-start.101 = (bf16[128,1024]{1,0:T(8,128)(2,1)}, bf16[128,1024]{1,0:T(8,128)(2,1)S(1)}, u32[]{:S(2)}, u32[]{:S(2)}) collective-permute-start(bf16[128,1024]{1,0:T(8,128)(2,1)} %get-tuple-element.320), channel_id=1, source_target_pairs={{0,1},{1,0},{2,3},{3,2},{4,5},{5,4},{6,7},{7,6},{8,9},{9,8},{10,11... | collective-permute-start | bytes 786440 | tf_op jit(solution)/shard_map/ppermute | solution.py:483
  214.6 57.2 %collective-permute-start.102 = (bf16[128,1024]{1,0:T(8,128)(2,1)}, bf16[128,1024]{1,0:T(8,128)(2,1)S(1)}, u32[]{:S(2)}, u32[]{:S(2)}) collective-permute-start(bf16[128,1024]{1,0:T(8,128)(2,1)} %get-tuple-element.321), channel_id=1, source_target_pairs={{0,2},{1,3},{2,0},{3,1},{4,6},{5,7},{6,4},{7,5},{8,10},{9,11},{10,... | collective-permute-start | bytes 786440 | tf_op jit(solution)/shard_map/ppermute | solution.py:483
  216.2 55.5 %collective-permute-start.103 = (bf16[128,1024]{1,0:T(8,128)(2,1)}, bf16[128,1024]{1,0:T(8,128)(2,1)S(1)}, u32[]{:S(2)}, u32[]{:S(2)}) collective-permute-start(bf16[128,1024]{1,0:T(8,128)(2,1)} %get-tuple-element.322), channel_id=1, source_target_pairs={{0,3},{1,2},{2,1},{3,0},{4,7},{5,6},{6,5},{7,4},{8,11},{9,10},{10,... | collective-permute-start | bytes 786440 | tf_op jit(solution)/shard_map/ppermute | solution.py:483
  283.1 17.2 %collective-permute-start.87 = (bf16[256,1024]{1,0:T(8,128)(2,1)S(1)}, bf16[256,1024]{1,0:T(8,128)(2,1)S(1)}, u32[]{:S(2)}, u32[]{:S(2)}) collective-permute-start(bf16[256,1024]{1,0:T(8,128)(2,1)S(1)} %slice.203), channel_id=1, source_target_pairs={{0,8},{4,12},{8,0},{12,4},{16,24},{20,28},{24,16},{28,20},{1,9},{5... | collective-permute-start | bytes 1572872 | tf_op jit(solution)/shard_map/ppermute | solution.py:479
  287.6 19.0 %collective-permute-start.79 = (bf16[128,1024]{1,0:T(8,128)(2,1)}, bf16[128,1024]{1,0:T(8,128)(2,1)}, u32[]{:S(2)}, u32[]{:S(2)}) collective-permute-start(bf16[128,1024]{1,0:T(8,128)(2,1)} %get-tuple-element.337), channel_id=1, source_target_pairs={{0,4},{4,0},{8,12},{12,8},{16,20},{20,16},{24,28},{28,24},{1,5},{5... | collective-permute-start | bytes 786440 | tf_op jit(solution)/shard_map/ppermute | solution.py:479
  288.1 18.8 %collective-permute-start.76 = (bf16[128,1024]{1,0:T(8,128)(2,1)}, bf16[128,1024]{1,0:T(8,128)(2,1)}, u32[]{:S(2)}, u32[]{:S(2)}) collective-permute-start(bf16[128,1024]{1,0:T(8,128)(2,1)} %get-tuple-element.338), channel_id=1, source_target_pairs={{0,4},{4,0},{8,12},{12,8},{16,20},{20,16},{24,28},{28,24},{1,5},{5... | collective-permute-start | bytes 786440 | tf_op jit(solution)/shard_map/ppermute | solution.py:479
  302.9 13.8 %collective-permute-start.88 = (bf16[128,1024]{1,0:T(8,128)(2,1)}, bf16[128,1024]{1,0:T(8,128)(2,1)S(1)}, u32[]{:S(2)}, u32[]{:S(2)}) collective-permute-start(bf16[128,1024]{1,0:T(8,128)(2,1)} %slice.205), channel_id=1, source_target_pairs={{0,16},{4,20},{8,24},{12,28},{16,0},{20,4},{24,8},{28,12},{1,17},{... | collective-permute-start | bytes 786440 | tf_op jit(solution)/shard_map/ppermute | solution.py:479
  304.2 15.1 %collective-permute-start.83 = (bf16[272,384]{1,0:T(8,128)(2,1)}, bf16[272,384]{1,0:T(8,128)(2,1)S(1)}, u32[]{:S(2)}, u32[]{:S(2)}) collective-permute-start(bf16[272,384]{1,0:T(8,128)(2,1)} %get-tuple-element.293), channel_id=1, source_target_pairs={{0,1},{1,0},{2,3},{3,2},{4,5},{5,4},{6,7},{7,6},{8,9},{9,8},{10,11... | collective-permute-start | bytes 626696 | tf_op jit(solution)/shard_map/ppermute | solution.py:483
  304.5 16.1 %collective-permute-start.84 = (bf16[272,384]{1,0:T(8,128)(2,1)}, bf16[272,384]{1,0:T(8,128)(2,1)S(1)}, u32[]{:S(2)}, u32[]{:S(2)}) collective-permute-start(bf16[272,384]{1,0:T(8,128)(2,1)} %get-tuple-element.294), channel_id=1, source_target_pairs={{0,2},{1,3},{2,0},{3,1},{4,6},{5,7},{6,4},{7,5},{8,10},{9,11},{10,... | collective-permute-start | bytes 626696 | tf_op jit(solution)/shard_map/ppermute | solution.py:483
  306.6 20.1 %collective-permute-start.85 = (bf16[272,384]{1,0:T(8,128)(2,1)}, bf16[272,384]{1,0:T(8,128)(2,1)S(1)}, u32[]{:S(2)}, u32[]{:S(2)}) collective-permute-start(bf16[272,384]{1,0:T(8,128)(2,1)} %get-tuple-element.295), channel_id=1, source_target_pairs={{0,3},{1,2},{2,1},{3,0},{4,7},{5,6},{6,5},{7,4},{8,11},{9,10},{10,... | collective-permute-start | bytes 626696 | tf_op jit(solution)/shard_map/ppermute | solution.py:483
  306.9 14.8 %collective-permute-start.73 = (bf16[256,1024]{1,0:T(8,128)(2,1)S(1)}, bf16[256,1024]{1,0:T(8,128)(2,1)S(1)}, u32[]{:S(2)}, u32[]{:S(2)}) collective-permute-start(bf16[256,1024]{1,0:T(8,128)(2,1)S(1)} %get-tuple-element.301), channel_id=1, source_target_pairs={{0,4},{4,0},{8,12},{12,8},{16,20},{20,16},{24,28},{28,24},{1,5},{5... | collective-permute-start | bytes 1572872 | tf_op jit(solution)/shard_map/ppermute | solution.py:479
  316.8 16.2 %collective-permute-start.75 = (bf16[256,1024]{1,0:T(8,128)(2,1)S(1)}, bf16[256,1024]{1,0:T(8,128)(2,1)S(1)}, u32[]{:S(2)}, u32[]{:S(2)}) collective-permute-start(bf16[256,1024]{1,0:T(8,128)(2,1)S(1)} %get-tuple-element.303), channel_id=1, source_target_pairs={{0,4},{4,0},{8,12},{12,8},{16,20},{20,16},{24,28},{28,24},{1,5},{5... | collective-permute-start | bytes 1572872 | tf_op jit(solution)/shard_map/ppermute | solution.py:479
  319.3 11.6 %collective-permute-start.91 = (bf16[32,1024]{1,0:T(8,128)(2,1)S(1)}, bf16[32,1024]{1,0:T(8,128)(2,1)S(1)}, u32[]{:S(2)}, u32[]{:S(2)}) collective-permute-start(bf16[32,1024]{1,0:T(8,128)(2,1)S(1)} %get-tuple-element.347), channel_id=1, source_target_pairs={{0,3},{1,2},{2,1},{3,0},{4,7},{5,6},{6,5},{7,4},{8,11},{9,10},{10,... | collective-permute-start | bytes 196616 | tf_op jit(solution)/shard_map/ppermute | solution.py:483
  326.7 18.8 %collective-permute-start.72 = (bf16[256,1024]{1,0:T(8,128)(2,1)S(1)}, bf16[256,1024]{1,0:T(8,128)(2,1)S(1)}, u32[]{:S(2)}, u32[]{:S(2)}) collective-permute-start(bf16[256,1024]{1,0:T(8,128)(2,1)S(1)} %get-tuple-element.299), channel_id=1, source_target_pairs={{0,4},{4,0},{8,12},{12,8},{16,20},{20,16},{24,28},{28,24},{1,5},{5... | collective-permute-start | bytes 1572872 | tf_op jit(solution)/shard_map/ppermute | solution.py:479
  339.7 21.5 %collective-permute-start.81 = (bf16[128,1024]{1,0:T(8,128)(2,1)S(1)}, bf16[128,1024]{1,0:T(8,128)(2,1)S(1)}, u32[]{:S(2)}, u32[]{:S(2)}) collective-permute-start(bf16[128,1024]{1,0:T(8,128)(2,1)S(1)} %fusion), channel_id=1, source_target_pairs={{0,8},{4,12},{8,0},{12,4},{16,24},{20,28},{24,16},{28,20},{1,9},{5... | collective-permute-start | bytes 786440 | tf_op jit(solution)/shard_map/ppermute | solution.py:479
  343.9 17.8 %collective-permute-start.82 = (bf16[128,1024]{1,0:T(8,128)(2,1)S(1)}, bf16[128,1024]{1,0:T(8,128)(2,1)S(1)}, u32[]{:S(2)}, u32[]{:S(2)}) collective-permute-start(bf16[128,1024]{1,0:T(8,128)(2,1)S(1)} %slice.234), channel_id=1, source_target_pairs={{0,16},{4,20},{8,24},{12,28},{16,0},{20,4},{24,8},{28,12},{1,17},{... | collective-permute-start | bytes 786440 | tf_op jit(solution)/shard_map/ppermute | solution.py:479
  344.1 17.6 %collective-permute-start.78 = (bf16[128,1024]{1,0:T(8,128)(2,1)S(1)}, bf16[128,1024]{1,0:T(8,128)(2,1)S(1)}, u32[]{:S(2)}, u32[]{:S(2)}) collective-permute-start(bf16[128,1024]{1,0:T(8,128)(2,1)S(1)} %fusion.1), channel_id=1, source_target_pairs={{0,16},{4,20},{8,24},{12,28},{16,0},{20,4},{24,8},{28,12},{1,17},{... | collective-permute-start | bytes 786440 | tf_op jit(solution)/shard_map/ppermute | solution.py:479
  345.5 15.6 %collective-permute-start.98 = (bf16[544,128]{1,0:T(8,128)(2,1)S(1)}, bf16[544,128]{1,0:T(8,128)(2,1)S(1)}, u32[]{:S(2)}, u32[]{:S(2)}) collective-permute-start(bf16[544,128]{1,0:T(8,128)(2,1)S(1)} %slice.180), channel_id=1, source_target_pairs={{0,8},{4,12},{8,0},{12,4},{16,24},{20,28},{24,16},{28,20},{1,9},{5... | collective-permute-start | bytes 417800 | tf_op jit(solution)/shard_map/ppermute | solution.py:479
  (175 other events, 1111.5 us)
Sparse Core Ops, SparseCore 0:
  45.0 29.1 all-gather.4
  81.8 27.7 all-gather.6
  214.2 43.0 reduce-scatter.1
  273.9 46.4 all-gather.8

commit v3 on v2

--- a/solution.py
+++ b/solution.py
@@ -166,37 +166,56 @@
     low_ref[...] = out.astype(BF)
 
 
-def attend(q, qt, k, kt, v, rows, heads, size):
+def attend(q, qt, k, kt, v, rows, heads, size, low, high):
     length, wide = q.shape
-    part = pl.BlockSpec((rows, wide), lambda i: (i, 0))
+    part = pl.BlockSpec((rows, wide), lambda i: (i + low, 0))
     whole = pl.BlockSpec((length, wide), lambda i: (0, 0))
     tail = pl.BlockSpec((length, LANES), lambda i: (0, 0))
+    out = pl.BlockSpec((rows, wide), lambda i: (i, 0))
+    count = (high - low) * rows
     return pl.pallas_call(
         functools.partial(attend_kernel, heads, size),
-        grid=(length // rows,),
-        in_specs=[part, pl.BlockSpec((rows, LANES), lambda i: (i, 0)), whole, tail, whole],
-        out_specs=[part, part, pl.BlockSpec((8, rows), lambda i: (0, i))],
-        out_shape=[struct((length, wide), BF), struct((length, wide), F32), struct((8, length), F32)],
+        grid=(high - low,),
+        in_specs=[part, pl.BlockSpec((rows, LANES), lambda i: (i + low, 0)), whole, tail, whole],
+        out_specs=[out, out, pl.BlockSpec((8, rows), lambda i: (0, i))],
+        out_shape=[struct((count, wide), BF), struct((count, wide), F32), struct((8, count), F32)],
         compiler_params=params(8 * MIB + 20 * rows * length + 8 * bytes_of([q])),
-        cost_estimate=micros(18),
+        cost_estimate=micros(9),
         name="attend",
     )(q, qt, k, kt, v)
 
 
-def attend_back_kernel(
-    heads, size, scale, q_ref, qt_ref, k_ref, kt_ref, v_ref, mg_ref, o_ref, lse_ref, out_ref, kx, dk_acc, dv_acc
-):
+def attend_back_kernel(heads, size, scale, first, last, count, done, q_ref, qt_ref, k_ref, kt_ref, v_ref, o_ref, lse_ref, *refs):
+    mgs, refs = refs[:count], refs[count:]
+    prior = ()
+    if not first:
+        prior, refs = refs[:3], refs[3:]
+    if last:
+        out_ref, kx, mg_s, dk_acc, dv_acc = refs
+    else:
+        out_ref, dk_acc, dv_acc, kx, mg_s = refs
     step = pl.program_id(0)
     rows, wide = q_ref.shape
 
     @pl.when(step == 0)
     def _():
-        dk_acc[...] = jnp.zeros_like(dk_acc)
-        dv_acc[...] = jnp.zeros_like(dv_acc)
+        if first:
+            dk_acc[...] = jnp.zeros_like(dk_acc)
+            dv_acc[...] = jnp.zeros_like(dv_acc)
+        else:
+            out_ref[:done, :wide] = prior[0][...]
+            dk_acc[...] = prior[1][...]
+            dv_acc[...] = prior[2][...]
         kx[...] = k_ref[...].astype(F32).T.astype(BF)
 
+    for i in range(count):
+
+        @pl.when(step == i)
+        def _(i=i):
+            mg_s[...] = mgs[i][...]
+
     keys = jnp.concatenate([k_ref[...], kt_ref[...]], axis=1)
-    query, tail, mg = q_ref[...], qt_ref[...], mg_ref[...]
+    query, tail, mg = q_ref[...], qt_ref[...], mg_s[...]
     spread = mg.astype(F32) * o_ref[...]
     turned = []
     for h in range(heads):
@@ -212,36 +231,54 @@
         turned.append(dot(kx[h * size : (h + 1) * size, :], grads))
     if heads * size < wide:
         turned.append(jnp.zeros((wide - heads * size, rows), F32))
-    at = block_at(step, rows)
+    at = pl.ds(pl.multiple_of(done + step * rows, rows), rows) if last else block_at(step, rows)
     out_ref[at, :wide] = (jnp.concatenate(turned, axis=0).T * scale).astype(BF)
-
-    @pl.when(step == pl.num_programs(0) - 1)
-    def _():
-        out_ref[:, wide : 2 * wide] = dk_acc[...].astype(BF)
-        out_ref[:, 2 * wide :] = dv_acc[...].astype(BF)
-
-
-def attend_back(q, qt, k, kt, v, mg, o, lse, rows, heads, size, scale):
+    if last:
+
+        @pl.when(step == pl.num_programs(0) - 1)
+        def _():
+            out_ref[:, wide : 2 * wide] = dk_acc[...].astype(BF)
+            out_ref[:, 2 * wide :] = dv_acc[...].astype(BF)
+
+
+def attend_back(q, qt, k, kt, v, mgs, o, lse, rows, heads, size, scale, low, high, prior):
     length, wide = q.shape
-    part = pl.BlockSpec((rows, wide), lambda i: (i, 0))
-    whole = pl.BlockSpec((length, wide), lambda i: (0, 0))
-    tail = pl.BlockSpec((length, LANES), lambda i: (0, 0))
+    last = high * rows == length
+    fixed = lambda i: (0, 0)
+    whole = pl.BlockSpec((length, wide), fixed)
+    full = struct((length, wide), F32)
+    scratch = [pltpu.VMEM((wide, length), BF), pltpu.VMEM((rows, wide), BF)]
+    if last:
+        out_specs = pl.BlockSpec((length, 3 * wide), fixed)
+        out_shape = struct((length, 3 * wide), BF)
+        scratch += [pltpu.VMEM((length, wide), F32)] * 2
+    else:
+        count = (high - low) * rows
+        out_specs = [pl.BlockSpec((count, wide), fixed), whole, whole]
+        out_shape = [struct((count, wide), BF), full, full]
     return pl.pallas_call(
-        functools.partial(attend_back_kernel, heads, size, scale),
-        grid=(length // rows,),
+        functools.partial(
+            attend_back_kernel, heads, size, scale, prior is None, last, high - low, low * rows
+        ),
+        grid=(high - low,),
         in_specs=[
-            part, pl.BlockSpec((rows, LANES), lambda i: (i, 0)), whole, tail, whole, part, part,
+            pl.BlockSpec((rows, wide), lambda i: (i + low, 0)),
+            pl.BlockSpec((rows, LANES), lambda i: (i + low, 0)),
+            whole,
+            pl.BlockSpec((length, LANES), fixed),
+            whole,
+            pl.BlockSpec((rows, wide), lambda i: (i, 0)),
             pl.BlockSpec((8, rows), lambda i: (0, i)),
-        ],
-        out_specs=pl.BlockSpec((length, 3 * wide), lambda i: (0, 0)),
-        out_shape=struct((length, 3 * wide), BF),
-        scratch_shapes=[
-            pltpu.VMEM((wide, length), BF), pltpu.VMEM((length, wide), F32), pltpu.VMEM((length, wide), F32)
-        ],
+        ]
+        + [pl.BlockSpec((rows, wide), fixed)] * (high - low)
+        + ([] if prior is None else [pl.BlockSpec((low * rows, wide), fixed), whole, whole]),
+        out_specs=out_specs,
+        out_shape=out_shape,
+        scratch_shapes=scratch,
         compiler_params=params(60 * MIB),
-        cost_estimate=micros(27),
+        cost_estimate=micros(25),
         name="attend_back",
-    )(q, qt, k, kt, v, mg, o, lse)
+    )(q, qt, k, kt, v, o, lse, *mgs, *(prior or ()))
 
 
 def normalize(source):
@@ -274,41 +311,35 @@
 
 
 def first_norm_kernel(count, offs_ref, x_ref, wo_ref, vec_ref, *refs):
-    blocks, (hidden_ref, low_ref, normed_ref, root_ref) = refs[:count], refs[count:]
+    blocks, (low_ref, normed_ref, root_ref) = refs[:count], refs[count:]
     wide = wo_ref.shape[0] // count
     out = x_ref[...].astype(F32) + vec_ref[2:3, :]
     for r, block in enumerate(blocks):
         out = out + dot(block[...], wo_ref[block_at(offs_ref[r], wide), :])
     normed, root = normalize(out)
-    hidden = normed * vec_ref[3:4, :] + vec_ref[4:5, :]
-    hidden_ref[...] = hidden
-    low_ref[...] = hidden.astype(BF)
-    normed_ref[...] = normed
+    low_ref[...] = (normed * vec_ref[3:4, :] + vec_ref[4:5, :]).astype(BF)
+    normed_ref[...] = normed.astype(BF)
     root_ref[...] = root
 
 
 def second_norm_kernel(whole, halves, hidden_ref, vec_ref, cot_ref, *refs):
-    parts, (res_ref, resid_ref, low_ref, sums_ref) = refs[:-4], refs[-4:]
-    normed, root = normalize(hidden_ref[...] + collected(parts, whole, halves) + vec_ref[5:6, :])
+    parts, (res_ref, low_ref, sums_ref) = refs[:-3], refs[-3:]
+    normed, root = normalize(hidden_ref[...].astype(F32) + collected(parts, whole, halves) + vec_ref[5:6, :])
     gain = vec_ref[6:7, :]
     res_ref[...] = (normed * gain + vec_ref[7:8, :]).astype(BF)
     grad = cot_ref[...].astype(F32)
-    resid = norm_back(normed, root, grad, gain)
-    resid_ref[...] = resid
-    low = resid.astype(BF)
+    low = norm_back(normed, root, grad, gain).astype(BF)
     low_ref[...] = low
     column_sums(sums_ref, [low.astype(F32), grad * normed, grad])
 
 
 def first_back_kernel(count, whole, halves, offs_ref, resid_ref, normed_ref, root_ref, vec_ref, wo_ref, *refs):
     parts = refs[: whole + 2 * halves]
-    first_ref, low_ref, sums_ref, *outs = refs[whole + 2 * halves :]
+    low_ref, sums_ref, *outs = refs[whole + 2 * halves :]
     wide = wo_ref.shape[0] // count
-    grad = resid_ref[...] + collected(parts, whole, halves)
-    normed = normed_ref[...]
-    first = norm_back(normed, root_ref[...], grad, vec_ref[3:4, :])
-    first_ref[...] = first
-    low = first.astype(BF)
+    grad = resid_ref[...].astype(F32) + collected(parts, whole, halves)
+    normed = normed_ref[...].astype(F32)
+    low = norm_back(normed, root_ref[...], grad, vec_ref[3:4, :]).astype(BF)
     low_ref[...] = low
     for r in range(count):
         outs[r][...] = dot_nt(low, wo_ref[block_at(offs_ref[r], wide), :]).astype(BF)
@@ -317,7 +348,7 @@
 
 def input_kernel(whole, halves, first_ref, *refs):
     parts, out_ref = refs[:-1], refs[-1]
-    out_ref[...] = (first_ref[...] + collected(parts, whole, halves)).astype(BF)
+    out_ref[...] = (first_ref[...].astype(F32) + collected(parts, whole, halves)).astype(BF)
 
 
 def assemble_kernel(shards, strip, shard_ref, ids_ref, *refs):
@@ -356,35 +387,60 @@
     refs[-1][...] = total
 
 
-def products_kernel(count, shard_ref, *refs):
+def early_product_kernel(count, *refs):
     acts, grads, hidden, inner = [refs[i * count : (i + 1) * count] for i in range(4)]
-    *outs, out_ref, outer_acc, inner_acc = refs[4 * count :]
-    for p in range(count):
-        term = dot_tn(acts[p][...], grads[p][...])
-        if p == 0:
-            outer_acc[...] = term
-        else:
-            outer_acc[...] += term
-    for r, out in enumerate(outs):
-        out[...] = outer_acc[block_at(shard_ref[r], out.shape[0]), :].astype(BF)
-    for p in range(count):
-        term = dot_tn(hidden[p][...], inner[p][...])
-        if p == 0:
-            inner_acc[...] = term
-        else:
-            inner_acc[...] += term
-    out_ref[...] = inner_acc[...].astype(BF)
-
-
-def inner_outer_kernel(inner_ref, *refs):
-    parts, out_ref = refs[:-1], refs[-1]
-    total = add_up([r[...] for r in parts])
-    units = total.shape[0]
-    out_ref[:units, :] = total.astype(BF)
-    times = out_ref.shape[1] // inner_ref.shape[1]
-    rows = inner_ref.shape[0] // times
-    for i in range(times):
-        out_ref[units:, i * inner_ref.shape[1] : (i + 1) * inner_ref.shape[1]] = inner_ref[i * rows : (i + 1) * rows, :]
+    outer_ref, inner_ref = refs[4 * count :]
+    for left, right, out in ((acts, grads, outer_ref), (hidden, inner, inner_ref)):
+        for p in range(count):
+            term = dot_tn(left[p][...], right[p][...])
+            if p == 0:
+                out[...] = term
+            else:
+                out[...] += term
+
+
+def late_product_kernel(count, given, shards, *refs):
+    sources, refs = refs[: 4 * count + given], refs[4 * count + given :]
+    out_ref, buffers, (outer_acc, inner_acc, sems) = refs[0], refs[1 : 4 * count + 1], refs[4 * count + 1 :]
+    targets = [*buffers, outer_acc, inner_acc]
+    copies = [pltpu.make_async_copy(a, b, sems.at[i]) for i, (a, b) in enumerate(zip(sources, targets))]
+    order = [4 * count + i for i in range(given)]
+    order += [i + g * count for g in (0, 2) for p in range(count) for i in (p, count + p)]
+    for i in order:
+        copies[i].start()
+    units = outer_acc.shape[0] // shards
+    height = out_ref.shape[0] // shards
+    depth, share = inner_acc.shape[0] // shards, inner_acc.shape[1]
+    for g, acc in ((0, outer_acc), (2, inner_acc)):
+        if given:
+            copies[4 * count + g // 2].wait()
+        for p in range(count):
+            left, right = g * count + p, (g + 1) * count + p
+            copies[left].wait()
+            copies[right].wait()
+            term = dot_tn(buffers[left][...], buffers[right][...])
+            if not given and p == 0:
+                acc[...] = term
+            else:
+                acc[...] += term
+    rows = height - units
+    for s in range(shards):
+        out_ref[s * height : s * height + units, :] = outer_acc[s * units : (s + 1) * units, :].astype(BF)
+        for i in range(depth // rows):
+            out_ref[s * height + units : (s + 1) * height, i * share : (i + 1) * share] = inner_acc[
+                s * depth + i * rows : s * depth + (i + 1) * rows, :
+            ].astype(BF)
+
+
+def weights_kernel(units, all_ref, inner_ref, outer_ref):
+    shards, height, width = all_ref.shape
+    rows = height - units
+    share = inner_ref.shape[1]
+    for s in range(shards):
+        outer_ref[s * units : (s + 1) * units, :] = all_ref[s, :units, :]
+        for i in range(width // share):
+            row = (s * (width // share) + i) * rows
+            inner_ref[row : row + rows, :] = all_ref[s, units:, i * share : (i + 1) * share]
 
 
 def finish_forward_kernel(units, all_ref, outer_ref, inner_ref):
@@ -402,28 +458,16 @@
                 ].astype(F32)
 
 
-def last_sum_kernel(count, *refs):
-    packs, wos, out_ref = refs[:count], refs[count : 2 * count], refs[-1]
-    total = add_up([r[...] for r in packs]).astype(BF)
-    height = total.shape[0]
-    for i in range(total.shape[1] // LANES):
-        out_ref[i * height : (i + 1) * height, :] = total[:, i * LANES : (i + 1) * LANES]
-    total = add_up([r[...] for r in wos]).astype(BF)
-    base = total.shape[1] // LANES
-    strip = total.shape[0]
-    for i in range(base):
-        row = height * 3 + i * strip
-        out_ref[row : row + strip, :] = total[:, i * LANES : (i + 1) * LANES]
-
-
-def into_kernel(factor, triple_ref, w_ref, *outs):
-    rows = outs[0].shape[0]
-    for r, out in enumerate(outs):
+def into_kernel(factor, order, triple_ref, w_ref, *outs):
+    rows = triple_ref.shape[0] // len(order)
+    per = len(order) // len(outs)
+    for i, r in enumerate(order):
         term = dot_nt(triple_ref[r * rows : (r + 1) * rows, :], w_ref[...])
-        out[...] = (term if factor == 1.0 else term * factor).astype(BF)
-
-
-def qkv_product_kernel(count, shard_ref, triple_ref, one_ref, two_ref, inner_ref, *refs):
+        at = i % per * rows
+        outs[i // per][at : at + rows, :] = (term if factor == 1.0 else term * factor).astype(BF)
+
+
+def qkv_product_kernel(count, shard_ref, triple_ref, one_ref, two_ref, inner_ref, wo_ref, *refs):
     pieces, outs, (acc, bias) = refs[:count], refs[count:-2], refs[-2:]
     row = 0
     bias[...] = jnp.zeros_like(bias)
@@ -438,18 +482,37 @@
         row += rows
     depth = acc.shape[0] // len(outs)
     units = inner_ref.shape[1]
+    strip = wo_ref.shape[0] // len(outs)
+    height = depth + EXTRA
     for r, out in enumerate(outs):
         at = shard_ref[r]
-        out[:depth, :] = acc[block_at(at, depth), :].astype(BF)
         for i in range(3):
             bias[1 + i : 2 + i, :depth] = one_ref[i : i + 1, block_at(at, depth)]
             bias[4 + i : 5 + i, :depth] = two_ref[i : i + 1, block_at(at, depth)]
         bias[7:8, 2 * LANES : 2 * LANES + units] = inner_ref[pl.ds(at, 1), :]
-        out[depth:, :] = bias[...].astype(BF)
+        for i in range(3):
+            lanes = slice(i * LANES, (i + 1) * LANES)
+            out[i * height : i * height + depth, :] = acc[block_at(at, depth), lanes].astype(BF)
+            out[i * height + depth : (i + 1) * height, :] = bias[:, lanes].astype(BF)
+        for i in range(wo_ref.shape[1] // LANES):
+            row = 3 * height + i * strip
+            out[row : row + strip, :] = wo_ref[block_at(at, strip), i * LANES : (i + 1) * LANES]
+
+
+def sum_kernel(*refs):
+    refs[-1][...] = add_up([r[...] for r in refs[:-1]]).astype(BF)
+
+
+def fold_kernel(keep_ref, other_ref, own_ref, *outs):
+    total = keep_ref[...].astype(F32) + other_ref[...].astype(F32)
+    rows = own_ref.shape[0]
+    own_ref[...] = total[:rows].astype(BF)
+    for i, out in enumerate(outs):
+        out[...] = total[rows + i * rows // 2 : rows + (i + 1) * rows // 2].astype(BF)
 
 
 def finish_kernel(shard_ref, offs_ref, *refs):
-    pieces, (q_ref, k_ref, v_ref, wo_ref, vec_ref, inner_ref, bias) = refs[:-7], refs[-7:]
+    pieces, (q_ref, k_ref, v_ref, wo_ref, inner_ref, *vecs, inner_all, bias) = refs[:-15], refs[-15:]
     depth = q_ref.shape[0]
     height = depth + EXTRA
     cols = LANES
@@ -462,7 +525,7 @@
         tails = [block[i * height + depth : (i + 1) * height, :].astype(F32) for i in range(3)]
         bias[0:8, lanes] = jnp.broadcast_to(tails[0][0:1, :], (8, cols))
         bias[8:16, lanes] = jnp.broadcast_to(tails[2][0:1, :], (8, cols))
-        inner_ref[:, lanes] = jnp.broadcast_to(tails[2][7:8, :], (8, cols))
+        inner_all[:, lanes] = jnp.broadcast_to(tails[2][7:8, :], (8, cols))
         tail = jnp.concatenate(tails, axis=1)
         total = tail if total is None else total + tail
         strip = (block.shape[0] - 3 * height) * LANES // wo_ref.shape[1]
@@ -470,9 +533,11 @@
             row = 3 * height + i * strip
             wo_ref[block_at(offs_ref[r], strip), i * LANES : (i + 1) * LANES] = block[row : row + strip, :].astype(F32)
     mine = block_at(shard_ref[0], depth)
-    vec_ref[0:1, :] = bias[0:1, mine]
-    vec_ref[1:2, :] = bias[8:9, mine]
-    vec_ref[2:8, :] = total[1:7, :depth]
+    vecs[0][...] = bias[0:1, mine]
+    vecs[1][...] = bias[8:9, mine]
+    for i in range(6):
+        vecs[2 + i][...] = total[1 + i : 2 + i, :depth]
+    inner_ref[...] = inner_all[0:1, :]
 
 
 def flip(source, bit):
@@ -508,22 +573,28 @@
         third = work(pieces[6:])
         return pieces, [[*a, *b, *c] for a, b, c in zip(first, second, third)]
 
-    def gather_slab(self, own, first, second):
-        pair = jnp.concatenate([own, after(flip(own, 2), first)], axis=0)
-        four = jnp.concatenate([pair, after(flip(pair, 4), second)], axis=0)
+    def gather_slab(self, own, beside):
+        others = after([flip(own, r) for r in (2, 4, 6)], beside)
+        four = jnp.concatenate([own, *others], axis=0)
         return [four, flip(four, 1)]
 
     slab_order = (0, 2, 4, 6, 1, 3, 5, 7)
 
-    def scatter_slab(self, keep, send):
-        def fold(half, other):
-            return half.astype(F32) + other.astype(F32)
-
-        four = fold(keep, flip(send, 1)).astype(BF)
-        half = four.shape[0] // 2
-        two = fold(four[:half], flip(four[half:], 2)).astype(BF)
-        half = half // 2
-        return fold(two[:half], flip(two[half:], 4)).astype(BF)
+    def scatter_whole(self, keep, send):
+        rows, width = keep.shape[0] // 4, keep.shape[1]
+        own, side_a, side_b, down_a, down_b, far_a, far_b = call(
+            fold_kernel, [], [keep, flip(send, 1)],
+            [struct((rows, width), BF)] + [struct((rows // 2, width), BF)] * 6, 3, "fold",
+        )
+        over_side, over_down = flip(far_a, 2), flip(far_b, 4)
+        side_a, down_b = flip(side_a, 2), flip(down_b, 4)
+        moved = self.fold(side_b, over_down), self.fold(down_a, over_side)
+        side_b, down_a = flip(moved[0], 2), flip(moved[1], 4)
+        return [own, side_a, down_a, side_b, down_b], 1, 2, moved
+
+    @staticmethod
+    def fold(half, other):
+        return (half.astype(F32) + other.astype(F32)).astype(BF)
 
     def places(self, rows):
         own = [self.at(r) * rows for r in range(8)]
@@ -545,12 +616,14 @@
         down = down.astype(F32) + flip(down1, 1).astype(F32)
         side_a = flip(side[:half].astype(BF), 2)
         down_b = flip(down[half:].astype(BF), 4)
-        side_b = flip((side[half:] + over_down.astype(F32)).astype(BF), 2)
-        down_a = flip((down[:half] + over_side.astype(F32)).astype(BF), 4)
-        return [own, flip(core, 1), side_a, down_a, side_b, down_b], 2, 2, (over_side, over_down)
-
-    def exchange(self, blocks):
-        return [blocks[0]] + [flip(blocks[r], r) for r in range(1, 8)]
+        side_b = (side[half:] + over_down.astype(F32)).astype(BF)
+        down_a = (down[:half] + over_side.astype(F32)).astype(BF)
+        return [own, flip(core, 1), side_a, flip(down_a, 4), flip(side_b, 2), down_b], 2, 2, (side_b, down_a)
+
+    parts = ((0, 4), (4, 8))
+
+    def exchange(self, blocks, low):
+        return [flip(block, low + i) if low + i else block for i, block in enumerate(blocks)]
 
 
 class Line:
@@ -574,7 +647,14 @@
         whole = jnp.concatenate(pieces, axis=0)
         return [lax.psum_scatter(whole, "ctx", scatter_dimension=0, tiled=True)], 1, 0, ()
 
-    def exchange(self, blocks):
+    @property
+    def parts(self):
+        return ((0, self.count),)
+
+    def scatter_whole(self, addends):
+        return [lax.psum_scatter(addends, "ctx", scatter_dimension=0, tiled=True)], 1, 0, ()
+
+    def exchange(self, blocks, low):
         return list(lax.all_to_all(jnp.stack(blocks), "ctx", 0, 0, tiled=False))
 
 
@@ -603,7 +683,6 @@
     strip = depth // count
     scale = size**-0.5
     shard_ids = jnp.stack([shard ^ r for r in range(shards)])
-    offs = jnp.stack([net.at(r) // copies for r in range(0, count, copies)])
     places = jnp.stack(net.places(rows))
 
     first_col = me // copies * cols
@@ -619,17 +698,24 @@
     vectors = [v.reshape(-1, LANES) for v in vectors]
     height = -(-sum(v.shape[0] for v in vectors) * LANES // (24 * wide)) * 8
     (pack,) = call(
-        pack_kernel, [lane[None]], [*weights, *vectors], [struct((depth + height, 3 * wide), BF)], 2, "pack"
+        pack_kernel, [lane[None]], [*weights, *vectors], [struct((depth + height, 3 * wide), BF)], 20, "pack", (), None,
     )
     packs = [pack] + [shard_flip(pack, r, shards) for r in range(1, shards)]
     vec, inner_all = call(
         functools.partial(unpack_kernel, shards), [shard_ids], packs,
         [struct((8, width), F32), struct((8 * shards, inner_bias.shape[0]), F32)], 2, "unpack",
     )
-    pieces = net.gather(x, early=[pack], late=[vec])
+    share = units * shards
+    times = width // share
+    inner_own = [
+        lax.dynamic_slice_in_dim(inner_weight, s * units * count + me * units, units, 1) for s in range(shards)
+    ]
+    inner_own = jnp.concatenate(inner_own, axis=1)
+    inner_own = jnp.concatenate([inner_own[i * depth // times : (i + 1) * depth // times] for i in range(times)], axis=1)
+    outer_own = lax.dynamic_slice_in_dim(outer_weight, me * units, units, 0)
+    forward_pack = jnp.concatenate([outer_own, inner_own], axis=0)
     wo_own = lax.dynamic_slice_in_dim(output_weight, me * strip, strip, 0)
-    wo_own = after(wo_own, pieces[6:8])
-    wo_parts = [wo_own] + [shard_flip(wo_own, r, shards) for r in range(1, shards)]
+    pieces = net.gather(x, early=[pack], late=[vec, forward_pack, wo_own])
     bias = jnp.pad(lax.dynamic_slice(vec, (0, first_col), (8, cols)), ((0, 0), (0, wide - cols)))
     inner_b = lax.dynamic_slice_in_dim(inner_all[::8], me * units, units, 1).reshape(1, -1)
 
@@ -650,18 +736,21 @@
         done += len(group)
     q, k, v, qt, kt = [made[0] if len(made) == 1 else jnp.concatenate(made) for made in zip(*qkv_rows)]
 
-    inner_own = jnp.concatenate(
-        [lax.dynamic_slice_in_dim(inner_weight, s * units * count + me * units, units, 1) for s in range(shards)],
-        axis=1,
-    )
-    outer_own = lax.dynamic_slice_in_dim(outer_weight, me * units, units, 0)
-    inner_own, outer_own = after((inner_own, outer_own), packs, pieces[6:8])
-    inner = lax.all_gather(inner_own, "wsh", axis=0, tiled=True)
-    outer = lax.all_gather(outer_own, "wsh", axis=0, tiled=True)
-    mixed_low, mixed, lse = attend(q, qt, k, kt, v, rows, heads, size)
+    wo_own = after(wo_own, q)
+    wo_parts = [wo_own] + [shard_flip(wo_own, r, shards) for r in range(1, shards)]
+
+    forward_pack = lax.all_gather(after(forward_pack, packs, pieces[6:8]), "wsh", axis=0, tiled=False)
+
+    attended, blocks = [], []
+    for low, high in net.parts:
+        made = attend(q, qt, k, kt, v, rows, heads, size, low, high)
+        attended.append(made)
+        blocks += net.exchange([made[0][i * rows : (i + 1) * rows, :cols] for i in range(high - low)], low)
+        q, k = (q, k) if high == count else after((q, k), made[0])
     if isinstance(net, Cube):
         ids = jnp.stack([net.at(r) for r in net.slab_order])
-        slabs = net.gather_slab(jnp.concatenate(wo_parts, axis=0), q, mixed_low)
+        slab = jnp.concatenate([wo_parts[0], *after(wo_parts[1:], attended[0][0])], axis=0)
+        slabs = net.gather_slab(slab, attended[1][0])
         (wo,) = call(
             functools.partial(assemble_kernel, shards, strip), [shard_ids, ids], slabs,
             [struct((width, width), BF)], 2, "assemble",
@@ -672,14 +761,18 @@
             wo_slab = lax.dynamic_update_slice(wo_slab, wo_parts[r][None], (shard ^ r, jnp.int32(0), jnp.int32(0)))
         wo = lax.all_gather(wo_slab, "ctx", axis=0, tiled=False)
         wo = wo.transpose(1, 0, 2, 3).reshape(width, width)
-
-    blocks = net.exchange([mixed_low[r * rows : (r + 1) * rows, :cols] for r in range(count)])[::copies]
+    blocks = blocks[::copies]
+    offs = jnp.stack([net.at(r) // copies for r in range(0, count, copies)])
     groups = len(blocks)
-    full, low_full, tall = struct((rows, width), F32), struct((rows, width), BF), struct((rows, 1), F32)
+    low_full, tall = struct((rows, width), BF), struct((rows, 1), F32)
     sums = struct((8, width), F32)
-    hidden, hidden_low, normed, root = call(
+    hidden_low, normed, root = call(
         functools.partial(first_norm_kernel, groups), [offs], [x, wo, vec, *blocks],
-        [full, low_full, full, tall], 5, "first_norm",
+        [low_full, low_full, tall], 5, "first_norm",
+    )
+    inner, outer = call(
+        functools.partial(weights_kernel, units), [], [forward_pack],
+        [struct((width, share), BF), struct((share, width), BF)], 2, "weights",
     )
 
     def forward(group):
@@ -694,9 +787,9 @@
 
     hidden_all, (acts, slopes, branch) = net.gather(hidden_low, forward)
     parts, n_whole, n_half, _ = net.scatter(branch)
-    result, resid, branch_grad, sums_two = call(
-        functools.partial(second_norm_kernel, n_whole, n_half), [], [hidden, vec, cotangent[0], *parts],
-        [low_full, full, low_full, sums], 4, "second_norm",
+    result, branch_grad, sums_two = call(
+        functools.partial(second_norm_kernel, n_whole, n_half), [], [hidden_low, vec, cotangent[0], *parts],
+        [low_full, low_full, sums], 4, "second_norm",
     )
 
     inner_sums, waiting = [], list(slopes)
@@ -713,31 +806,43 @@
             1.5 * sum(sizes) / 256, "backward",
         )
         inner_sums.append(made[-1])
-        return made[:n], made[n:-1]
-
-    grad_all, (inner_grads, hidden_grads) = net.gather(branch_grad, backward)
+        given = []
+        if isinstance(net, Cube) and len(inner_sums) == 1:
+            given = call(
+                functools.partial(early_product_kernel, n), [], [*acts[:n], *group, *hidden_all[:n], *made[:n]],
+                [struct((share, width), F32), struct((width, share), F32)], 4, "early_product",
+            )
+        return made[:n], made[n:-1], given
+
+    grad_all, (inner_grads, hidden_grads, given) = net.gather(branch_grad, backward)
     parts, n_whole, n_half, moved = net.scatter(hidden_grads)
-    *outer_parts, inner_wg = call(
-        functools.partial(products_kernel, len(acts)), [shard_ids],
-        [*after(acts, moved), *grad_all, *hidden_all, *inner_grads],
-        [struct((units, width), BF)] * shards + [struct((width, units * shards), BF)], 12, "products",
-        [pltpu.VMEM((units * shards, width), F32), pltpu.VMEM((width, units * shards), F32)], None,
-    )
-    parts = after(parts, inner_wg)
-    outer_parts = [outer_parts[0]] + [shard_flip(outer_parts[r], r, shards) for r in range(1, shards)]
-    inner_own_grad = lax.psum_scatter(inner_wg, "wsh", scatter_dimension=0, tiled=True)
-
-    first, attn_grad, sums_one, *mixed_grads = call(
+    skip = 2 if given else 0
+    terms = [*acts[skip:], *grad_all[skip:], *hidden_all[skip:], *inner_grads[skip:]]
+    height = units + depth * share // width
+    forward_wg = pl.pallas_call(
+        functools.partial(late_product_kernel, len(acts) - skip, len(given), shards),
+        in_specs=[pl.BlockSpec(memory_space=pl.ANY)] * (len(terms) + len(given)),
+        out_specs=IN_VMEM,
+        out_shape=struct((shards * height, width), BF),
+        scratch_shapes=[pltpu.VMEM(t.shape, BF) for t in terms]
+        + [pltpu.VMEM((share, width), F32), pltpu.VMEM((width, share), F32)]
+        + [pltpu.SemaphoreType.DMA((len(terms) + 2,))],
+        compiler_params=params(60 * MIB),
+        cost_estimate=micros(12),
+        name="late_product",
+    )(*after(terms, moved), *given)
+    parts = after(parts, forward_wg)
+    forward_own = lax.psum_scatter(forward_wg, "wsh", scatter_dimension=0, tiled=True)
+    attn_grad, sums_one, *mixed_grads = call(
         functools.partial(first_back_kernel, groups, n_whole, n_half), [offs],
-        [resid, normed, root, vec, wo, *parts],
-        [full, low_full, sums] + [struct((rows, cols), BF)] * groups, 5, "first_back",
+        [branch_grad, normed, root, vec, wo, *parts],
+        [low_full, sums] + [struct((rows, cols), BF)] * groups, 5, "first_back",
     )
     if copies > 1:
         mixed_grads = [b for b in mixed_grads for _ in range(copies)]
-    exchanged = net.exchange(mixed_grads)
-    mixed_grad = jnp.concatenate(exchanged, axis=0)
-    mixed_grad = jnp.pad(mixed_grad, ((0, 0), (0, wide - cols)))
-
+    exchanged = []
+    for low, high in net.parts:
+        exchanged += net.exchange(mixed_grads[low:high], low)
     order = [0, 4, 2, 6, 1, 5, 3, 7] if isinstance(net, Cube) else list(range(count))
     halves = 2 if isinstance(net, Cube) else 1
     ids = jnp.stack([net.at(r) for r in order])
@@ -758,70 +863,67 @@
         [struct((width // halves, width), BF)] * halves, 4, "mixed_product", [pltpu.VMEM((width, width), F32)],
     )
     if isinstance(net, Cube):
-        wo_grad = net.scatter_slab(*wo_grad)
+        folded = net.fold(wo_grad[0], flip(wo_grad[1], 1))
     else:
-        wo_grad = lax.psum_scatter(wo_grad[0], "ctx", scatter_dimension=0, tiled=True)
-    wo_parts = [lax.dynamic_slice_in_dim(wo_grad, (shard ^ r) * strip, strip, 0) for r in range(shards)]
-    wo_parts = [wo_parts[0]] + [shard_flip(wo_parts[r], r, shards) for r in range(1, shards)]
-    triple = attend_back(q, qt, k, kt, v, mixed_grad, mixed, lse, rows, heads, size, scale)
-    (forward_own,) = call(
-        inner_outer_kernel, [], [inner_own_grad, *after(outer_parts, triple)],
-        [struct((units + depth * units * shards // width, width), BF)], 2, "pack_forward",
-    )
-    forward_all = lax.all_gather(forward_own, "ctx", axis=0, tiled=False)
+        folded = lax.psum_scatter(wo_grad[0], "ctx", scatter_dimension=0, tiled=True)
+    prior = None
+    for (low, high), (_, o, lse) in zip(net.parts, attended):
+        mgs = [jnp.pad(b, ((0, 0), (0, wide - cols))) for b in exchanged[low:high]]
+        mgs = after(mgs, folded)
+        prior = attend_back(q, qt, k, kt, v, mgs, o, lse, rows, heads, size, scale, low, high, prior)
+        if isinstance(net, Cube):
+            half = folded.shape[0] // 2
+            sent = flip(folded[half:], 2 if low == 0 else 4)
+            folded = net.fold(folded[:half], after(sent, prior if high == count else prior[0]))
+    triple = after(prior, folded)
+    forward_all = lax.all_gather(after(forward_own, triple), "ctx", axis=0, tiled=False)
     inner_sum = add_up(inner_sums).reshape(shards, units)
-    qkv_pack = struct((depth + EXTRA, 3 * wide), BF)
+    last_pack = struct((3 * (depth + EXTRA) + strip * width // LANES, LANES), BF)
     packs = call(
         functools.partial(qkv_product_kernel, len(pieces)), [shard_ids],
-        [triple, sums_one, sums_two, inner_sum, *pieces], [qkv_pack] * shards, 5, "qkv_product",
+        [triple, sums_one, sums_two, inner_sum, folded, *pieces], [last_pack] * shards, 6, "qkv_product",
         [pltpu.VMEM((width, 3 * wide), F32), pltpu.VMEM((EXTRA, 3 * wide), F32)], None,
     )
+    order = [0, 2, 4, 6, 1, 3, 5, 7] if isinstance(net, Cube) else list(range(count))
     into = call(
-        functools.partial(into_kernel, 1.0 / copies), [], [after(triple, packs), qkv], [low_full] * count, 3, "into",
-    )
+        functools.partial(into_kernel, 1.0 / copies, order), [], [after(triple, packs), qkv],
+        [struct((length // halves, width), BF)] * halves, 4, "into",
+    )
+    parts, n_whole, n_half, moved = net.scatter_whole(*into)
+    (input_grad,) = call(
+        functools.partial(input_kernel, n_whole, n_half), [], [attn_grad, *parts], [low_full], 2, "input_sum"
+    )
+    packs = [packs[0]] + [shard_flip(packs[r], r, shards) for r in range(1, shards)]
+    (last_own,) = call(sum_kernel, [], after(packs, moved), [last_pack], 2, "last_sum")
     if isinstance(net, Cube):
-        half = rows // 2
-        into = [*into[:6]] + [into[6][:half], into[6][half:], into[7][:half], into[7][half:]]
-    parts, n_whole, n_half, _ = net.scatter(into)
-    (input_grad,) = call(
-        functools.partial(input_kernel, n_whole, n_half), [], [first, *parts], [low_full], 2, "input_sum"
-    )
-    packs = [packs[0]] + [shard_flip(packs[r], r, shards) for r in range(1, shards)]
-    if isinstance(net, Cube):
-        (last_own,) = call(
-            functools.partial(last_sum_kernel, shards), [], [*packs, *wo_parts],
-            [struct((3 * (depth + EXTRA) + strip * width // LANES, LANES), BF)], 2, "last_sum",
-        )
-        square = struct((depth, width), F32)
-        query_out, key_out, value_out, wo_out, vecs, inner_vec = call(
-            finish_kernel, [shard_ids, offs], net.gather(last_own),
-            [square, square, square, square, struct((8, depth), F32), struct((8, units * count), F32)], 4, "finish",
-            [pltpu.VMEM((16, width), F32)],
-        )
         outer_out, inner_out = call(
             functools.partial(finish_forward_kernel, units), [], [forward_all],
             [struct((units * count, width), F32), struct((depth, units * count * shards), F32)], 6, "finish_forward",
+            (), None,
         )
-        vecs = [vecs[i] for i in range(8)]
-        inner_vec = inner_vec[0]
+        last_all = net.gather(last_own, late=[outer_out])
+        square = struct((depth, width), F32)
+        query_out, key_out, value_out, wo_out, *vecs = call(
+            finish_kernel, [shard_ids, offs], last_all,
+            [square] * 4 + [struct((1, units * count), F32)] + [struct((1, depth), F32)] * 8, 4, "finish",
+            [pltpu.VMEM((8, units * count), F32), pltpu.VMEM((16, width), F32)], None,
+        )
+        inner_vec, *vecs = [v.reshape(-1) for v in vecs]
     else:
-
-        def everywhere(parts):
-            return lax.all_gather(add_up(parts).astype(BF), "ctx", axis=0, tiled=False).astype(F32)
-
-        wo_out = everywhere(wo_parts).reshape(depth, width)
-        gathered = everywhere(packs)
-        out3 = gathered[::copies, :depth].reshape(-1, depth, 3, wide)[..., :cols]
-        query_out, key_out, value_out = out3.transpose(2, 1, 0, 3).reshape(3, depth, width)
-        tail = gathered[:, depth:]
-        both = tail[::copies, 0].reshape(-1, 3, wide)[..., :cols].transpose(1, 0, 2).reshape(3, width)
+        last_all = jnp.stack(net.gather(last_own)).astype(F32)
+        triples = last_all[:, : 3 * (depth + EXTRA)].reshape(count, 3, depth + EXTRA, LANES)
+        wo_out = last_all[:, 3 * (depth + EXTRA) :].reshape(count, width // LANES, strip, LANES)
+        wo_out = wo_out.transpose(0, 2, 1, 3).reshape(depth, width)
+        out3 = triples[::copies, :, :depth, :cols].transpose(1, 2, 0, 3).reshape(3, depth, width)
+        query_out, key_out, value_out = out3[0], out3[1], out3[2]
+        both = triples[::copies, :, depth, :cols].transpose(1, 0, 2).reshape(3, width)
         both = lax.dynamic_slice_in_dim(both, shard * depth, depth, 1)
+        tail = triples[:, :, depth:].transpose(0, 2, 1, 3).reshape(count, EXTRA, 3 * LANES)
         six = jnp.sum(tail[:, 1:7, :depth], axis=0)
         vecs = [both[0], both[2]] + [six[i] for i in range(6)]
-        inner_vec = tail[:, 7, 2 * wide : 2 * wide + units].reshape(-1)
+        inner_vec = tail[:, 7, 2 * LANES : 2 * LANES + units].reshape(-1)
         forward_all = forward_all.astype(F32)
         outer_out = forward_all[:, :units].reshape(-1, width)
-        times = width // (units * shards)
         inner_out = forward_all[:, units:].reshape(count, depth // times, times, shards, units)
         inner_out = inner_out.transpose(2, 1, 3, 0, 4).reshape(depth, -1)
     return (

time: 387 us -> 357 us (0.922)
  local copies, waits for them, and re-layouts: 45.3 us -> 27 us
  starting transfers between devices: 94.4 us -> 83.4 us
  Pallas kernels: 103 us -> 113 us
  waiting for transfers between devices: 113 us -> 103 us
    ppermute x89 -> x86, waiting for transfers between devices: 98.4 us -> 80.3 us  [flip(): return lax.ppermute(source, 'ctx', [(i, i ^ bit) for i in range(8)])]
    ppermute x15 -> x9, waiting for transfers between devices: 5 us -> 23 us  [shard_flip(): return lax.ppermute(source, 'wsh', [(i, i ^ bit) for i in range(shards)])]
    pallas_call x2 -> x5, Pallas kernels: 41.9 us -> 56.7 us  [the longest x2 31.5 us: attend_back(): pl.pallas_call(functools.partial(attend_back_kernel, heads, size, scale,...]
    unnamed x241 -> x237, local copies, waits for them, and re-layouts: 35.7 us -> 23 us
    all_gather x3 -> x2, waiting for transfers between devices: 9.42 us -> 0.01 us  [the longest x1 0.01 us: local(): lax.all_gather(after(forward_pack, packs, pieces[6:8]), 'wsh', axis=0, ti...]
    ppermute x89 -> x86, starting transfers between devices: 78.1 us -> 72.2 us  [flip(): return lax.ppermute(source, 'ctx', [(i, i ^ bit) for i in range(8)])]
    pallas_call x22 -> x23, Pallas kernels: 61.1 us -> 56.2 us  [call(): pl.pallas_call(kernel, in_specs=[IN_SMEM] * len(scalars) + [IN_VMEM] * le...]
    ppermute x15 -> x9, starting transfers between devices: 15.9 us -> 11.1 us  [shard_flip(): return lax.ppermute(source, 'wsh', [(i, i ^ bit) for i in range(shards)])]
  transfers between devices with their start and end apart: 108 -> 98, of which waited for: 37 -> 47; matrix products, arithmetic and copies ran while one was open for 6% -> 3% of each run, Pallas kernels for 25% -> 28%
where the time goes in v3:
time: 357 us; the launch traced here: 349 us
  Pallas kernels  113 us (32%)
  waiting for transfers between devices  103 us (29%)
  starting transfers between devices  83.4 us (23%)
  local copies, waits for them, and re-layouts  27 us (8%)
  between operations  15.7 us (4%)
  other arithmetic  7.11 us (2%)
    ppermute x86, waiting for transfers between devices, flip(): return lax.ppermute(source, 'ctx', [(i, i ^ bit) for i in range(8)])  80.3 us
    ppermute x86, starting transfers between devices, flip(): return lax.ppermute(source, 'ctx', [(i, i ^ bit) for i in range(8)])  72.2 us
    pallas_call x23, Pallas kernels, call(): pl.pallas_call(kernel, in_specs=[IN_SMEM] * len(scalars) + [IN_VMEM] * le...  56.2 us
    pallas_call x2, Pallas kernels, attend_back(): pl.pallas_call(functools.partial(attend_back_kernel, heads, size, scale,...  31.5 us
    unnamed x237, local copies, waits for them, and re-layouts  23 us
    ppermute x9, waiting for transfers between devices, shard_flip(): return lax.ppermute(source, 'wsh', [(i, i ^ bit) for i in range(shards)])  23 us
    pallas_call x2, Pallas kernels, attend(): pl.pallas_call(functools.partial(attend_kernel, heads, size), grid=(high...  15.2 us
    ppermute x9, starting transfers between devices, shard_flip(): return lax.ppermute(source, 'wsh', [(i, i ^ bit) for i in range(shards)])  11.1 us
  transfers between devices with their start and end apart: 98, of which 47 were waited for; matrix products, arithmetic and copies ran while one was open for 3% of the time, Pallas kernels for 28%

profile of v3, /device:TPU:9, one launch (start us, length us, event | category | flops | bytes accessed | tf_op | source)
XLA Modules:
  0.0 349.5 jit_solution(13706425198036370983)
XLA Ops:
  7.3 2.3 pack.1.refs_0_.refs_10_
  17.3 1.8 maximum_maximum_fusion
  20.9 5.7 %collective-permute-done.1.refs_4_ = bf16[256,1024]{1,0:T(8,128)(2,1)S(1)} collective-permute-done((bf16[256,1024]{1,0:T(8,128)(2,1)}, bf16[256,1024]{1,0:T(8,128)(2,1)S(1)}, u32[]{:S(2)}, u32[]{:S(2)}) %collective-permute-start.1) | collective-permute-done | bytes 524320 | tf_op jit(solution)/shard_map/ppermute | solution.py:544
  33.4 3.7 %collective-permute-done.6.refs_7_ = bf16[128,1024]{1,0:T(8,128)(2,1)S(1)} collective-permute-done((bf16[128,1024]{1,0:T(8,128)(2,1)S(1)}, bf16[128,1024]{1,0:T(8,128)(2,1)S(1)}, u32[]{:S(2)}, u32[]{:S(2)}) %collective-permute-start.6) | collective-permute-done | bytes 262176 | tf_op jit(solution)/shard_map/ppermute | solution.py:544
  38.0 1.7 collective-permute-start.10
  42.6 4.8 %project.1 = (bf16[1024,384]{1,0:T(8,128)(2,1)S(1)}, bf16[2048,128]{1,0:T(8,128)(2,1)S(1)}, bf16[2048,128]{1,0:T(8,128)(2,1)S(1)}, bf16[2048,128]{1,0:T(8,128)(2...) custom-call(s32[4]{0:T(128)S(1)} %pad_add_fusion.shard_ref, s32[10]{0:T(128)S(1)} %stack.122.place_ref, ...), custom_call_target="tpu_custom_call" | custom-call | flops 4000000000 | tf_op jit(solution)/shard_map/project/pallas_call | solution.py:55
  48.3 2.5 collective-permute-start.14
  52.1 7.4 %attend.2 = (bf16[1024,128]{1,0:T(8,128)(2,1)S(1)}, f32[1024,128]{1,0:T(8,128)S(1)}, f32[8,1024]{1,0:T(8,128)S(1)}) custom-call(bf16[2048,128]{1,0:T(8,128)(2,1)S(1)} %get-tuple-element.238.q_ref, bf16[2048,128]{1,0:T(8,128)(2,1)S(1)} %get-tuple-element.230.qt_ref, bf16[2048,128]{1,0:T(8,128)(2,1)S(1)} %get-tuple-element.239.k_ref, ...), custom_call_target="tpu_custom_call" | custom-call | flops 8999999488 | tf_op jit(solution)/shard_map/attend/pallas_call | solution.py:176
  59.5 3.7 %collective-permute-done.13 = bf16[32,1024]{1,0:T(8,128)(2,1)S(1)} collective-permute-done((bf16[32,1024]{1,0:T(8,128)(2,1)S(1)}, bf16[32,1024]{1,0:T(8,128)(2,1)S(1)}, u32[]{:S(2)}, u32[]{:S(2)}) %collective-permute-start.13) | collective-permute-done | bytes 65568 | tf_op jit(solution)/shard_map/ppermute | solution.py:548
  66.0 7.8 %attend.3 = (bf16[1024,128]{1,0:T(8,128)(2,1)S(1)}, f32[1024,128]{1,0:T(8,128)S(1)}, f32[8,1024]{1,0:T(8,128)S(1)}) custom-call(bf16[2048,128]{1,0:T(8,128)(2,1)S(1)} %get-tuple-element.238.q_ref, bf16[2048,128]{1,0:T(8,128)(2,1)S(1)} %get-tuple-element.230.qt_ref, bf16[2048,128]{1,0:T(8,128)(2,1)S(1)} %get-tuple-element.239.k_ref, ...), custom_call_target="tpu_custom_call" | custom-call | flops 8999999488 | tf_op jit(solution)/shard_map/attend/pallas_call | solution.py:176
  73.9 2.6 collective-permute-done.16
  82.2 1.7 collective-permute-start.24
  90.1 2.6 first_norm.1
  98.3 1.7 forward.3
  100.1 8.1 %collective-permute-done.29.refs_2_.refs_18_ = bf16[256,1024]{1,0:T(8,128)(2,1)S(1)} collective-permute-done((bf16[256,1024]{1,0:T(8,128)(2,1)S(1)}, bf16[256,1024]{1,0:T(8,128)(2,1)S(1)}, u32[]{:S(2)}, u32[]{:S(2)}) %collective-permute-start.29) | collective-permute-done | bytes 524320 | tf_op jit(solution)/shard_map/ppermute | solution.py:544
  112.7 3.3 forward.4
  118.1 1.7 collective-permute-start.37
  121.3 2.1 forward.5
  128.2 9.3 %collective-permute-done.40 = bf16[128,1024]{1,0:T(8,128)(2,1)S(1)} collective-permute-done((bf16[128,1024]{1,0:T(8,128)(2,1)S(1)}, bf16[128,1024]{1,0:T(8,128)(2,1)S(1)}, u32[]{:S(2)}, u32[]{:S(2)}) %collective-permute-start.40) | collective-permute-done | bytes 262176 | tf_op jit(solution)/shard_map/ppermute | solution.py:544
  139.3 5.0 %collective-permute-done.41.refs_3_ = bf16[128,1024]{1,0:T(8,128)(2,1)S(1)} collective-permute-done((bf16[128,1024]{1,0:T(8,128)(2,1)S(1)}, bf16[128,1024]{1,0:T(8,128)(2,1)S(1)}, u32[]{:S(2)}, u32[]{:S(2)}) %collective-permute-start.41) | collective-permute-done | bytes 262176 | tf_op jit(solution)/shard_map/ppermute | solution.py:544
  145.1 1.8 second_norm.1
  146.9 2.4 collective-permute-start.46
  150.8 2.4 backward.3
  158.0 4.9 %collective-permute-done.49.refs_2_.refs_10_ = bf16[256,1024]{1,0:T(8,128)(2,1)S(1)} collective-permute-done((bf16[256,1024]{1,0:T(8,128)(2,1)S(1)}, bf16[256,1024]{1,0:T(8,128)(2,1)S(1)}, u32[]{:S(2)}, u32[]{:S(2)}) %collective-permute-start.49) | collective-permute-done | bytes 524320 | tf_op jit(solution)/shard_map/ppermute | solution.py:544
  166.4 2.7 backward.4
  169.9 1.7 collective-permute-done.56.refs_1_.refs_13_
  172.2 1.7 collective-permute-start.57
  175.4 3.0 backward.5
  186.3 4.3 %collective-permute-done.63 = bf16[128,1024]{1,0:T(8,128)(2,1)S(1)} collective-permute-done((bf16[128,1024]{1,0:T(8,128)(2,1)S(1)}, bf16[128,1024]{1,0:T(8,128)(2,1)S(1)}, u32[]{:S(2)}, u32[]{:S(2)}) %collective-permute-start.63) | collective-permute-done | bytes 262176 | tf_op jit(solution)/shard_map/ppermute | solution.py:544
  193.0 9.9 %late_product.1 = bf16[1024,1024]{1,0:T(8,128)(2,1)} custom-call(bf16[256,512]{1,0:T(8,128)(2,1)} %copy-done.88, bf16[256,512]{1,0:T(8,128)(2,1)} %copy-done.89, bf16[256,512]{1,0:T(8,128)(2,1)} %copy-done.90, bf16[256,512]{1,0:T(8,128)(2,1)} %copy-done.91, bf16[128,512]{1,0:T(8,128)(2,1)} %copy-done.80, bf16[128,512]{1,0:T(8,128)(2,1)} %copy-done.81, ...), custom_call_target="tpu_custom_call" | custom-call | flops 12000000000 | tf_op jit(solution)/shard_map/late_product/pallas_call | solution.py:822
  206.7 3.0 first_back.1
  212.9 2.6 collective-permute-start.70
  227.2 2.3 collective-permute-start.69
  230.6 15.3 %attend_back.2 = (bf16[1024,128]{1,0:T(8,128)(2,1)}, f32[2048,128]{1,0:T(8,128)}, f32[2048,128]{1,0:T(8,128)}) custom-call(bf16[2048,128]{1,0:T(8,128)(2,1)} %copy-done.69, bf16[2048,128]{1,0:T(8,128)(2,1)} %copy-done.72, bf16[2048,128]{1,0:T(8,128)(2,1)} %copy-done.70, bf16[2048,128]{1,0:T(8,128)(2,1)} %copy-done.73, bf16[2048,128]{1,0:T(8,128)(2,1)} %copy-done.71, ...), custom_call_target="tpu_custom_call" | custom-call | flops 24999999488 | tf_op jit(solution)/shard_map/attend_back/pallas_call | solution.py:259
  246.9 16.2 %attend_back.3.triple_ref = bf16[2048,384]{1,0:T(8,128)(2,1)} custom-call(bf16[2048,128]{1,0:T(8,128)(2,1)} %copy-done.69, bf16[2048,128]{1,0:T(8,128)(2,1)} %copy-done.72, bf16[2048,128]{1,0:T(8,128)(2,1)} %copy-done.70, bf16[2048,128]{1,0:T(8,128)(2,1)} %copy-done.73, bf16[2048,128]{1,0:T(8,128)(2,1)} %copy-done.71, f32[1024,128]{1,0:T(8,128)} %copy-done.95, ...), custom_call_target="tpu_custom_call" | custom-call | flops 24999999488 | tf_op jit(solution)/shard_map/attend_back/pallas_call | solution.py:259
  264.5 6.6 %qkv_product.1 = (bf16[1072,128]{1,0:T(8,128)(2,1)}, bf16[1072,128]{1,0:T(8,128)(2,1)}, bf16[1072,128]{1,0:T(8,128)(2,1)}, bf16[1072,128]{1,0:T(8,128)(2,1)}) custom-call(s32[4]{0:T(128)} %copy-done.8, bf16[2048,384]{1,0:T(8,128)(2,1)} %attend_back.3.triple_ref, f32[8,1024]{1,0:T(8,128)} %copy-done.98, f32[8,1024]{1,0:T(8,128)} %copy-done.97, ...), custom_call_target="tpu_custom_call" | custom-call | flops 6000000000 | tf_op jit(solution)/shard_map/qkv_product/pallas_call | solution.py:55
  271.2 2.4 into.1
  273.6 4.1 %collective-permute-done.76.other_ref = bf16[1024,1024]{1,0:T(8,128)(2,1)S(1)} collective-permute-done((bf16[1024,1024]{1,0:T(8,128)(2,1)S(1)}, bf16[1024,1024]{1,0:T(8,128)(2,1)S(1)}, u32[]{:S(2)}, u32[]{:S(2)}) %collective-permute-start.76) | collective-permute-done | bytes 2097184 | tf_op jit(solution)/shard_map/ppermute | solution.py:544
  280.2 2.5 collective-permute-start.83
  284.3 4.0 %collective-permute-done.78 = bf16[128,1024]{1,0:T(8,128)(2,1)S(1)} collective-permute-done((bf16[128,1024]{1,0:T(8,128)(2,1)S(1)}, bf16[128,1024]{1,0:T(8,128)(2,1)S(1)}, u32[]{:S(2)}, u32[]{:S(2)}) %collective-permute-start.78) | collective-permute-done | bytes 262176 | tf_op jit(solution)/shard_map/ppermute | solution.py:544
  288.5 4.6 %collective-permute-done.83.refs_1_ = bf16[1072,128]{1,0:T(8,128)(2,1)S(1)} collective-permute-done((bf16[1072,128]{1,0:T(8,128)(2,1)S(1)}, bf16[1072,128]{1,0:T(8,128)(2,1)S(1)}, u32[]{:S(2)}, u32[]{:S(2)}) %collective-permute-start.83) | collective-permute-done | bytes 274464 | tf_op jit(solution)/shard_map/ppermute | solution.py:548
  293.1 2.7 collective-permute-done.84.refs_2_
  295.8 12.0 %collective-permute-done.85.refs_3_ = bf16[1072,128]{1,0:T(8,128)(2,1)S(1)} collective-permute-done((bf16[1072,128]{1,0:T(8,128)(2,1)S(1)}, bf16[1072,128]{1,0:T(8,128)(2,1)S(1)}, u32[]{:S(2)}, u32[]{:S(2)}) %collective-permute-start.85) | collective-permute-done | bytes 274464 | tf_op jit(solution)/shard_map/ppermute | solution.py:548
  311.9 5.9 %collective-permute-done.87.refs_4_ = bf16[1072,128]{1,0:T(8,128)(2,1)S(1)} collective-permute-done((bf16[1072,128]{1,0:T(8,128)(2,1)S(1)}, bf16[1072,128]{1,0:T(8,128)(2,1)S(1)}, u32[]{:S(2)}, u32[]{:S(2)}) %collective-permute-start.87) | collective-permute-done | bytes 274464 | tf_op jit(solution)/shard_map/ppermute | solution.py:544
  321.3 2.5 collective-permute-done.77.refs_1_
  324.4 3.4 collective-permute-start.89
  328.9 6.4 %finish_forward.1 = (f32[1024,1024]{1,0:T(8,128)}, f32[256,4096]{1,0:T(8,128)}) custom-call(bf16[8,256,1024]{2,1,0:T(8,128)(2,1)} %bitcast.57), custom_call_target="tpu_custom_call" | custom-call | flops 6000000000 | tf_op jit(solution)/shard_map/finish_forward/pallas_call | solution.py:55
  338.6 3.9 %finish.1 = (f32[256,1024]{1,0:T(8,128)}, f32[256,1024]{1,0:T(8,128)}, f32[256,1024]{1,0:T(8,128)}, f32[256,1024]{1,0:T(8,128)}, f32[1,1024]{1,0:T(1,128)}, /*in...) custom-call(s32[4]{0:T(128)} %copy-done.8, ...), custom_call_target="tpu_custom_call" | custom-call | flops 4000000000 | tf_op jit(solution)/shard_map/finish/pallas_call | solution.py:55
  (466 shorter events, 118.9 us)
Async XLA Ops:
  7.2 89.4 %all-gather.5.cloned.1.call-start = ((), (), s32[]{:S(2)}) async-start(), calls=%async_computation.2 | async-start | bytes 2621440 | tf_op jit(solution)/shard_map/all_gather | solution.py:742
  9.6 19.5 %collective-permute-start.9 = (bf16[264,384]{1,0:T(8,128)(2,1)}, bf16[264,384]{1,0:T(8,128)(2,1)S(1)}, u32[]{:S(2)}, u32[]{:S(2)}) collective-permute-start(bf16[264,384]{1,0:T(8,128)(2,1)} %pack.1.refs_0_.refs_10_), channel_id=1, source_target_pairs={{0,3},{1,2},{2,1},{3,0},{4,7},{5,6},{6,5},{7,4},{8,11},{9,10},{10,... | collective-permute-start | bytes 608264 | tf_op jit(solution)/shard_map/ppermute | solution.py:548
  10.9 20.1 %collective-permute-start.8 = (bf16[264,384]{1,0:T(8,128)(2,1)}, bf16[264,384]{1,0:T(8,128)(2,1)}, u32[]{:S(2)}, u32[]{:S(2)}) collective-permute-start(bf16[264,384]{1,0:T(8,128)(2,1)} %pack.1.refs_0_.refs_10_), channel_id=1, source_target_pairs={{0,2},{1,3},{2,0},{3,1},{4,6},{5,7},{6,4},{7,5},{8,10},{9,11},{10,... | collective-permute-start | bytes 608264 | tf_op jit(solution)/shard_map/ppermute | solution.py:548
  12.8 13.8 %collective-permute-start.1 = (bf16[256,1024]{1,0:T(8,128)(2,1)}, bf16[256,1024]{1,0:T(8,128)(2,1)S(1)}, u32[]{:S(2)}, u32[]{:S(2)}) collective-permute-start(bf16[256,1024]{1,0:T(8,128)(2,1)} %bitcast.8.refs_0_.x_ref), channel_id=1, source_target_pairs={{0,16},{4,20},{8,24},{12,28},{16,0},{20,4},{24,8},{28,12},{1,17},{... | collective-permute-start | bytes 1572872 | tf_op jit(solution)/shard_map/ppermute | solution.py:544
  14.3 13.4 %collective-permute-start = (bf16[256,1024]{1,0:T(8,128)(2,1)}, bf16[256,1024]{1,0:T(8,128)(2,1)S(1)}, u32[]{:S(2)}, u32[]{:S(2)}) collective-permute-start(bf16[256,1024]{1,0:T(8,128)(2,1)} %bitcast.8.refs_0_.x_ref), channel_id=1, source_target_pairs={{0,8},{4,12},{8,0},{12,4},{16,24},{20,28},{24,16},{28,20},{1,9},{5... | collective-permute-start | bytes 1572872 | tf_op jit(solution)/shard_map/ppermute | solution.py:544
  19.1 12.2 %collective-permute-start.7 = (bf16[264,384]{1,0:T(8,128)(2,1)}, bf16[264,384]{1,0:T(8,128)(2,1)S(1)}, u32[]{:S(2)}, u32[]{:S(2)}) collective-permute-start(bf16[264,384]{1,0:T(8,128)(2,1)} %pack.1.refs_0_.refs_10_), channel_id=1, source_target_pairs={{0,1},{1,0},{2,3},{3,2},{4,5},{5,4},{6,7},{7,6},{8,9},{9,8},{10,11... | collective-permute-start | bytes 608264 | tf_op jit(solution)/shard_map/ppermute | solution.py:548
  27.8 13.6 %collective-permute-start.3 = (bf16[256,1024]{1,0:T(8,128)(2,1)S(1)}, bf16[256,1024]{1,0:T(8,128)(2,1)S(1)}, u32[]{:S(2)}, u32[]{:S(2)}) collective-permute-start(bf16[256,1024]{1,0:T(8,128)(2,1)S(1)} %collective-permute-done.refs_2_), channel_id=1, source_target_pairs={{0,4},{4,0},{8,12},{12,8},{16,20},{20,16},{24,28},{28,24},{1,5},{5... | collective-permute-start | bytes 1572872 | tf_op jit(solution)/shard_map/ppermute | solution.py:544
  29.0 12.4 %collective-permute-start.4 = (bf16[256,1024]{1,0:T(8,128)(2,1)S(1)}, bf16[256,1024]{1,0:T(8,128)(2,1)S(1)}, u32[]{:S(2)}, u32[]{:S(2)}) collective-permute-start(bf16[256,1024]{1,0:T(8,128)(2,1)S(1)} %collective-permute-done.1.refs_4_), channel_id=1, source_target_pairs={{0,4},{4,0},{8,12},{12,8},{16,20},{20,16},{24,28},{28,24},{1,5},{5... | collective-permute-start | bytes 1572872 | tf_op jit(solution)/shard_map/ppermute | solution.py:544
  39.8 224.1 %reduce-scatter.2.cloned.1.call-start = ((), (), s32[]{:S(2)}) async-start(), calls=%async_computation.1 | async-start | bytes 2621440 | tf_op jit(solution)/shard_map/reduce_scatter | solution.py:835
  48.3 11.2 %collective-permute-start.14 = (bf16[32,1024]{1,0:T(8,128)(2,1)S(1)}, bf16[32,1024]{1,0:T(8,128)(2,1)S(1)}, u32[]{:S(2)}, u32[]{:S(2)}) collective-permute-start(bf16[32,1024]{1,0:T(8,128)(2,1)S(1)} %constant_dynamic-slice_fusion.7), channel_id=1, source_target_pairs={{0,3},{1,2},{2,1},{3,0},{4,7},{5,6},{6,5},{7,4},{8,11},{9,10},{10,... | collective-permute-start | bytes 196616 | tf_op jit(solution)/shard_map/ppermute | solution.py:548
  50.8 12.4 %collective-permute-start.13 = (bf16[32,1024]{1,0:T(8,128)(2,1)S(1)}, bf16[32,1024]{1,0:T(8,128)(2,1)S(1)}, u32[]{:S(2)}, u32[]{:S(2)}) collective-permute-start(bf16[32,1024]{1,0:T(8,128)(2,1)S(1)} %constant_dynamic-slice_fusion.7), channel_id=1, source_target_pairs={{0,2},{1,3},{2,0},{3,1},{4,6},{5,7},{6,4},{7,5},{8,10},{9,11},{10,... | collective-permute-start | bytes 196616 | tf_op jit(solution)/shard_map/ppermute | solution.py:548
  51.4 11.8 %collective-permute-start.12 = (bf16[32,1024]{1,0:T(8,128)(2,1)S(1)}, bf16[32,1024]{1,0:T(8,128)(2,1)S(1)}, u32[]{:S(2)}, u32[]{:S(2)}) collective-permute-start(bf16[32,1024]{1,0:T(8,128)(2,1)S(1)} %constant_dynamic-slice_fusion.7), channel_id=1, source_target_pairs={{0,1},{1,0},{2,3},{3,2},{4,5},{5,4},{6,7},{7,6},{8,9},{9,8},{10,11... | collective-permute-start | bytes 196616 | tf_op jit(solution)/shard_map/ppermute | solution.py:548
  63.3 10.6 %collective-permute-start.17 = (bf16[128,1024]{1,0:T(8,128)(2,1)S(1)}, bf16[128,1024]{1,0:T(8,128)(2,1)S(1)}, u32[]{:S(2)}, u32[]{:S(2)}) collective-permute-start(bf16[128,1024]{1,0:T(8,128)(2,1)S(1)} %get-tuple-element.441), channel_id=1, source_target_pairs={{0,24},{4,28},{8,16},{12,20},{16,8},{20,12},{24,0},{28,4},{1,25},{... | collective-permute-start | bytes 786440 | tf_op jit(solution)/shard_map/ppermute | solution.py:544
  63.4 13.1 %collective-permute-start.16 = (bf16[128,1024]{1,0:T(8,128)(2,1)S(1)}, bf16[128,1024]{1,0:T(8,128)(2,1)S(1)}, u32[]{:S(2)}, u32[]{:S(2)}) collective-permute-start(bf16[128,1024]{1,0:T(8,128)(2,1)S(1)} %get-tuple-element.441), channel_id=1, source_target_pairs={{0,16},{4,20},{8,24},{12,28},{16,0},{20,4},{24,8},{28,12},{1,17},{... | collective-permute-start | bytes 786440 | tf_op jit(solution)/shard_map/ppermute | solution.py:544
  64.9 11.6 %collective-permute-start.15 = (bf16[128,1024]{1,0:T(8,128)(2,1)S(1)}, bf16[128,1024]{1,0:T(8,128)(2,1)S(1)}, u32[]{:S(2)}, u32[]{:S(2)}) collective-permute-start(bf16[128,1024]{1,0:T(8,128)(2,1)S(1)} %get-tuple-element.441), channel_id=1, source_target_pairs={{0,8},{4,12},{8,0},{12,4},{16,24},{20,28},{24,16},{28,20},{1,9},{5... | collective-permute-start | bytes 786440 | tf_op jit(solution)/shard_map/ppermute | solution.py:544
  94.7 13.5 %collective-permute-start.29 = (bf16[256,1024]{1,0:T(8,128)(2,1)S(1)}, bf16[256,1024]{1,0:T(8,128)(2,1)S(1)}, u32[]{:S(2)}, u32[]{:S(2)}) collective-permute-start(bf16[256,1024]{1,0:T(8,128)(2,1)S(1)} %get-tuple-element.244.refs_0_.hidden_ref.refs_4_), channel_id=1, source_target_pairs={{0,16},{4,20},{8,24},{12,28},{16,0},{20,4},{24,8},{28,12},{1,17},{... | collective-permute-start | bytes 1572872 | tf_op jit(solution)/shard_map/ppermute | solution.py:544
  96.1 13.1 %collective-permute-start.28 = (bf16[256,1024]{1,0:T(8,128)(2,1)S(1)}, bf16[256,1024]{1,0:T(8,128)(2,1)S(1)}, u32[]{:S(2)}, u32[]{:S(2)}) collective-permute-start(bf16[256,1024]{1,0:T(8,128)(2,1)S(1)} %get-tuple-element.244.refs_0_.hidden_ref.refs_4_), channel_id=1, source_target_pairs={{0,8},{4,12},{8,0},{12,4},{16,24},{20,28},{24,16},{28,20},{1,9},{5... | collective-permute-start | bytes 1572872 | tf_op jit(solution)/shard_map/ppermute | solution.py:544
  120.3 18.7 %collective-permute-start.27 = (bf16[256,1024]{1,0:T(8,128)(2,1)S(1)}, bf16[256,1024]{1,0:T(8,128)(2,1)S(1)}, u32[]{:S(2)}, u32[]{:S(2)}) collective-permute-start(bf16[256,1024]{1,0:T(8,128)(2,1)S(1)} %get-tuple-element.250), channel_id=1, source_target_pairs={{0,4},{4,0},{8,12},{12,8},{16,20},{20,16},{24,28},{28,24},{1,5},{5... | collective-permute-start | bytes 1572872 | tf_op jit(solution)/shard_map/ppermute | solution.py:544
  124.3 14.6 %collective-permute-start.33 = (bf16[128,1024]{1,0:T(8,128)(2,1)S(1)}, bf16[128,1024]{1,0:T(8,128)(2,1)S(1)}, u32[]{:S(2)}, u32[]{:S(2)}) collective-permute-start(bf16[128,1024]{1,0:T(8,128)(2,1)S(1)} %slice.163), channel_id=1, source_target_pairs={{0,8},{4,12},{8,0},{12,4},{16,24},{20,28},{24,16},{28,20},{1,9},{5... | collective-permute-start | bytes 786440 | tf_op jit(solution)/shard_map/ppermute | solution.py:544
  125.5 12.1 %collective-permute-start.40 = (bf16[128,1024]{1,0:T(8,128)(2,1)S(1)}, bf16[128,1024]{1,0:T(8,128)(2,1)S(1)}, u32[]{:S(2)}, u32[]{:S(2)}) collective-permute-start(bf16[128,1024]{1,0:T(8,128)(2,1)S(1)} %add_convert_fusion.8), channel_id=1, source_target_pairs={{0,8},{4,12},{8,0},{12,4},{16,24},{20,28},{24,16},{28,20},{1,9},{5... | collective-permute-start | bytes 786440 | tf_op jit(solution)/shard_map/ppermute | solution.py:544
  126.4 12.3 %collective-permute-start.43 = (bf16[128,1024]{1,0:T(8,128)(2,1)S(1)}, bf16[128,1024]{1,0:T(8,128)(2,1)S(1)}, u32[]{:S(2)}, u32[]{:S(2)}) collective-permute-start(bf16[128,1024]{1,0:T(8,128)(2,1)S(1)} %add_convert_fusion.7), channel_id=1, source_target_pairs={{0,16},{4,20},{8,24},{12,28},{16,0},{20,4},{24,8},{28,12},{1,17},{... | collective-permute-start | bytes 786440 | tf_op jit(solution)/shard_map/ppermute | solution.py:544
  127.4 11.9 %collective-permute-start.45 = (bf16[128,1024]{1,0:T(8,128)(2,1)S(1)}, bf16[128,1024]{1,0:T(8,128)(2,1)S(1)}, u32[]{:S(2)}, u32[]{:S(2)}) collective-permute-start(bf16[128,1024]{1,0:T(8,128)(2,1)S(1)} %slice.162), channel_id=1, source_target_pairs={{0,16},{4,20},{8,24},{12,28},{16,0},{20,4},{24,8},{28,12},{1,17},{... | collective-permute-start | bytes 786440 | tf_op jit(solution)/shard_map/ppermute | solution.py:544
  149.3 13.6 %collective-permute-start.49 = (bf16[256,1024]{1,0:T(8,128)(2,1)S(1)}, bf16[256,1024]{1,0:T(8,128)(2,1)S(1)}, u32[]{:S(2)}, u32[]{:S(2)}) collective-permute-start(bf16[256,1024]{1,0:T(8,128)(2,1)S(1)} %get-tuple-element.276.refs_0_.refs_2_.resid_ref), channel_id=1, source_target_pairs={{0,16},{4,20},{8,24},{12,28},{16,0},{20,4},{24,8},{28,12},{1,17},{... | collective-permute-start | bytes 1572872 | tf_op jit(solution)/shard_map/ppermute | solution.py:544
  149.8 13.2 %collective-permute-start.48 = (bf16[256,1024]{1,0:T(8,128)(2,1)S(1)}, bf16[256,1024]{1,0:T(8,128)(2,1)S(1)}, u32[]{:S(2)}, u32[]{:S(2)}) collective-permute-start(bf16[256,1024]{1,0:T(8,128)(2,1)S(1)} %get-tuple-element.276.refs_0_.refs_2_.resid_ref), channel_id=1, source_target_pairs={{0,8},{4,12},{8,0},{12,4},{16,24},{20,28},{24,16},{28,20},{1,9},{5... | collective-permute-start | bytes 1572872 | tf_op jit(solution)/shard_map/ppermute | solution.py:544
  180.8 22.1 %collective-permute-start.47 = (bf16[256,1024]{1,0:T(8,128)(2,1)}, bf16[256,1024]{1,0:T(8,128)(2,1)S(1)}, u32[]{:S(2)}, u32[]{:S(2)}) collective-permute-start(bf16[256,1024]{1,0:T(8,128)(2,1)} %get-tuple-element.280), channel_id=1, source_target_pairs={{0,4},{4,0},{8,12},{12,8},{16,20},{20,16},{24,28},{28,24},{1,5},{5... | collective-permute-start | bytes 1572872 | tf_op jit(solution)/shard_map/ppermute | solution.py:544
  181.5 10.4 %collective-permute-start.60 = (bf16[128,1024]{1,0:T(8,128)(2,1)S(1)}, bf16[128,1024]{1,0:T(8,128)(2,1)S(1)}, u32[]{:S(2)}, u32[]{:S(2)}) collective-permute-start(bf16[128,1024]{1,0:T(8,128)(2,1)S(1)} %add_convert_fusion.6), channel_id=1, source_target_pairs={{0,8},{4,12},{8,0},{12,4},{16,24},{20,28},{24,16},{28,20},{1,9},{5... | collective-permute-start | bytes 786440 | tf_op jit(solution)/shard_map/ppermute | solution.py:544
  184.2 18.7 %collective-permute-start.53 = (bf16[128,1024]{1,0:T(8,128)(2,1)}, bf16[128,1024]{1,0:T(8,128)(2,1)S(1)}, u32[]{:S(2)}, u32[]{:S(2)}) collective-permute-start(bf16[128,1024]{1,0:T(8,128)(2,1)} %slice.161), channel_id=1, source_target_pairs={{0,8},{4,12},{8,0},{12,4},{16,24},{20,28},{24,16},{28,20},{1,9},{5... | collective-permute-start | bytes 786440 | tf_op jit(solution)/shard_map/ppermute | solution.py:544
  185.7 17.2 %collective-permute-start.65 = (bf16[128,1024]{1,0:T(8,128)(2,1)S(1)}, bf16[128,1024]{1,0:T(8,128)(2,1)S(1)}, u32[]{:S(2)}, u32[]{:S(2)}) collective-permute-start(bf16[128,1024]{1,0:T(8,128)(2,1)S(1)} %slice.160), channel_id=1, source_target_pairs={{0,16},{4,20},{8,24},{12,28},{16,0},{20,4},{24,8},{28,12},{1,17},{... | collective-permute-start | bytes 786440 | tf_op jit(solution)/shard_map/ppermute | solution.py:544
  191.3 11.6 %collective-permute-start.64 = (bf16[128,1024]{1,0:T(8,128)(2,1)}, bf16[128,1024]{1,0:T(8,128)(2,1)S(1)}, u32[]{:S(2)}, u32[]{:S(2)}) collective-permute-start(bf16[128,1024]{1,0:T(8,128)(2,1)} %fusion), channel_id=1, source_target_pairs={{0,8},{4,12},{8,0},{12,4},{16,24},{20,28},{24,16},{28,20},{1,9},{5... | collective-permute-start | bytes 786440 | tf_op jit(solution)/shard_map/ppermute | solution.py:544
  191.9 11.0 %collective-permute-start.61 = (bf16[128,1024]{1,0:T(8,128)(2,1)S(1)}, bf16[128,1024]{1,0:T(8,128)(2,1)S(1)}, u32[]{:S(2)}, u32[]{:S(2)}) collective-permute-start(bf16[128,1024]{1,0:T(8,128)(2,1)S(1)} %fusion.1), channel_id=1, source_target_pairs={{0,16},{4,20},{8,24},{12,28},{16,0},{20,4},{24,8},{28,12},{1,17},{... | collective-permute-start | bytes 786440 | tf_op jit(solution)/shard_map/ppermute | solution.py:544
  220.1 108.8 %all-gather.7.cloned.1.call-start = ((), (), s32[]{:S(2)}) async-start(), calls=%async_computation.3 | async-start | bytes 4718592 | tf_op jit(solution)/shard_map/all_gather | solution.py:879
  220.1 26.0 %collective-permute-start.66 = (bf16[256,128]{1,0:T(8,128)(2,1)S(1)}, bf16[256,128]{1,0:T(8,128)(2,1)S(1)}, u32[]{:S(2)}, u32[]{:S(2)}) collective-permute-start(bf16[256,128]{1,0:T(8,128)(2,1)S(1)} %get-tuple-element.355), channel_id=1, source_target_pairs={{0,16},{4,20},{8,24},{12,28},{16,0},{20,4},{24,8},{28,12},{1,17},{... | collective-permute-start | bytes 196616 | tf_op jit(solution)/shard_map/ppermute | solution.py:544
  220.7 25.5 %collective-permute-start.67 = (bf16[256,128]{1,0:T(8,128)(2,1)S(1)}, bf16[256,128]{1,0:T(8,128)(2,1)S(1)}, u32[]{:S(2)}, u32[]{:S(2)}) collective-permute-start(bf16[256,128]{1,0:T(8,128)(2,1)S(1)} %get-tuple-element.356), channel_id=1, source_target_pairs={{0,20},{4,16},{8,28},{12,24},{16,4},{20,0},{24,12},{28,8},{1,21},{... | collective-permute-start | bytes 196616 | tf_op jit(solution)/shard_map/ppermute | solution.py:544
  222.0 24.2 %collective-permute-start.68 = (bf16[256,128]{1,0:T(8,128)(2,1)S(1)}, bf16[256,128]{1,0:T(8,128)(2,1)S(1)}, u32[]{:S(2)}, u32[]{:S(2)}) collective-permute-start(bf16[256,128]{1,0:T(8,128)(2,1)S(1)} %get-tuple-element.357), channel_id=1, source_target_pairs={{0,24},{4,28},{8,16},{12,20},{16,8},{20,12},{24,0},{28,4},{1,25},{... | collective-permute-start | bytes 196616 | tf_op jit(solution)/shard_map/ppermute | solution.py:544
  227.2 19.0 %collective-permute-start.69 = (bf16[256,128]{1,0:T(8,128)(2,1)S(1)}, bf16[256,128]{1,0:T(8,128)(2,1)S(1)}, u32[]{:S(2)}, u32[]{:S(2)}) collective-permute-start(bf16[256,128]{1,0:T(8,128)(2,1)S(1)} %get-tuple-element.358), channel_id=1, source_target_pairs={{0,28},{4,24},{8,20},{12,16},{16,12},{20,8},{24,4},{28,0},{1,29},{... | collective-permute-start | bytes 196616 | tf_op jit(solution)/shard_map/ppermute | solution.py:544
  229.5 16.4 %collective-permute-start.72 = (bf16[256,1024]{1,0:T(8,128)(2,1)S(1)}, bf16[256,1024]{1,0:T(8,128)(2,1)S(1)}, u32[]{:S(2)}, u32[]{:S(2)}) collective-permute-start(bf16[256,1024]{1,0:T(8,128)(2,1)S(1)} %slice.139), channel_id=1, source_target_pairs={{0,8},{4,12},{8,0},{12,4},{16,24},{20,28},{24,16},{28,20},{1,9},{5... | collective-permute-start | bytes 1572872 | tf_op jit(solution)/shard_map/ppermute | solution.py:544
  246.2 16.9 %collective-permute-start.75 = (bf16[128,1024]{1,0:T(8,128)(2,1)S(1)}, bf16[128,1024]{1,0:T(8,128)(2,1)S(1)}, u32[]{:S(2)}, u32[]{:S(2)}) collective-permute-start(bf16[128,1024]{1,0:T(8,128)(2,1)S(1)} %slice.141), channel_id=1, source_target_pairs={{0,16},{4,20},{8,24},{12,28},{16,0},{20,4},{24,8},{28,12},{1,17},{... | collective-permute-start | bytes 786440 | tf_op jit(solution)/shard_map/ppermute | solution.py:544
  278.3 10.0 %collective-permute-start.78 = (bf16[128,1024]{1,0:T(8,128)(2,1)S(1)}, bf16[128,1024]{1,0:T(8,128)(2,1)S(1)}, u32[]{:S(2)}, u32[]{:S(2)}) collective-permute-start(bf16[128,1024]{1,0:T(8,128)(2,1)S(1)} %get-tuple-element.398), channel_id=1, source_target_pairs={{0,8},{4,12},{8,0},{12,4},{16,24},{20,28},{24,16},{28,20},{1,9},{5... | collective-permute-start | bytes 786440 | tf_op jit(solution)/shard_map/ppermute | solution.py:544
  280.2 12.9 %collective-permute-start.83 = (bf16[1072,128]{1,0:T(8,128)(2,1)S(1)}, bf16[1072,128]{1,0:T(8,128)(2,1)S(1)}, u32[]{:S(2)}, u32[]{:S(2)}) collective-permute-start(bf16[1072,128]{1,0:T(8,128)(2,1)S(1)} %copy-done.106), channel_id=1, source_target_pairs={{0,1},{1,0},{2,3},{3,2},{4,5},{5,4},{6,7},{7,6},{8,9},{9,8},{10,11... | collective-permute-start | bytes 823304 | tf_op jit(solution)/shard_map/ppermute | solution.py:548
  282.7 13.0 %collective-permute-start.84 = (bf16[1072,128]{1,0:T(8,128)(2,1)S(1)}, bf16[1072,128]{1,0:T(8,128)(2,1)S(1)}, u32[]{:S(2)}, u32[]{:S(2)}) collective-permute-start(bf16[1072,128]{1,0:T(8,128)(2,1)S(1)} %copy-done.105), channel_id=1, source_target_pairs={{0,2},{1,3},{2,0},{3,1},{4,6},{5,7},{6,4},{7,5},{8,10},{9,11},{10,... | collective-permute-start | bytes 823304 | tf_op jit(solution)/shard_map/ppermute | solution.py:548
  284.2 23.6 %collective-permute-start.85 = (bf16[1072,128]{1,0:T(8,128)(2,1)S(1)}, bf16[1072,128]{1,0:T(8,128)(2,1)S(1)}, u32[]{:S(2)}, u32[]{:S(2)}) collective-permute-start(bf16[1072,128]{1,0:T(8,128)(2,1)S(1)} %copy-done.104), channel_id=1, source_target_pairs={{0,3},{1,2},{2,1},{3,0},{4,7},{5,6},{6,5},{7,4},{8,11},{9,10},{10,... | collective-permute-start | bytes 823304 | tf_op jit(solution)/shard_map/ppermute | solution.py:548
  311.0 12.8 %collective-permute-start.77 = (bf16[128,1024]{1,0:T(8,128)(2,1)S(1)}, bf16[128,1024]{1,0:T(8,128)(2,1)S(1)}, u32[]{:S(2)}, u32[]{:S(2)}) collective-permute-start(bf16[128,1024]{1,0:T(8,128)(2,1)S(1)} %get-tuple-element.396), channel_id=1, source_target_pairs={{0,8},{4,12},{8,0},{12,4},{16,24},{20,28},{24,16},{28,20},{1,9},{5... | collective-permute-start | bytes 786440 | tf_op jit(solution)/shard_map/ppermute | solution.py:544
  318.2 9.6 %collective-permute-start.92 = (bf16[544,128]{1,0:T(8,128)(2,1)S(1)}, bf16[544,128]{1,0:T(8,128)(2,1)}, u32[]{:S(2)}, u32[]{:S(2)}) collective-permute-start(bf16[544,128]{1,0:T(8,128)(2,1)S(1)} %slice.127), channel_id=1, source_target_pairs={{0,8},{4,12},{8,0},{12,4},{16,24},{20,28},{24,16},{28,20},{1,9},{5... | collective-permute-start | bytes 417800 | tf_op jit(solution)/shard_map/ppermute | solution.py:544
  319.9 15.4 %collective-permute-start.82 = (bf16[128,1024]{1,0:T(8,128)(2,1)S(1)}, bf16[128,1024]{1,0:T(8,128)(2,1)S(1)}, u32[]{:S(2)}, u32[]{:S(2)}) collective-permute-start(bf16[128,1024]{1,0:T(8,128)(2,1)S(1)} %get-tuple-element.401), channel_id=1, source_target_pairs={{0,16},{4,20},{8,24},{12,28},{16,0},{20,4},{24,8},{28,12},{1,17},{... | collective-permute-start | bytes 786440 | tf_op jit(solution)/shard_map/ppermute | solution.py:544
  320.4 14.9 %collective-permute-start.79 = (bf16[128,1024]{1,0:T(8,128)(2,1)S(1)}, bf16[128,1024]{1,0:T(8,128)(2,1)S(1)}, u32[]{:S(2)}, u32[]{:S(2)}) collective-permute-start(bf16[128,1024]{1,0:T(8,128)(2,1)S(1)} %add_convert_fusion.3), channel_id=1, source_target_pairs={{0,16},{4,20},{8,24},{12,28},{16,0},{20,4},{24,8},{28,12},{1,17},{... | collective-permute-start | bytes 786440 | tf_op jit(solution)/shard_map/ppermute | solution.py:544
  323.8 12.4 %collective-permute-start.81 = (bf16[128,1024]{1,0:T(8,128)(2,1)S(1)}, bf16[128,1024]{1,0:T(8,128)(2,1)S(1)}, u32[]{:S(2)}, u32[]{:S(2)}) collective-permute-start(bf16[128,1024]{1,0:T(8,128)(2,1)S(1)} %add_convert_fusion.2), channel_id=1, source_target_pairs={{0,8},{4,12},{8,0},{12,4},{16,24},{20,28},{24,16},{28,20},{1,9},{5... | collective-permute-start | bytes 786440 | tf_op jit(solution)/shard_map/ppermute | solution.py:544
  324.4 12.8 %collective-permute-start.89 = (bf16[1072,128]{1,0:T(8,128)(2,1)S(1)}, bf16[1072,128]{1,0:T(8,128)(2,1)}, u32[]{:S(2)}, u32[]{:S(2)}) collective-permute-start(bf16[1072,128]{1,0:T(8,128)(2,1)S(1)} %collective-permute-done.86.refs_2_), channel_id=1, source_target_pairs={{0,4},{4,0},{8,12},{12,8},{16,20},{20,16},{24,28},{28,24},{1,5},{5... | collective-permute-start | bytes 823304 | tf_op jit(solution)/shard_map/ppermute | solution.py:544
  327.8 9.4 %collective-permute-start.90 = (bf16[1072,128]{1,0:T(8,128)(2,1)S(1)}, bf16[1072,128]{1,0:T(8,128)(2,1)}, u32[]{:S(2)}, u32[]{:S(2)}) collective-permute-start(bf16[1072,128]{1,0:T(8,128)(2,1)S(1)} %collective-permute-done.87.refs_4_), channel_id=1, source_target_pairs={{0,4},{4,0},{8,12},{12,8},{16,20},{20,16},{24,28},{28,24},{1,5},{5... | collective-permute-start | bytes 823304 | tf_op jit(solution)/shard_map/ppermute | solution.py:544
  (166 other events, 1147.1 us)
Sparse Core Ops, SparseCore 0:
  39.9 47.5 all-gather.4
  220.2 42.7 reduce-scatter.1
  265.0 38.9 all-gather.6
